TPU v7x, 32 devices: a whole 2x2x4 slice. The times are simulated.
32 devices in a mesh: tok: 8 (over y, x, core), hid: 4 (over z).
Axes of the slice: x: 2, y: 2, z: 4, core: 2. Of those that a mesh axis runs over, the one named last changes fastest.
Arguments:
- tokens: bfloat16 [6144, 2048], P('tok', 'hid')
- qkv_weight: bfloat16 [2048, 6144], P('tok', 'hid')
- out_weight: bfloat16 [2048, 2048], P('tok', 'hid'), may hold values from -0.125 to 0.125
- neighbours: int32 [96, 9], replicated, may hold values from 0 to 95, as said below
- counts: int32 [96], replicated, may hold values from 7 to 9
Outputs:
- attended: bfloat16 [6144, 2048], P('tok', 'hid')
Inputs may be any that keep to these rules, and one draw needn't show every extreme that they name: `neighbours`: entry 0 of each list is the block itself. Block b lies on index b // 12 of tok. Among the valid entries of the lists of one device's blocks, at most 2 distinct blocks of any one other device are named, and every device names exactly 2 blocks of some other device.
All inputs are finite; a program needn't handle non-finite values.
Results may differ from a plain program's by a relative error of at most 0.012.
Values may be sent and summed in bfloat16 or wider, within the bound.
No kernel may reach another device: no remote copies, remote signals or barrier semaphores. Data moves between devices by JAX's collectives and lax.ppermute only.
A program may use at most 128 MiB of HBM per device.

v0:
```python
import jax
import jax.numpy as jnp
from jax import lax
from jax.sharding import PartitionSpec as P

HEAD_WIDTH = 128
BLK = 64
NEIGH = 9


def shards(tokens, qkv_weight, out_weight, neighbours, counts):
    self_index = lax.axis_index("tok")
    tok_rows = tokens.shape[0]
    blocks_here = tok_rows // BLK
    local_head_count = qkv_weight.shape[1] // (3 * HEAD_WIDTH)
    qkv_rows, out_rows = (
        lax.all_gather(qkv_weight, "tok", axis=0, tiled=True),
        lax.all_gather(out_weight, "tok", axis=0, tiled=True),
    )
    panel = qkv_rows
    projected = jnp.dot(
        lax.all_gather(tokens, "hid", axis=1, tiled=True), panel, preferred_element_type=jnp.float32
    ).astype(jnp.bfloat16)
    projected = projected.reshape(blocks_here, BLK, local_head_count, 3, HEAD_WIDTH)
    query_matrix = projected[:, :, :, 0]
    key_values = projected[:, :, :, 1:].reshape(blocks_here, BLK, local_head_count * 2 * HEAD_WIDTH)
    my_lists = lax.dynamic_slice_in_dim(neighbours, self_index * blocks_here, blocks_here, 0)
    my_counts = lax.dynamic_slice_in_dim(counts, self_index * blocks_here, blocks_here, 0)
    usable = jnp.arange(NEIGH)[None, :] < my_counts[:, None]
    key_pool = lax.all_gather(key_values, "tok", axis=0, tiled=True)
    gathered = key_pool[my_lists].reshape(blocks_here, NEIGH, BLK, local_head_count, 2, HEAD_WIDTH)
    attention_logits = jnp.einsum(
        "bqhd,bjkhd->bhqjk", query_matrix, gathered[..., 0, :], preferred_element_type=jnp.float32
    ) * HEAD_WIDTH ** (-0.5)
    attention_logits = jnp.where(usable[:, None, None, :, None], attention_logits, -1e30)
    highest = jnp.max(attention_logits, axis=(3, 4), keepdims=True)
    expon = jnp.exp(attention_logits - highest)
    attention_probs = (expon / jnp.sum(expon, axis=(3, 4), keepdims=True)).astype(jnp.bfloat16)
    blended_values = jnp.einsum(
        "bhqjk,bjkhd->bqhd",
        attention_probs,
        gathered[..., 1, :],
        preferred_element_type=jnp.float32,
    ).astype(jnp.bfloat16)
    blended_values = blended_values.reshape(tok_rows, local_head_count * HEAD_WIDTH)
    panel = out_rows
    result = jnp.dot(
        lax.all_gather(blended_values, "hid", axis=1, tiled=True),
        panel,
        preferred_element_type=jnp.float32,
    )
    return result.astype(jnp.bfloat16)


def solution(mesh):
    placed = (P("tok", "hid"), P("tok", "hid"), P("tok", "hid"), P(), P())
    return jax.shard_map(
        shards, mesh=mesh, in_specs=placed, out_specs=P("tok", "hid"), check_vma=False
    )
```

profile of v0, /device:TPU:0, one launch (start us, length us, event | category | flops | bytes accessed | tf_op | source)
XLA Modules:
  0.0 405.9 jit_solution(14836799237860070348)
XLA Ops:
  6.5 0.0 all-gather.6.cloned.1.call-start
  6.5 0.7 all-gather.6.cloned.1.call-update
  7.3 0.0 all-gather.8.cloned.1.call-start
  7.3 0.7 all-gather.8.cloned.1.call-update
  8.0 0.0 all-gather.10.cloned.1.call-start
  8.1 67.1 %all-gather.6.cloned.1.call-done = bf16[768,2048]{1,0:T(8,128)(2,1)} async-done(((bf16[768,512]{1,0:T(8,128)(2,1)}), bf16[768,2048]{1,0:T(8,128)(2,1)}) %all-gather.6.cloned.1.call-update) | async-done | bytes 3145744 | tf_op jit(solution)/shard_map/all_gather | solution.py:22
  75.1 46.1 %all-gather.8.cloned.1.call-done = bf16[2048,1536]{1,0:T(8,128)(2,1)} async-done(((bf16[256,1536]{1,0:T(8,128)(2,1)}), bf16[2048,1536]{1,0:T(8,128)(2,1)}) %all-gather.8.cloned.1.call-update) | async-done | bytes 6291472 | tf_op jit(solution)/shard_map/all_gather | solution.py:17
  121.2 9.2 %convolution_convert_fusion = bf16[768,1536]{1,0:T(8,128)(2,1)} fusion(bf16[768,2048]{1,0:T(8,128)(2,1)} %all-gather.6.cloned.1.call-done, bf16[2048,1536]{1,0:T(8,128)(2,1)} %all-gather.8.cloned.1.call-done), kind=kOutput, calls=%fused_computation.12 | convolution fusion | flops 4833017856 | bytes 11796480 | tf_op jit(solution)/shard_map/dot_general | solution.py:21
  130.4 0.0 copy-start.1
  130.4 0.0 copy-start.2
  130.4 5.0 %reshape.34 = bf16[12,64,4,3,128]{4,3,2,1,0:T(4,128)(2,1)S(1)} reshape(bf16[768,1536]{1,0:T(8,128)(2,1)} %convolution_convert_fusion) | data formatting | bytes 4718592 | tf_op jit(solution)/shard_map/reshape | solution.py:24
  135.4 3.1 slice.18
  138.5 3.8 reshape.35
  142.3 0.0 all-gather.10.cloned.1.call-update
  142.3 0.0 all-gather.14.cloned.1.call-start
  142.3 0.5 all-gather.14.cloned.1.call-update
  142.9 0.0 all-gather.12.cloned.1.call-start
  142.9 0.0 copy-done.1
  142.9 0.1 compare_select_fusion
  143.0 0.1 copy.15
  143.1 0.1 reshape.40
  143.2 0.0 copy-done.2
  143.2 0.1 dynamic_slice.7
  143.3 0.1 iota_compare_fusion
  143.4 2.5 slice.20
  145.9 68.7 %all-gather.10.cloned.1.call-done = bf16[96,64,1024]{2,1,0:T(8,128)(2,1)} async-done(((bf16[12,64,1024]{2,1,0:T(8,128)(2,1)}), bf16[96,64,1024]{2,1,0:T(8,128)(2,1)}) %all-gather.10.cloned.1.call-update) | async-done | bytes 12582928 | tf_op jit(solution)/shard_map/all_gather | solution.py:30
  214.6 12.1 %gather_fusion = bf16[108,64,1024]{2,1,0:T(8,128)(2,1)} fusion(bf16[96,64,1024]{2,1,0:T(8,128)(2,1)} %all-gather.10.cloned.1.call-done, s32[1024]{0:T(1024)S(1)} %pad_clamp_fusion), kind=kCustom, calls=%fused_computation | custom fusion | bytes 28311984 | tf_op jit(solution)/shard_map/gather | solution.py:31
  226.7 23.4 %reshape.36 = bf16[12,9,64,4,2,128]{5,4,3,2,1,0:T(2,128)(2,1)} reshape(bf16[108,64,1024]{2,1,0:T(8,128)(2,1)} %gather_fusion) | data formatting | bytes 28311552 | tf_op jit(solution)/shard_map/reshape | solution.py:31
  250.2 28.2 %fusion.11 = (bf16[12,9,64,4,1,128]{5,4,3,2,1,0:T(2,128)(2,1)}, bf16[12,9,64,4,1,128]{5,4,3,2,1,0:T(2,128)(2,1)}) fusion(bf16[12,9,64,4,2,128]{5,4,3,2,1,0:T(2,128)(2,1)} %reshape.36), kind=kLoop, calls=%fused_computation.24 | loop fusion | bytes 28311552 | tf_op jit(solution)/shard_map/slice | solution.py:42
  278.4 0.0 copy-start
  278.4 10.2 %copy.25 = bf16[12,9,64,4,1,128]{5,2,1,3,0,4:T(8,128)(2,1)} copy(bf16[12,9,64,4,1,128]{5,4,3,2,1,0:T(2,128)(2,1)} %get-tuple-element.6) | data formatting | bytes 14155776
  288.6 0.0 copy-done
  288.6 10.0 %fusion.8 = f32[12,4,64,576]{2,3,1,0} fusion(bf16[12,4,128,576]{2,3,1,0:T(8,128)(2,1)} %bitcast.36, bf16[12,64,4,1,128]{4,3,2,1,0:T(2,128)(2,1)S(1)} %copy-done), kind=kOutput, calls=%fused_computation.18 | convolution fusion | flops 452984832 | bytes 14942208
  298.7 8.9 %fusion = f32[12,4,64]{2,1,0:T(4,128)S(1)} fusion(f32[12,4,64,9,64]{2,4,3,1,0:T(8,128)} %bitcast.33, pred[12,9]{1,0:T(8,128)(4,1)S(1)} %iota_compare_fusion), kind=kLoop, calls=%fused_computation.4 | loop fusion | flops 5305344 | bytes 7090284 | tf_op jit(solution)/shard_map/reduce_max | solution.py:36
  307.5 9.2 %fusion.1 = f32[12,4,64]{2,1,0:T(4,128)S(1)} fusion(f32[12,4,64,9,64]{2,4,3,1,0:T(8,128)} %bitcast.34, f32[12,4,64]{2,1,0:T(4,128)S(1)} %fusion, pred[12,9]{1,0:T(8,128)(4,1)S(1)} %iota_compare_fusion), kind=kLoop, calls=%fused_computation.5 | loop fusion | flops 7074816 | bytes 7102572 | tf_op jit(solution)/shard_map/reduce_sum | solution.py:38
  316.7 12.1 %fusion.7 = bf16[12,64,4,128]{3,1,2,0:T(8,128)(2,1)S(1)} fusion(f32[12,4,64,9,64]{2,4,3,1,0:T(8,128)} %bitcast.35, f32[12,4,64]{2,1,0:T(4,128)S(1)} %fusion.1, f32[12,4,64]{2,1,0:T(4,128)S(1)} %fusion, pred[12,9]{1,0:T(8,128)(4,1)S(1)} %iota_compare_fusion, bf16[12,9,64,4,1,128]{5,4,3,2,1,0:T(2,128)(2,1)} %get-tuple-element.5), kind=kOutput, calls=%fused_computation.15 | convolution fusion | flops 462225408 | bytes 14966892 | tf_op jit(solution)/shard_map/bhqjk,bjkhd->bqhd/dot_general | solution.py:39
  328.8 0.6 copy.20
  329.4 1.0 copy.36
  330.4 0.0 all-gather.12.cloned.1.call-update
  330.4 0.0 all-gather.14.cloned.1.call-done
  330.5 63.7 %all-gather.12.cloned.1.call-done = bf16[768,2048]{1,0:T(8,128)(2,1)} async-done(((bf16[768,512]{1,0:T(8,128)(2,1)}), bf16[768,2048]{1,0:T(8,128)(2,1)}) %all-gather.12.cloned.1.call-update) | async-done | bytes 3145744 | tf_op jit(solution)/shard_map/all_gather | solution.py:48
  394.1 5.2 %convolution_convert_fusion.1 = bf16[768,512]{1,0:T(8,128)(2,1)} fusion(bf16[768,2048]{1,0:T(8,128)(2,1)} %all-gather.12.cloned.1.call-done, bf16[2048,512]{1,0:T(8,128)(2,1)} %all-gather.14.cloned.1.call-done), kind=kOutput, calls=%fused_computation.14 | convolution fusion | flops 1611005952 | bytes 6029312 | tf_op jit(solution)/shard_map/dot_general | solution.py:47
  (1 shorter events, 0.0 us)
Async XLA Ops:
  6.5 68.6 %all-gather.6.cloned.1.call-start = ((), (), s32[]{:S(2)}) async-start(), calls=%async_computation | async-start | bytes 3932160 | tf_op jit(solution)/shard_map/all_gather | solution.py:22
  7.3 114.0 %all-gather.8.cloned.1.call-start = ((), (), s32[]{:S(2)}) async-start(), calls=%async_computation.1 | async-start | bytes 7077888 | tf_op jit(solution)/shard_map/all_gather | solution.py:17
  8.0 206.6 %all-gather.10.cloned.1.call-start = ((), (), s32[]{:S(2)}) async-start(), calls=%async_computation.2 | async-start | bytes 14155776 | tf_op jit(solution)/shard_map/all_gather | solution.py:30
  130.4 12.5 %copy-start.1 = (s32[96,9]{0,1:T(8,128)S(1)}, s32[96,9]{0,1:T(8,128)}, u32[]{:S(2)}) copy-start(s32[96,9]{0,1:T(8,128)} %param.8) | copy-start | bytes 10372
  130.4 12.8 %copy-start.2 = (s32[96]{0:T(128)S(1)}, s32[96]{0:T(128)}, u32[]{:S(2)}) copy-start(s32[96]{0:T(128)} %param.9) | copy-start | bytes 1156
  142.3 188.2 %all-gather.14.cloned.1.call-start = ((), (), s32[]{:S(2)}) async-start(), calls=%async_computation.4 | async-start | bytes 2359296 | tf_op jit(solution)/shard_map/all_gather | solution.py:18
  142.9 251.3 %all-gather.12.cloned.1.call-start = ((), (), s32[]{:S(2)}) async-start(), calls=%async_computation.3 | async-start | bytes 3932160 | tf_op jit(solution)/shard_map/all_gather | solution.py:48
  278.4 10.2 %copy-start = (bf16[12,64,4,1,128]{4,3,2,1,0:T(2,128)(2,1)S(1)}, bf16[12,64,4,1,128]{4,3,2,1,0:T(2,128)(2,1)}, u32[]{:S(2)}) copy-start(bf16[12,64,4,1,128]{4,3,2,1,0:T(2,128)(2,1)} %slice.20) | copy-start | bytes 2359300
Sparse Core Ops, SparseCore 0:
  8.9 66.1 all-gather.5
  77.0 44.2 all-gather.7
  142.4 72.1 all-gather.9
  216.3 27.8 all-gather.13
  330.6 63.5 all-gather.11
where the time goes:
time: 407 us; the launch traced here: 406 us
  waiting for transfers between devices  248 us (61%)
  local copies, waits for them, and re-layouts  90.2 us (22%)
  matrix products  36.5 us (9%)
  other arithmetic  18.2 us (4%)
  between operations  13.2 us (3%)
    all_gather x1, waiting for transfers between devices, shards(): key_pool = lax.all_gather(key_values, 'tok', axis=0, tiled=True)  68.7 us
    all_gather x1, waiting for transfers between devices, shards(): lax.all_gather(tokens, 'hid', axis=1, tiled=True)  67.1 us
    all_gather x1, waiting for transfers between devices, shards(): lax.all_gather(blended_values, 'hid', axis=1, tiled=True)  63.7 us
    all_gather x1, waiting for transfers between devices, shards(): lax.all_gather(qkv_weight, 'tok', axis=0, tiled=True)  46.1 us
    slice x1, local copies, waits for them, and re-layouts, shards(): gathered[..., 1, :]  28.2 us
    reshape x1, local copies, waits for them, and re-layouts, shards(): key_pool[my_lists]  23.4 us
    gather x1, local copies, waits for them, and re-layouts, shards(): key_pool[my_lists]  12.1 us
    dot_general x1, matrix products, shards(): jnp.einsum('bhqjk,bjkhd->bqhd', attention_probs, gathered[..., 1, :], pre...  12.1 us
  transfers between devices with their start and end apart: 5, of which 4 were waited for; matrix products, arithmetic and copies ran while one was open for 29% of the time, Pallas kernels for 0%

commit v1 on v0

v1 whole, which is shorter than its diff:
```python
import functools

import jax
import jax.numpy as jnp
from jax import lax
from jax.experimental import pallas as pl
from jax.experimental.pallas import tpu as pltpu
from jax.sharding import PartitionSpec as P

HEAD_WIDTH = 128
BLK = 64
NEIGH = 9
VMEM_LIMIT = 60 * 1024 * 1024
LOG2E = 1.4426950408889634


def line_gather(part, axis, size):
    to_right = [(i, i + 1) for i in range(size - 1)]
    to_left = [(i + 1, i) for i in range(size - 1)]
    left, right, from_left, from_right = part, part, [], []
    for _ in range(size - 1):
        left = lax.ppermute(left, axis, to_right)
        right = lax.ppermute(right, axis, to_left)
        from_left.append(left)
        from_right.append(right)
    return from_left, from_right


def exchange_gather(shard, axis, size):
    pieces = [shard] + [None] * (size - 1)
    for s in range(2, size, 2):
        pieces[s] = lax.ppermute(shard, axis, [(i, i ^ s) for i in range(size)])
    for s in range(0, size, 2):
        pieces[s + 1] = lax.ppermute(pieces[s], axis, [(i, i ^ 1) for i in range(size)])
    return pieces


def load_rows_parts(place, parts, dest, sem, hid_size, width):
    at_hid = place[0]
    chunks = len(parts)
    cut = width // chunks

    def each(act):
        for c, (own, from_left, from_right) in enumerate(parts):
            def copy(ref, source, k, c=c):
                begin = pl.multiple_of(source * width + c * cut, cut)
                return pltpu.make_async_copy(ref, dest.at[:, pl.ds(begin, cut)], sem.at[c, k])

            act(copy(own, at_hid, 0))
            for k in range(1, hid_size):
                @pl.when(at_hid >= k)
                def _():
                    act(copy(from_left[k - 1], at_hid - k, k))

                @pl.when(at_hid + k < hid_size)
                def _():
                    act(copy(from_right[k - 1], at_hid + k, hid_size - 1 + k))

    return (lambda: each(lambda d: d.start())), (lambda: each(lambda d: d.wait()))


def group_parts(refs, chunks, hid_size):
    per = 1 + 2 * (hid_size - 1)
    parts = []
    for c in range(chunks):
        r = refs[c * per : (c + 1) * per]
        parts.append((r[0], r[1 : hid_size], r[hid_size:]))
    return parts


def flat_parts(parts):
    return [x for own, a, b in parts for x in [own, *a, *b]]


def project_kernel(place, send_ids, *refs, chunks, hid_size, tok_size, width, columns, step, sends):
    n_parts = chunks * (1 + 2 * (hid_size - 1))
    parts = group_parts(refs[:n_parts], chunks, hid_size)
    pieces = refs[n_parts : n_parts + tok_size]
    outs = refs[n_parts + tok_size :]
    n_sends = tok_size - 1 if sends else 0
    result, send_refs = outs[0], outs[1 : 1 + n_sends]
    rows, weights, row_sem, weight_sem = outs[1 + n_sends :]
    at_tok = place[1]
    depth = pieces[0].shape[0]
    begin, total = columns
    start, wait = load_rows_parts(place, parts, rows, row_sem, hid_size, width)
    start()

    def weight_copy(s, n):
        at = pl.multiple_of((at_tok ^ s) * depth, depth)
        return pltpu.make_async_copy(
            pieces[s].at[:, pl.ds(begin + n * step, step)],
            weights.at[pl.ds(at, depth), pl.ds(n * step, step)],
            weight_sem.at[n, s],
        )

    steps = total // step
    for n in range(steps):
        for s in range(tok_size):
            weight_copy(s, n).start()
    wait()
    for n in range(steps):
        for s in range(tok_size):
            weight_copy(s, n).wait()
        result[:, n * step : (n + 1) * step] = jnp.dot(
            rows[...], weights[:, n * step : (n + 1) * step], preferred_element_type=jnp.float32
        ).astype(result.dtype)
    if sends:
        for s in range(1, tok_size):
            for slot in range(2):
                at = pl.multiple_of(send_ids[s, slot] * BLK, BLK)
                for j in range(total // (3 * HEAD_WIDTH)):
                    send_refs[s - 1][slot * BLK : (slot + 1) * BLK, j * 2 * HEAD_WIDTH : (j + 1) * 2 * HEAD_WIDTH] = (
                        result[pl.ds(at, BLK), (3 * j + 1) * HEAD_WIDTH : (3 * j + 3) * HEAD_WIDTH]
                    )


def project(place, send_ids, parts, pieces, columns, step, tok_size, hid_size, sends):
    chunks = len(parts)
    own = parts[0][0]
    tok_rows, width = own.shape[0], own.shape[1] * chunks
    full = width * hid_size
    total = columns[1]
    heads = total // (3 * HEAD_WIDTH)
    shapes = [jax.ShapeDtypeStruct((tok_rows, total), jnp.bfloat16)]
    if sends:
        shapes += [jax.ShapeDtypeStruct((2 * BLK, heads * 2 * HEAD_WIDTH), jnp.bfloat16)] * (tok_size - 1)
    flat = flat_parts(parts)
    return pl.pallas_call(
        functools.partial(
            project_kernel, chunks=chunks, hid_size=hid_size, tok_size=tok_size, width=width,
            columns=columns, step=step, sends=sends,
        ),
        out_shape=shapes,
        in_specs=[pl.BlockSpec(memory_space=pltpu.SMEM)] * 2
        + [pl.BlockSpec(memory_space=pl.ANY)] * (len(flat) + tok_size),
        out_specs=[pl.BlockSpec(memory_space=pltpu.VMEM)] * len(shapes),
        scratch_shapes=[
            pltpu.VMEM((tok_rows, full), jnp.bfloat16),
            pltpu.VMEM((full, total), jnp.bfloat16),
            pltpu.SemaphoreType.DMA((chunks, 2 * hid_size - 1)),
            pltpu.SemaphoreType.DMA((total // step, tok_size)),
        ],
        compiler_params=pltpu.CompilerParams(vmem_limit_bytes=VMEM_LIMIT),
        cost_estimate=pl.CostEstimate(
            flops=2 * tok_rows * full * total, bytes_accessed=2 * full * (tok_rows + total), transcendentals=0
        ),
    )(place, send_ids, *flat, *pieces)


def attend_kernel(lists, counts, projected, *refs, tok_size, heads):
    remote = refs[: tok_size - 1]
    result, pool, sem = refs[tok_size - 1 :]
    tok_rows = projected.shape[0]
    blocks = tok_rows // BLK
    pair = 2 * HEAD_WIDTH
    copies = []
    for j in range(heads):
        copies.append(pltpu.make_async_copy(
            projected.at[:, pl.ds((3 * j + 1) * HEAD_WIDTH, pair)],
            pool.at[pl.ds(0, tok_rows), pl.ds(j * pair, pair)],
            sem.at[tok_size - 1 + j],
        ))
    for s in range(tok_size - 1):
        copies.append(pltpu.make_async_copy(
            remote[s], pool.at[pl.ds(tok_rows + s * 2 * BLK, 2 * BLK), :], sem.at[s]
        ))
    for copy in copies:
        copy.start()
    for copy in copies:
        copy.wait()
    scale = HEAD_WIDTH ** (-0.5) * LOG2E

    def block(b, carry):
        at = pl.multiple_of(b * BLK, BLK)
        starts = [pl.multiple_of(lists[b, j] * BLK, BLK) for j in range(NEIGH)]
        limit = counts[b] * BLK
        usable = lax.broadcasted_iota(jnp.int32, (BLK, NEIGH * BLK), 1) < limit
        for h in range(heads):
            query = projected[pl.ds(at, BLK), 3 * h * HEAD_WIDTH : (3 * h + 1) * HEAD_WIDTH]
            keys = jnp.concatenate(
                [pool[pl.ds(i, BLK), h * pair : h * pair + HEAD_WIDTH] for i in starts], axis=0
            )
            logits = lax.dot_general(query, keys, (((1,), (1,)), ((), ())), preferred_element_type=jnp.float32)
            logits = jnp.where(usable, logits, -1e30)
            highest = jnp.max(logits, axis=1, keepdims=True)
            expon = jnp.exp2((logits - highest) * scale)
            total = jnp.sum(expon, axis=1, keepdims=True)
            values = jnp.concatenate(
                [pool[pl.ds(i, BLK), h * pair + HEAD_WIDTH : (h + 1) * pair] for i in starts], axis=0
            )
            blended = jnp.dot(expon.astype(jnp.bfloat16), values, preferred_element_type=jnp.float32)
            result[pl.ds(at, BLK), h * HEAD_WIDTH : (h + 1) * HEAD_WIDTH] = (blended / total).astype(result.dtype)
        return carry

    lax.fori_loop(0, blocks, block, 0)


def attend(lists, counts, projected, remote, tok_size):
    tok_rows = projected.shape[0]
    heads = projected.shape[1] // (3 * HEAD_WIDTH)
    return pl.pallas_call(
        functools.partial(attend_kernel, tok_size=tok_size, heads=heads),
        out_shape=jax.ShapeDtypeStruct((tok_rows, heads * HEAD_WIDTH), jnp.bfloat16),
        in_specs=[pl.BlockSpec(memory_space=pltpu.SMEM)] * 2
        + [pl.BlockSpec(memory_space=pltpu.VMEM)]
        + [pl.BlockSpec(memory_space=pl.ANY)] * (tok_size - 1),
        out_specs=pl.BlockSpec(memory_space=pltpu.VMEM),
        scratch_shapes=[
            pltpu.VMEM((tok_rows + (tok_size - 1) * 2 * BLK, heads * 2 * HEAD_WIDTH), jnp.bfloat16),
            pltpu.SemaphoreType.DMA((tok_size - 1 + heads,)),
        ],
        compiler_params=pltpu.CompilerParams(vmem_limit_bytes=VMEM_LIMIT),
        cost_estimate=pl.CostEstimate(
            flops=4 * tok_rows * NEIGH * BLK * HEAD_WIDTH * heads,
            bytes_accessed=4 * tok_rows * HEAD_WIDTH * heads * 8,
            transcendentals=tok_rows * NEIGH * BLK * heads,
        ),
    )(lists, counts, projected, *remote)


def routes(neighbours, counts, at_tok, tok_size, blocks):
    lists = neighbours.reshape(tok_size, blocks * NEIGH)
    valid = (jnp.arange(NEIGH)[None, :] < counts[:, None]).reshape(tok_size, blocks * NEIGH)
    owner = lists // blocks
    peers = jnp.arange(tok_size) ^ at_tok
    named = valid & (owner == at_tok)
    low = jnp.min(jnp.where(named, lists, tok_size * blocks), axis=1)
    high = jnp.max(jnp.where(named, lists, -1), axis=1)
    base = at_tok * blocks
    sends = jnp.clip(jnp.stack([low, high], axis=1) - base, 0, blocks - 1)
    send_ids = sends[peers]
    mine = lax.dynamic_slice_in_dim(lists, at_tok, 1, 0)[0]
    mine_valid = lax.dynamic_slice_in_dim(valid, at_tok, 1, 0)[0]
    mine_owner = mine // blocks
    same = (mine_owner[:, None] == mine_owner[None, :]) & mine_valid[None, :]
    first = jnp.min(jnp.where(same, mine[None, :], tok_size * blocks), axis=1)
    slot = (mine != first).astype(jnp.int32)
    there = blocks + ((mine_owner ^ at_tok) - 1) * 2 + slot
    pool_at = jnp.where(mine_owner == at_tok, mine - base, there)
    pool_at = jnp.where(mine_valid, pool_at, 0).reshape(blocks, NEIGH)
    my_counts = lax.dynamic_slice_in_dim(counts, at_tok * blocks, blocks, 0)
    return send_ids.astype(jnp.int32), pool_at.astype(jnp.int32), my_counts


def column_chunks(width):
    return 2 if width % (4 * HEAD_WIDTH) == 0 else 1


def shards(tokens, qkv_weight, out_weight, neighbours, counts, *, tok_size, hid_size):
    at_tok, at_hid = lax.axis_index("tok"), lax.axis_index("hid")
    blocks = tokens.shape[0] // BLK
    place = jnp.stack([at_hid, at_tok]).astype(jnp.int32)
    width = tokens.shape[1]
    chunks = column_chunks(width)
    cut = width // chunks
    parts = []
    for c in range(chunks):
        own = tokens[:, c * cut : (c + 1) * cut]
        parts.append((own, *line_gather(own, "hid", hid_size)))
    qkv_pieces = exchange_gather(qkv_weight, "tok", tok_size)
    out_pieces = exchange_gather(out_weight, "tok", tok_size)
    send_ids, pool_at, my_counts = routes(neighbours, counts, at_tok, tok_size, blocks)

    total = qkv_weight.shape[1]
    step = 256 if total % 256 == 0 else 128
    projected, *sends = project(
        place, send_ids, parts, qkv_pieces, (0, total), step, tok_size, hid_size, True
    )
    remote = [
        lax.ppermute(sends[s - 1], "tok", [(i, i ^ s) for i in range(tok_size)]) for s in range(1, tok_size)
    ]
    mixed = attend(pool_at, my_counts, projected, remote, tok_size)
    parts = []
    for c in range(chunks):
        own = mixed[:, c * cut : (c + 1) * cut]
        parts.append((own, *line_gather(own, "hid", hid_size)))
    out_columns = out_weight.shape[1]
    (result,) = project(
        place, send_ids, parts, out_pieces, (0, out_columns), min(256, out_columns), tok_size, hid_size, False
    )
    return result


def solution(mesh):
    placed = (P("tok", "hid"), P("tok", "hid"), P("tok", "hid"), P(), P())
    return jax.shard_map(
        functools.partial(shards, tok_size=mesh.shape["tok"], hid_size=mesh.shape["hid"]),
        mesh=mesh, in_specs=placed, out_specs=P("tok", "hid"), check_vma=False,
    )
```

time: 407 us -> 220 us (0.54)
  waiting for transfers between devices: 248 us -> 70.9 us
  starting transfers between devices: 0.16 us -> 88.7 us
  local copies, waits for them, and re-layouts: 90.2 us -> 10.7 us
  Pallas kernels: 0 us -> 45.1 us
  matrix products: 36.5 us -> 0 us
  other arithmetic: 18.2 us -> 3.07 us
  between operations: 13.2 us -> 0.64 us
    all_gather x5 -> x0, waiting for transfers between devices: 246 us -> none  [the longest x1 68.7 us: shards(): key_pool = lax.all_gather(key_values, 'tok', axis=0, tiled=True)]
    ppermute x0 -> x45, starting transfers between devices: none -> 88.7 us  [the longest x12 56.7 us: line_gather(): left = lax.ppermute(left, axis, to_right)]
    ppermute x0 -> x45, waiting for transfers between devices: none -> 70.9 us  [the longest x12 27.3 us: line_gather(): right = lax.ppermute(right, axis, to_left)]
    pallas_call x0 -> x3, Pallas kernels: none -> 45.1 us  [the longest x2 25.9 us: project(): pl.pallas_call(functools.partial(project_kernel, chunks=chunks, hid_size=...]
    reshape x3 -> x1, local copies, waits for them, and re-layouts: 32.2 us -> 0.07 us  [routes(): lists = neighbours.reshape(tok_size, blocks * NEIGH)]
    slice x3 -> x2, local copies, waits for them, and re-layouts: 33.8 us -> 2.34 us  [the longest x1 1.17 us: shards(): own = mixed[:, c * cut:(c + 1) * cut]]
    dot_general x3 -> x0, matrix products: 26.5 us -> none  [the longest x1 12.1 us: shards(): jnp.einsum('bhqjk,bjkhd->bqhd', attention_probs, gathered[..., 1, :], pre...]
    gather x1, local copies, waits for them, and re-layouts: 12.1 us -> 1.14 us  [routes(): send_ids = sends[peers]]
  transfers between devices with their start and end apart: 5 -> 45, of which waited for: 4 -> 26; matrix products, arithmetic and copies ran while one was open for 29% -> 4% of each run, Pallas kernels for 0% -> 9%
where the time goes in v1:
time: 220 us; the launch traced here: 219 us
  starting transfers between devices  88.7 us (40%)
  waiting for transfers between devices  70.9 us (32%)
  Pallas kernels  45.1 us (20%)
  local copies, waits for them, and re-layouts  10.7 us (5%)
  other arithmetic  3.07 us (1%)
    ppermute x12, starting transfers between devices, line_gather(): left = lax.ppermute(left, axis, to_right)  56.7 us
    ppermute x12, waiting for transfers between devices, line_gather(): right = lax.ppermute(right, axis, to_left)  27.3 us
    pallas_call x2, Pallas kernels, project(): pl.pallas_call(functools.partial(project_kernel, chunks=chunks, hid_size=...  25.9 us
    ppermute x12, waiting for transfers between devices, line_gather(): left = lax.ppermute(left, axis, to_right)  20.2 us
    pallas_call x1, Pallas kernels, attend(): pl.pallas_call(functools.partial(attend_kernel, tok_size=tok_size, heads=...  19.2 us
    ppermute x7, waiting for transfers between devices, shards(): lax.ppermute(sends[s - 1], 'tok', [(i, i ^ s) for i in range(tok_size)])  18.1 us
    ppermute x12, starting transfers between devices, line_gather(): right = lax.ppermute(right, axis, to_left)  15.4 us
    ppermute x6, starting transfers between devices, exchange_gather(): pieces[s] = lax.ppermute(shard, axis, [(i, i ^ s) for i in range(size)])  9.75 us
  transfers between devices with their start and end apart: 45, of which 26 were waited for; matrix products, arithmetic and copies ran while one was open for 4% of the time, Pallas kernels for 9%

profile of v1, /device:TPU:0, one launch (start us, length us, event | category | flops | bytes accessed | tf_op | source)
XLA Modules:
  0.0 219.0 jit_solution(12595632114399176904)
XLA Ops:
  1.2 1.3 collective-permute-start.9
  2.5 5.6 %collective-permute-start = (bf16[768,256]{1,0:T(8,128)(2,1)S(1)}, bf16[768,256]{1,0:T(8,128)(2,1)S(1)}, u32[]{:S(2)}, u32[]{:S(2)}) collective-permute-start(bf16[768,256]{1,0:T(8,128)(2,1)S(1)} %get-tuple-element.28.refs_0_), channel_id=1, source_target_pairs={{0,1},{1,2},{2,3},{4,5},{5,6},{6,7},{8,9},{9,10},{10,11},{12,13},{... | collective-permute-start | bytes 1179656 | tf_op jit(solution)/shard_map/ppermute | solution.py:22
  8.1 1.3 collective-permute-start.3
  9.4 5.3 %collective-permute-start.6 = (bf16[768,256]{1,0:T(8,128)(2,1)S(1)}, bf16[768,256]{1,0:T(8,128)(2,1)}, u32[]{:S(2)}, u32[]{:S(2)}) collective-permute-start(bf16[768,256]{1,0:T(8,128)(2,1)S(1)} %get-tuple-element.27.refs_7_), channel_id=1, source_target_pairs={{0,1},{1,2},{2,3},{4,5},{5,6},{6,7},{8,9},{9,10},{10,11},{12,13},{... | collective-permute-start | bytes 1179656 | tf_op jit(solution)/shard_map/ppermute | solution.py:22
  14.7 1.3 collective-permute-done.9.refs_11_
  16.1 1.3 collective-permute-start.10
  17.6 5.2 %collective-permute-start.1 = (bf16[768,256]{1,0:T(8,128)(2,1)S(1)}, bf16[768,256]{1,0:T(8,128)(2,1)}, u32[]{:S(2)}, u32[]{:S(2)}) collective-permute-start(bf16[768,256]{1,0:T(8,128)(2,1)S(1)} %collective-permute-done.refs_1_), channel_id=1, source_target_pairs={{0,1},{1,2},{2,3},{4,5},{5,6},{6,7},{8,9},{9,10},{10,11},{12,13},{... | collective-permute-start | bytes 1179656 | tf_op jit(solution)/shard_map/ppermute | solution.py:22
  22.8 1.7 collective-permute-done.3.refs_4_
  24.5 1.3 collective-permute-start.4
  25.8 2.0 collective-permute-start.13
  27.8 1.5 collective-permute-start.15
  29.3 3.6 %collective-permute-done.10.refs_12_ = bf16[768,256]{1,0:T(8,128)(2,1)S(1)} collective-permute-done((bf16[768,256]{1,0:T(8,128)(2,1)S(1)}, bf16[768,256]{1,0:T(8,128)(2,1)S(1)}, u32[]{:S(2)}, u32[]{:S(2)}) %collective-permute-start.10) | collective-permute-done | bytes 393248 | tf_op jit(solution)/shard_map/ppermute | solution.py:23
  32.9 2.9 %collective-permute-start.17 = (bf16[256,1536]{1,0:T(8,128)(2,1)}, bf16[256,1536]{1,0:T(8,128)(2,1)}, u32[]{:S(2)}, u32[]{:S(2)}) collective-permute-start(bf16[256,1536]{1,0:T(8,128)(2,1)} %refs_14_.2), channel_id=1, source_target_pairs={{0,24},{4,28},{8,16},{12,20},{16,8},{20,12},{24,0},{28,4},{1,25},{... | collective-permute-start | bytes 2359304 | tf_op jit(solution)/shard_map/ppermute | solution.py:32
  35.8 4.7 %collective-permute-done.4.refs_5_ = bf16[768,256]{1,0:T(8,128)(2,1)S(1)} collective-permute-done((bf16[768,256]{1,0:T(8,128)(2,1)S(1)}, bf16[768,256]{1,0:T(8,128)(2,1)S(1)}, u32[]{:S(2)}, u32[]{:S(2)}) %collective-permute-start.4) | collective-permute-done | bytes 393248 | tf_op jit(solution)/shard_map/ppermute | solution.py:23
  41.3 3.6 %collective-permute-start.7 = (bf16[768,256]{1,0:T(8,128)(2,1)}, bf16[768,256]{1,0:T(8,128)(2,1)S(1)}, u32[]{:S(2)}, u32[]{:S(2)}) collective-permute-start(bf16[768,256]{1,0:T(8,128)(2,1)} %collective-permute-done.6.refs_8_), channel_id=1, source_target_pairs={{0,1},{1,2},{2,3},{4,5},{5,6},{6,7},{8,9},{9,10},{10,11},{12,13},{... | collective-permute-start | bytes 1179656 | tf_op jit(solution)/shard_map/ppermute | solution.py:22
  46.1 6.6 %collective-permute-done.7.refs_9_ = bf16[768,256]{1,0:T(8,128)(2,1)S(1)} collective-permute-done((bf16[768,256]{1,0:T(8,128)(2,1)}, bf16[768,256]{1,0:T(8,128)(2,1)S(1)}, u32[]{:S(2)}, u32[]{:S(2)}) %collective-permute-start.7) | collective-permute-done | bytes 393248 | tf_op jit(solution)/shard_map/ppermute | solution.py:22
  54.0 5.7 %collective-permute-start.2 = (bf16[768,256]{1,0:T(8,128)(2,1)}, bf16[768,256]{1,0:T(8,128)(2,1)}, u32[]{:S(2)}, u32[]{:S(2)}) collective-permute-start(bf16[768,256]{1,0:T(8,128)(2,1)} %collective-permute-done.1.refs_2_), channel_id=1, source_target_pairs={{0,1},{1,2},{2,3},{4,5},{5,6},{6,7},{8,9},{9,10},{10,11},{12,13},{... | collective-permute-start | bytes 1179656 | tf_op jit(solution)/shard_map/ppermute | solution.py:22
  59.7 2.2 collective-permute-done.15.refs_18_
  65.6 1.3 collective-permute-start.5
  66.9 4.9 %collective-permute-start.8 = (bf16[768,256]{1,0:T(8,128)(2,1)}, bf16[768,256]{1,0:T(8,128)(2,1)S(1)}, u32[]{:S(2)}, u32[]{:S(2)}) collective-permute-start(bf16[768,256]{1,0:T(8,128)(2,1)} %copy-done.36), channel_id=1, source_target_pairs={{0,1},{1,2},{2,3},{4,5},{5,6},{6,7},{8,9},{9,10},{10,11},{12,13},{... | collective-permute-start | bytes 1179656 | tf_op jit(solution)/shard_map/ppermute | solution.py:22
  72.4 7.3 %collective-permute-done.5.refs_6_ = bf16[768,256]{1,0:T(8,128)(2,1)S(1)} collective-permute-done((bf16[768,256]{1,0:T(8,128)(2,1)}, bf16[768,256]{1,0:T(8,128)(2,1)S(1)}, u32[]{:S(2)}, u32[]{:S(2)}) %collective-permute-start.5) | collective-permute-done | bytes 393248 | tf_op jit(solution)/shard_map/ppermute | solution.py:23
  79.8 1.3 collective-permute-done.8.refs_10_
  81.9 17.9 %shard_map.55 = (bf16[768,1536]{1,0:T(8,128)(2,1)}, bf16[128,1024]{1,0:T(8,128)(2,1)}, bf16[128,1024]{1,0:T(8,128)(2,1)}, bf16[128,1024]{1,0:T(8,128)(2,1)}, bf1...) custom-call(s32[2]{0:T(128)} %pad_add_fusion.1.place, ...), custom_call_target="tpu_custom_call" | custom-call | flops 4831838208 | bytes 9437184 | tf_op jit(solution)/shard_map/pallas_call | solution.py:129
  103.0 1.5 collective-permute-start.22
  104.7 1.5 collective-permute-start.24
  106.2 3.1 %collective-permute-done.20.refs_1_ = bf16[128,1024]{1,0:T(8,128)(2,1)S(1)} collective-permute-done((bf16[128,1024]{1,0:T(8,128)(2,1)}, bf16[128,1024]{1,0:T(8,128)(2,1)S(1)}, u32[]{:S(2)}, u32[]{:S(2)}) %collective-permute-start.20) | collective-permute-done | bytes 262176 | tf_op jit(solution)/shard_map/ppermute | solution.py:271
  111.2 2.7 %collective-permute-done.21.refs_2_ = bf16[128,1024]{1,0:T(8,128)(2,1)S(1)} collective-permute-done((bf16[128,1024]{1,0:T(8,128)(2,1)}, bf16[128,1024]{1,0:T(8,128)(2,1)S(1)}, u32[]{:S(2)}, u32[]{:S(2)}) %collective-permute-start.21) | collective-permute-done | bytes 262176 | tf_op jit(solution)/shard_map/ppermute | solution.py:271
  116.0 12.3 %collective-permute-done.23.refs_4_ = bf16[128,1024]{1,0:T(8,128)(2,1)S(1)} collective-permute-done((bf16[128,1024]{1,0:T(8,128)(2,1)}, bf16[128,1024]{1,0:T(8,128)(2,1)S(1)}, u32[]{:S(2)}, u32[]{:S(2)}) %collective-permute-start.23) | collective-permute-done | bytes 262176 | tf_op jit(solution)/shard_map/ppermute | solution.py:271
  130.3 19.2 %shard_map.56 = bf16[768,512]{1,0:T(8,128)(2,1)} custom-call(s32[12,9]{1,0:T(8,128)} %select_select_fusion.lists, s32[12]{0:T(128)} %dynamic_slice.11.counts, bf16[768,1536]{1,0:T(8,128)(2,1)} %get-tuple-element.13.projected, bf16[128,1024]{1,0:T(8,128)(2,1)} %copy-done.17, bf16[128,1024]{1,0:T(8,128)(2,1)} %copy-done.19, bf16[128,1024]{1,0:T(8,128)(2,1)} %copy-done.21, ...), custom_call_target="tpu_custom_call" | custom-call | flops 905969664 | bytes 12582912 | tf_op jit(solution)/shard_map/pallas_call | solution.py:202
  150.7 4.2 %collective-permute-start.26 = (bf16[768,256]{1,0:T(8,128)(2,1)S(1)}, bf16[768,256]{1,0:T(8,128)(2,1)S(1)}, u32[]{:S(2)}, u32[]{:S(2)}) collective-permute-start(bf16[768,256]{1,0:T(8,128)(2,1)S(1)} %get-tuple-element.26.refs_0_), channel_id=1, source_target_pairs={{0,1},{1,2},{2,3},{4,5},{5,6},{6,7},{8,9},{9,10},{10,11},{12,13},{... | collective-permute-start | bytes 1179656 | tf_op jit(solution)/shard_map/ppermute | solution.py:22
  154.9 1.3 collective-permute-start.29
  156.2 4.6 %collective-permute-start.32 = (bf16[768,256]{1,0:T(8,128)(2,1)S(1)}, bf16[768,256]{1,0:T(8,128)(2,1)S(1)}, u32[]{:S(2)}, u32[]{:S(2)}) collective-permute-start(bf16[768,256]{1,0:T(8,128)(2,1)S(1)} %get-tuple-element.25.refs_7_), channel_id=1, source_target_pairs={{0,1},{1,2},{2,3},{4,5},{5,6},{6,7},{8,9},{9,10},{10,11},{12,13},{... | collective-permute-start | bytes 1179656 | tf_op jit(solution)/shard_map/ppermute | solution.py:22
  160.8 1.3 collective-permute-start.35
  162.5 1.3 collective-permute-done.38.refs_15_
  164.3 4.4 %collective-permute-start.27 = (bf16[768,256]{1,0:T(8,128)(2,1)S(1)}, bf16[768,256]{1,0:T(8,128)(2,1)S(1)}, u32[]{:S(2)}, u32[]{:S(2)}) collective-permute-start(bf16[768,256]{1,0:T(8,128)(2,1)S(1)} %collective-permute-done.26.refs_1_), channel_id=1, source_target_pairs={{0,1},{1,2},{2,3},{4,5},{5,6},{6,7},{8,9},{9,10},{10,11},{12,13},{... | collective-permute-start | bytes 1179656 | tf_op jit(solution)/shard_map/ppermute | solution.py:22
  168.8 1.3 collective-permute-start.30
  170.1 2.6 %collective-permute-done.32.refs_8_ = bf16[768,256]{1,0:T(8,128)(2,1)S(1)} collective-permute-done((bf16[768,256]{1,0:T(8,128)(2,1)S(1)}, bf16[768,256]{1,0:T(8,128)(2,1)S(1)}, u32[]{:S(2)}, u32[]{:S(2)}) %collective-permute-start.32) | collective-permute-done | bytes 393248 | tf_op jit(solution)/shard_map/ppermute | solution.py:22
  172.7 4.4 %collective-permute-start.33 = (bf16[768,256]{1,0:T(8,128)(2,1)S(1)}, bf16[768,256]{1,0:T(8,128)(2,1)S(1)}, u32[]{:S(2)}, u32[]{:S(2)}) collective-permute-start(bf16[768,256]{1,0:T(8,128)(2,1)S(1)} %collective-permute-done.32.refs_8_), channel_id=1, source_target_pairs={{0,1},{1,2},{2,3},{4,5},{5,6},{6,7},{8,9},{9,10},{10,11},{12,13},{... | collective-permute-start | bytes 1179656 | tf_op jit(solution)/shard_map/ppermute | solution.py:22
  177.2 1.3 collective-permute-start.36
  179.2 1.9 collective-permute-done.27.refs_2_
  181.1 4.4 %collective-permute-start.28 = (bf16[768,256]{1,0:T(8,128)(2,1)S(1)}, bf16[768,256]{1,0:T(8,128)(2,1)S(1)}, u32[]{:S(2)}, u32[]{:S(2)}) collective-permute-start(bf16[768,256]{1,0:T(8,128)(2,1)S(1)} %collective-permute-done.27.refs_2_), channel_id=1, source_target_pairs={{0,1},{1,2},{2,3},{4,5},{5,6},{6,7},{8,9},{9,10},{10,11},{12,13},{... | collective-permute-start | bytes 1179656 | tf_op jit(solution)/shard_map/ppermute | solution.py:22
  187.0 2.6 %collective-permute-done.33.refs_9_ = bf16[768,256]{1,0:T(8,128)(2,1)S(1)} collective-permute-done((bf16[768,256]{1,0:T(8,128)(2,1)S(1)}, bf16[768,256]{1,0:T(8,128)(2,1)S(1)}, u32[]{:S(2)}, u32[]{:S(2)}) %collective-permute-start.33) | collective-permute-done | bytes 393248 | tf_op jit(solution)/shard_map/ppermute | solution.py:22
  189.6 4.4 %collective-permute-start.34 = (bf16[768,256]{1,0:T(8,128)(2,1)S(1)}, bf16[768,256]{1,0:T(8,128)(2,1)S(1)}, u32[]{:S(2)}, u32[]{:S(2)}) collective-permute-start(bf16[768,256]{1,0:T(8,128)(2,1)S(1)} %collective-permute-done.33.refs_9_), channel_id=1, source_target_pairs={{0,1},{1,2},{2,3},{4,5},{5,6},{6,7},{8,9},{9,10},{10,11},{12,13},{... | collective-permute-start | bytes 1179656 | tf_op jit(solution)/shard_map/ppermute | solution.py:22
  195.5 1.7 collective-permute-done.44.refs_21_
  198.0 4.5 %collective-permute-done.31.refs_6_ = bf16[768,256]{1,0:T(8,128)(2,1)S(1)} collective-permute-done((bf16[768,256]{1,0:T(8,128)(2,1)S(1)}, bf16[768,256]{1,0:T(8,128)(2,1)S(1)}, u32[]{:S(2)}, u32[]{:S(2)}) %collective-permute-start.31) | collective-permute-done | bytes 393248 | tf_op jit(solution)/shard_map/ppermute | solution.py:23
  202.5 3.9 %collective-permute-done.34.refs_10_ = bf16[768,256]{1,0:T(8,128)(2,1)S(1)} collective-permute-done((bf16[768,256]{1,0:T(8,128)(2,1)S(1)}, bf16[768,256]{1,0:T(8,128)(2,1)S(1)}, u32[]{:S(2)}, u32[]{:S(2)}) %collective-permute-start.34) | collective-permute-done | bytes 393248 | tf_op jit(solution)/shard_map/ppermute | solution.py:22
  207.2 3.7 %collective-permute-done.37.refs_13_ = bf16[768,256]{1,0:T(8,128)(2,1)} collective-permute-done((bf16[768,256]{1,0:T(8,128)(2,1)S(1)}, bf16[768,256]{1,0:T(8,128)(2,1)}, u32[]{:S(2)}, u32[]{:S(2)}) %collective-permute-start.37) | collective-permute-done | bytes 393248 | tf_op jit(solution)/shard_map/ppermute | solution.py:23
  211.0 8.0 %shard_map.57 = bf16[768,512]{1,0:T(8,128)(2,1)} custom-call(s32[2]{0:T(128)} %pad_add_fusion.1.place, s32[8,2]{1,0:T(8,128)} %gather_fusion, bf16[768,256]{1,0:T(8,128)(2,1)} %copy-done.1, bf16[768,256]{1,0:T(8,128)(2,1)} %copy-done.4, bf16[768,256]{1,0:T(8,128)(2,1)} %copy-done.8, bf16[768,256]{1,0:T(8,128)(2,1)} %copy-done.12, ...), custom_call_target="tpu_custom_call" | custom-call | flops 1610612736 | bytes 5242880 | tf_op jit(solution)/shard_map/pallas_call | solution.py:129
  (155 shorter events, 26.4 us)
Async XLA Ops:
  1.2 80.7 %copy-start.2 = (bf16[768,256]{1,0:T(8,128)(2,1)}, bf16[768,256]{1,0:T(8,128)(2,1)S(1)}, u32[]{:S(2)}) copy-start(bf16[768,256]{1,0:T(8,128)(2,1)S(1)} %get-tuple-element.27.refs_7_) | copy-start | bytes 1179652
  1.2 80.7 %copy-start.3 = (bf16[768,256]{1,0:T(8,128)(2,1)}, bf16[768,256]{1,0:T(8,128)(2,1)S(1)}, u32[]{:S(2)}) copy-start(bf16[768,256]{1,0:T(8,128)(2,1)S(1)} %get-tuple-element.28.refs_0_) | copy-start | bytes 1179652
  1.2 14.9 %collective-permute-start.9 = (bf16[768,256]{1,0:T(8,128)(2,1)S(1)}, bf16[768,256]{1,0:T(8,128)(2,1)S(1)}, u32[]{:S(2)}, u32[]{:S(2)}) collective-permute-start(bf16[768,256]{1,0:T(8,128)(2,1)S(1)} %get-tuple-element.27.refs_7_), channel_id=1, source_target_pairs={{1,0},{2,1},{3,2},{5,4},{6,5},{7,6},{9,8},{10,9},{11,10},{13,12},{... | collective-permute-start | bytes 1179656 | tf_op jit(solution)/shard_map/ppermute | solution.py:23
  2.5 15.1 %collective-permute-start = (bf16[768,256]{1,0:T(8,128)(2,1)S(1)}, bf16[768,256]{1,0:T(8,128)(2,1)S(1)}, u32[]{:S(2)}, u32[]{:S(2)}) collective-permute-start(bf16[768,256]{1,0:T(8,128)(2,1)S(1)} %get-tuple-element.28.refs_0_), channel_id=1, source_target_pairs={{0,1},{1,2},{2,3},{4,5},{5,6},{6,7},{8,9},{9,10},{10,11},{12,13},{... | collective-permute-start | bytes 1179656 | tf_op jit(solution)/shard_map/ppermute | solution.py:22
  8.1 16.4 %collective-permute-start.3 = (bf16[768,256]{1,0:T(8,128)(2,1)S(1)}, bf16[768,256]{1,0:T(8,128)(2,1)S(1)}, u32[]{:S(2)}, u32[]{:S(2)}) collective-permute-start(bf16[768,256]{1,0:T(8,128)(2,1)S(1)} %get-tuple-element.28.refs_0_), channel_id=1, source_target_pairs={{1,0},{2,1},{3,2},{5,4},{6,5},{7,6},{9,8},{10,9},{11,10},{13,12},{... | collective-permute-start | bytes 1179656 | tf_op jit(solution)/shard_map/ppermute | solution.py:23
  9.4 18.4 %collective-permute-start.6 = (bf16[768,256]{1,0:T(8,128)(2,1)S(1)}, bf16[768,256]{1,0:T(8,128)(2,1)}, u32[]{:S(2)}, u32[]{:S(2)}) collective-permute-start(bf16[768,256]{1,0:T(8,128)(2,1)S(1)} %get-tuple-element.27.refs_7_), channel_id=1, source_target_pairs={{0,1},{1,2},{2,3},{4,5},{5,6},{6,7},{8,9},{9,10},{10,11},{12,13},{... | collective-permute-start | bytes 1179656 | tf_op jit(solution)/shard_map/ppermute | solution.py:22
  16.1 65.8 %copy-start.31 = (bf16[768,256]{1,0:T(8,128)(2,1)}, bf16[768,256]{1,0:T(8,128)(2,1)S(1)}, u32[]{:S(2)}) copy-start(bf16[768,256]{1,0:T(8,128)(2,1)S(1)} %collective-permute-done.9.refs_11_) | copy-start | bytes 1179652
  16.1 16.9 %collective-permute-start.10 = (bf16[768,256]{1,0:T(8,128)(2,1)S(1)}, bf16[768,256]{1,0:T(8,128)(2,1)S(1)}, u32[]{:S(2)}, u32[]{:S(2)}) collective-permute-start(bf16[768,256]{1,0:T(8,128)(2,1)S(1)} %collective-permute-done.9.refs_11_), channel_id=1, source_target_pairs={{1,0},{2,1},{3,2},{5,4},{6,5},{7,6},{9,8},{10,9},{11,10},{13,12},{... | collective-permute-start | bytes 1179656 | tf_op jit(solution)/shard_map/ppermute | solution.py:23
  17.6 18.3 %collective-permute-start.1 = (bf16[768,256]{1,0:T(8,128)(2,1)S(1)}, bf16[768,256]{1,0:T(8,128)(2,1)}, u32[]{:S(2)}, u32[]{:S(2)}) collective-permute-start(bf16[768,256]{1,0:T(8,128)(2,1)S(1)} %collective-permute-done.refs_1_), channel_id=1, source_target_pairs={{0,1},{1,2},{2,3},{4,5},{5,6},{6,7},{8,9},{9,10},{10,11},{12,13},{... | collective-permute-start | bytes 1179656 | tf_op jit(solution)/shard_map/ppermute | solution.py:22
  24.5 16.0 %collective-permute-start.4 = (bf16[768,256]{1,0:T(8,128)(2,1)S(1)}, bf16[768,256]{1,0:T(8,128)(2,1)S(1)}, u32[]{:S(2)}, u32[]{:S(2)}) collective-permute-start(bf16[768,256]{1,0:T(8,128)(2,1)S(1)} %collective-permute-done.3.refs_4_), channel_id=1, source_target_pairs={{1,0},{2,1},{3,2},{5,4},{6,5},{7,6},{9,8},{10,9},{11,10},{13,12},{... | collective-permute-start | bytes 1179656 | tf_op jit(solution)/shard_map/ppermute | solution.py:23
  25.8 28.2 %collective-permute-start.13 = (bf16[256,1536]{1,0:T(8,128)(2,1)}, bf16[256,1536]{1,0:T(8,128)(2,1)S(1)}, u32[]{:S(2)}, u32[]{:S(2)}) collective-permute-start(bf16[256,1536]{1,0:T(8,128)(2,1)} %refs_14_.2), channel_id=1, source_target_pairs={{0,8},{4,12},{8,0},{12,4},{16,24},{20,28},{24,16},{28,20},{1,9},{5... | collective-permute-start | bytes 2359304 | tf_op jit(solution)/shard_map/ppermute | solution.py:32
  27.8 34.0 %collective-permute-start.15 = (bf16[256,1536]{1,0:T(8,128)(2,1)}, bf16[256,1536]{1,0:T(8,128)(2,1)S(1)}, u32[]{:S(2)}, u32[]{:S(2)}) collective-permute-start(bf16[256,1536]{1,0:T(8,128)(2,1)} %refs_14_.2), channel_id=1, source_target_pairs={{0,16},{4,20},{8,24},{12,28},{16,0},{20,4},{24,8},{28,12},{1,17},{... | collective-permute-start | bytes 2359304 | tf_op jit(solution)/shard_map/ppermute | solution.py:32
  32.9 28.9 %collective-permute-start.17 = (bf16[256,1536]{1,0:T(8,128)(2,1)}, bf16[256,1536]{1,0:T(8,128)(2,1)}, u32[]{:S(2)}, u32[]{:S(2)}) collective-permute-start(bf16[256,1536]{1,0:T(8,128)(2,1)} %refs_14_.2), channel_id=1, source_target_pairs={{0,24},{4,28},{8,16},{12,20},{16,8},{20,12},{24,0},{28,4},{1,25},{... | collective-permute-start | bytes 2359304 | tf_op jit(solution)/shard_map/ppermute | solution.py:32
  35.8 26.5 %collective-permute-start.12 = (bf16[256,1536]{1,0:T(8,128)(2,1)}, bf16[256,1536]{1,0:T(8,128)(2,1)}, u32[]{:S(2)}, u32[]{:S(2)}) collective-permute-start(bf16[256,1536]{1,0:T(8,128)(2,1)} %refs_14_.2), channel_id=1, source_target_pairs={{0,4},{4,0},{8,12},{12,8},{16,20},{20,16},{24,28},{28,24},{1,5},{5... | collective-permute-start | bytes 2359304 | tf_op jit(solution)/shard_map/ppermute | solution.py:34
  41.3 11.4 %collective-permute-start.7 = (bf16[768,256]{1,0:T(8,128)(2,1)}, bf16[768,256]{1,0:T(8,128)(2,1)S(1)}, u32[]{:S(2)}, u32[]{:S(2)}) collective-permute-start(bf16[768,256]{1,0:T(8,128)(2,1)} %collective-permute-done.6.refs_8_), channel_id=1, source_target_pairs={{0,1},{1,2},{2,3},{4,5},{5,6},{6,7},{8,9},{9,10},{10,11},{12,13},{... | collective-permute-start | bytes 1179656 | tf_op jit(solution)/shard_map/ppermute | solution.py:22
  52.7 12.9 %collective-permute-start.11 = (bf16[768,256]{1,0:T(8,128)(2,1)S(1)}, bf16[768,256]{1,0:T(8,128)(2,1)}, u32[]{:S(2)}, u32[]{:S(2)}) collective-permute-start(bf16[768,256]{1,0:T(8,128)(2,1)S(1)} %collective-permute-done.10.refs_12_), channel_id=1, source_target_pairs={{1,0},{2,1},{3,2},{5,4},{6,5},{7,6},{9,8},{10,9},{11,10},{13,12},{... | collective-permute-start | bytes 1179656 | tf_op jit(solution)/shard_map/ppermute | solution.py:23
  54.0 12.9 %collective-permute-start.2 = (bf16[768,256]{1,0:T(8,128)(2,1)}, bf16[768,256]{1,0:T(8,128)(2,1)}, u32[]{:S(2)}, u32[]{:S(2)}) collective-permute-start(bf16[768,256]{1,0:T(8,128)(2,1)} %collective-permute-done.1.refs_2_), channel_id=1, source_target_pairs={{0,1},{1,2},{2,3},{4,5},{5,6},{6,7},{8,9},{9,10},{10,11},{12,13},{... | collective-permute-start | bytes 1179656 | tf_op jit(solution)/shard_map/ppermute | solution.py:22
  61.9 19.2 %collective-permute-start.14 = (bf16[256,1536]{1,0:T(8,128)(2,1)S(1)}, bf16[256,1536]{1,0:T(8,128)(2,1)}, u32[]{:S(2)}, u32[]{:S(2)}) collective-permute-start(bf16[256,1536]{1,0:T(8,128)(2,1)S(1)} %collective-permute-done.13.refs_16_), channel_id=1, source_target_pairs={{0,4},{4,0},{8,12},{12,8},{16,20},{20,16},{24,28},{28,24},{1,5},{5... | collective-permute-start | bytes 2359304 | tf_op jit(solution)/shard_map/ppermute | solution.py:34
  61.9 19.2 %collective-permute-start.16 = (bf16[256,1536]{1,0:T(8,128)(2,1)S(1)}, bf16[256,1536]{1,0:T(8,128)(2,1)}, u32[]{:S(2)}, u32[]{:S(2)}) collective-permute-start(bf16[256,1536]{1,0:T(8,128)(2,1)S(1)} %collective-permute-done.15.refs_18_), channel_id=1, source_target_pairs={{0,4},{4,0},{8,12},{12,8},{16,20},{20,16},{24,28},{28,24},{1,5},{5... | collective-permute-start | bytes 2359304 | tf_op jit(solution)/shard_map/ppermute | solution.py:34
  62.4 19.4 %collective-permute-start.18 = (bf16[256,1536]{1,0:T(8,128)(2,1)}, bf16[256,1536]{1,0:T(8,128)(2,1)}, u32[]{:S(2)}, u32[]{:S(2)}) collective-permute-start(bf16[256,1536]{1,0:T(8,128)(2,1)} %collective-permute-done.17.refs_20_), channel_id=1, source_target_pairs={{0,4},{4,0},{8,12},{12,8},{16,20},{20,16},{24,28},{28,24},{1,5},{5... | collective-permute-start | bytes 2359304 | tf_op jit(solution)/shard_map/ppermute | solution.py:34
  65.6 14.2 %collective-permute-start.5 = (bf16[768,256]{1,0:T(8,128)(2,1)}, bf16[768,256]{1,0:T(8,128)(2,1)S(1)}, u32[]{:S(2)}, u32[]{:S(2)}) collective-permute-start(bf16[768,256]{1,0:T(8,128)(2,1)} %copy-done.35), channel_id=1, source_target_pairs={{1,0},{2,1},{3,2},{5,4},{6,5},{7,6},{9,8},{10,9},{11,10},{13,12},{... | collective-permute-start | bytes 1179656 | tf_op jit(solution)/shard_map/ppermute | solution.py:23
  66.9 14.2 %collective-permute-start.8 = (bf16[768,256]{1,0:T(8,128)(2,1)}, bf16[768,256]{1,0:T(8,128)(2,1)S(1)}, u32[]{:S(2)}, u32[]{:S(2)}) collective-permute-start(bf16[768,256]{1,0:T(8,128)(2,1)} %copy-done.36), channel_id=1, source_target_pairs={{0,1},{1,2},{2,3},{4,5},{5,6},{6,7},{8,9},{9,10},{10,11},{12,13},{... | collective-permute-start | bytes 1179656 | tf_op jit(solution)/shard_map/ppermute | solution.py:22
  99.8 4.9 %collective-permute-start.19 = (bf16[128,1024]{1,0:T(8,128)(2,1)}, bf16[128,1024]{1,0:T(8,128)(2,1)S(1)}, u32[]{:S(2)}, u32[]{:S(2)}) collective-permute-start(bf16[128,1024]{1,0:T(8,128)(2,1)} %get-tuple-element.14), channel_id=1, source_target_pairs={{0,4},{4,0},{8,12},{12,8},{16,20},{20,16},{24,28},{28,24},{1,5},{5... | collective-permute-start | bytes 786440 | tf_op jit(solution)/shard_map/ppermute | solution.py:271
  99.9 9.4 %collective-permute-start.20 = (bf16[128,1024]{1,0:T(8,128)(2,1)}, bf16[128,1024]{1,0:T(8,128)(2,1)S(1)}, u32[]{:S(2)}, u32[]{:S(2)}) collective-permute-start(bf16[128,1024]{1,0:T(8,128)(2,1)} %get-tuple-element.15), channel_id=1, source_target_pairs={{0,8},{4,12},{8,0},{12,4},{16,24},{20,28},{24,16},{28,20},{1,9},{5... | collective-permute-start | bytes 786440 | tf_op jit(solution)/shard_map/ppermute | solution.py:271
  102.0 12.0 %collective-permute-start.21 = (bf16[128,1024]{1,0:T(8,128)(2,1)}, bf16[128,1024]{1,0:T(8,128)(2,1)S(1)}, u32[]{:S(2)}, u32[]{:S(2)}) collective-permute-start(bf16[128,1024]{1,0:T(8,128)(2,1)} %get-tuple-element.16), channel_id=1, source_target_pairs={{0,12},{4,8},{8,4},{12,0},{16,28},{20,24},{24,20},{28,16},{1,13},{... | collective-permute-start | bytes 786440 | tf_op jit(solution)/shard_map/ppermute | solution.py:271
  103.0 11.9 %collective-permute-start.22 = (bf16[128,1024]{1,0:T(8,128)(2,1)}, bf16[128,1024]{1,0:T(8,128)(2,1)S(1)}, u32[]{:S(2)}, u32[]{:S(2)}) collective-permute-start(bf16[128,1024]{1,0:T(8,128)(2,1)} %get-tuple-element.17), channel_id=1, source_target_pairs={{0,16},{4,20},{8,24},{12,28},{16,0},{20,4},{24,8},{28,12},{1,17},{... | collective-permute-start | bytes 786440 | tf_op jit(solution)/shard_map/ppermute | solution.py:271
  104.5 23.8 %collective-permute-start.23 = (bf16[128,1024]{1,0:T(8,128)(2,1)}, bf16[128,1024]{1,0:T(8,128)(2,1)S(1)}, u32[]{:S(2)}, u32[]{:S(2)}) collective-permute-start(bf16[128,1024]{1,0:T(8,128)(2,1)} %get-tuple-element.18), channel_id=1, source_target_pairs={{0,20},{4,16},{8,28},{12,24},{16,4},{20,0},{24,12},{28,8},{1,21},{... | collective-permute-start | bytes 786440 | tf_op jit(solution)/shard_map/ppermute | solution.py:271
  104.7 24.8 %collective-permute-start.24 = (bf16[128,1024]{1,0:T(8,128)(2,1)}, bf16[128,1024]{1,0:T(8,128)(2,1)S(1)}, u32[]{:S(2)}, u32[]{:S(2)}) collective-permute-start(bf16[128,1024]{1,0:T(8,128)(2,1)} %get-tuple-element.19), channel_id=1, source_target_pairs={{0,24},{4,28},{8,16},{12,20},{16,8},{20,12},{24,0},{28,4},{1,25},{... | collective-permute-start | bytes 786440 | tf_op jit(solution)/shard_map/ppermute | solution.py:271
  109.2 20.3 %collective-permute-start.25 = (bf16[128,1024]{1,0:T(8,128)(2,1)}, bf16[128,1024]{1,0:T(8,128)(2,1)S(1)}, u32[]{:S(2)}, u32[]{:S(2)}) collective-permute-start(bf16[128,1024]{1,0:T(8,128)(2,1)} %get-tuple-element.20), channel_id=1, source_target_pairs={{0,28},{4,24},{8,20},{12,16},{16,12},{20,8},{24,4},{28,0},{1,29},{... | collective-permute-start | bytes 786440 | tf_op jit(solution)/shard_map/ppermute | solution.py:271
  114.0 42.3 %collective-permute-start.39 = (bf16[256,512]{1,0:T(8,128)(2,1)S(1)}, bf16[256,512]{1,0:T(8,128)(2,1)}, u32[]{:S(2)}, u32[]{:S(2)}) collective-permute-start(bf16[256,512]{1,0:T(8,128)(2,1)S(1)} %copy-done.15), channel_id=1, source_target_pairs={{0,8},{4,12},{8,0},{12,4},{16,24},{20,28},{24,16},{28,20},{1,9},{5... | collective-permute-start | bytes 786440 | tf_op jit(solution)/shard_map/ppermute | solution.py:32
  114.8 46.0 %collective-permute-start.41 = (bf16[256,512]{1,0:T(8,128)(2,1)S(1)}, bf16[256,512]{1,0:T(8,128)(2,1)}, u32[]{:S(2)}, u32[]{:S(2)}) collective-permute-start(bf16[256,512]{1,0:T(8,128)(2,1)S(1)} %copy-done.15), channel_id=1, source_target_pairs={{0,16},{4,20},{8,24},{12,28},{16,0},{20,4},{24,8},{28,12},{1,17},{... | collective-permute-start | bytes 786440 | tf_op jit(solution)/shard_map/ppermute | solution.py:32
  128.3 33.8 %collective-permute-start.43 = (bf16[256,512]{1,0:T(8,128)(2,1)S(1)}, bf16[256,512]{1,0:T(8,128)(2,1)S(1)}, u32[]{:S(2)}, u32[]{:S(2)}) collective-permute-start(bf16[256,512]{1,0:T(8,128)(2,1)S(1)} %copy-done.15), channel_id=1, source_target_pairs={{0,24},{4,28},{8,16},{12,20},{16,8},{20,12},{24,0},{28,4},{1,25},{... | collective-permute-start | bytes 786440 | tf_op jit(solution)/shard_map/ppermute | solution.py:32
  150.7 13.6 %collective-permute-start.26 = (bf16[768,256]{1,0:T(8,128)(2,1)S(1)}, bf16[768,256]{1,0:T(8,128)(2,1)S(1)}, u32[]{:S(2)}, u32[]{:S(2)}) collective-permute-start(bf16[768,256]{1,0:T(8,128)(2,1)S(1)} %get-tuple-element.26.refs_0_), channel_id=1, source_target_pairs={{0,1},{1,2},{2,3},{4,5},{5,6},{6,7},{8,9},{9,10},{10,11},{12,13},{... | collective-permute-start | bytes 1179656 | tf_op jit(solution)/shard_map/ppermute | solution.py:22
  154.9 13.9 %collective-permute-start.29 = (bf16[768,256]{1,0:T(8,128)(2,1)S(1)}, bf16[768,256]{1,0:T(8,128)(2,1)S(1)}, u32[]{:S(2)}, u32[]{:S(2)}) collective-permute-start(bf16[768,256]{1,0:T(8,128)(2,1)S(1)} %get-tuple-element.26.refs_0_), channel_id=1, source_target_pairs={{1,0},{2,1},{3,2},{5,4},{6,5},{7,6},{9,8},{10,9},{11,10},{13,12},{... | collective-permute-start | bytes 1179656 | tf_op jit(solution)/shard_map/ppermute | solution.py:23
  156.2 16.5 %collective-permute-start.32 = (bf16[768,256]{1,0:T(8,128)(2,1)S(1)}, bf16[768,256]{1,0:T(8,128)(2,1)S(1)}, u32[]{:S(2)}, u32[]{:S(2)}) collective-permute-start(bf16[768,256]{1,0:T(8,128)(2,1)S(1)} %get-tuple-element.25.refs_7_), channel_id=1, source_target_pairs={{0,1},{1,2},{2,3},{4,5},{5,6},{6,7},{8,9},{9,10},{10,11},{12,13},{... | collective-permute-start | bytes 1179656 | tf_op jit(solution)/shard_map/ppermute | solution.py:22
  160.8 16.4 %collective-permute-start.35 = (bf16[768,256]{1,0:T(8,128)(2,1)S(1)}, bf16[768,256]{1,0:T(8,128)(2,1)S(1)}, u32[]{:S(2)}, u32[]{:S(2)}) collective-permute-start(bf16[768,256]{1,0:T(8,128)(2,1)S(1)} %get-tuple-element.25.refs_7_), channel_id=1, source_target_pairs={{1,0},{2,1},{3,2},{5,4},{6,5},{7,6},{9,8},{10,9},{11,10},{13,12},{... | collective-permute-start | bytes 1179656 | tf_op jit(solution)/shard_map/ppermute | solution.py:23
  162.1 1.6 collective-permute-start.38
  163.7 14.8 %collective-permute-start.40 = (bf16[256,512]{1,0:T(8,128)(2,1)}, bf16[256,512]{1,0:T(8,128)(2,1)S(1)}, u32[]{:S(2)}, u32[]{:S(2)}) collective-permute-start(bf16[256,512]{1,0:T(8,128)(2,1)} %collective-permute-done.39.refs_16_), channel_id=1, source_target_pairs={{0,4},{4,0},{8,12},{12,8},{16,20},{20,16},{24,28},{28,24},{1,5},{5... | collective-permute-start | bytes 786440 | tf_op jit(solution)/shard_map/ppermute | solution.py:34
  164.3 16.9 %collective-permute-start.27 = (bf16[768,256]{1,0:T(8,128)(2,1)S(1)}, bf16[768,256]{1,0:T(8,128)(2,1)S(1)}, u32[]{:S(2)}, u32[]{:S(2)}) collective-permute-start(bf16[768,256]{1,0:T(8,128)(2,1)S(1)} %collective-permute-done.26.refs_1_), channel_id=1, source_target_pairs={{0,1},{1,2},{2,3},{4,5},{5,6},{6,7},{8,9},{9,10},{10,11},{12,13},{... | collective-permute-start | bytes 1179656 | tf_op jit(solution)/shard_map/ppermute | solution.py:22
  168.8 16.9 %collective-permute-start.30 = (bf16[768,256]{1,0:T(8,128)(2,1)S(1)}, bf16[768,256]{1,0:T(8,128)(2,1)S(1)}, u32[]{:S(2)}, u32[]{:S(2)}) collective-permute-start(bf16[768,256]{1,0:T(8,128)(2,1)S(1)} %collective-permute-done.29.refs_4_), channel_id=1, source_target_pairs={{1,0},{2,1},{3,2},{5,4},{6,5},{7,6},{9,8},{10,9},{11,10},{13,12},{... | collective-permute-start | bytes 1179656 | tf_op jit(solution)/shard_map/ppermute | solution.py:23
  172.7 16.9 %collective-permute-start.33 = (bf16[768,256]{1,0:T(8,128)(2,1)S(1)}, bf16[768,256]{1,0:T(8,128)(2,1)S(1)}, u32[]{:S(2)}, u32[]{:S(2)}) collective-permute-start(bf16[768,256]{1,0:T(8,128)(2,1)S(1)} %collective-permute-done.32.refs_8_), channel_id=1, source_target_pairs={{0,1},{1,2},{2,3},{4,5},{5,6},{6,7},{8,9},{9,10},{10,11},{12,13},{... | collective-permute-start | bytes 1179656 | tf_op jit(solution)/shard_map/ppermute | solution.py:22
  177.2 16.9 %collective-permute-start.36 = (bf16[768,256]{1,0:T(8,128)(2,1)S(1)}, bf16[768,256]{1,0:T(8,128)(2,1)S(1)}, u32[]{:S(2)}, u32[]{:S(2)}) collective-permute-start(bf16[768,256]{1,0:T(8,128)(2,1)S(1)} %collective-permute-done.35.refs_11_), channel_id=1, source_target_pairs={{1,0},{2,1},{3,2},{5,4},{6,5},{7,6},{9,8},{10,9},{11,10},{13,12},{... | collective-permute-start | bytes 1179656 | tf_op jit(solution)/shard_map/ppermute | solution.py:23
  178.5 16.8 %collective-permute-start.42 = (bf16[256,512]{1,0:T(8,128)(2,1)}, bf16[256,512]{1,0:T(8,128)(2,1)S(1)}, u32[]{:S(2)}, u32[]{:S(2)}) collective-permute-start(bf16[256,512]{1,0:T(8,128)(2,1)} %collective-permute-done.41.refs_18_), channel_id=1, source_target_pairs={{0,4},{4,0},{8,12},{12,8},{16,20},{20,16},{24,28},{28,24},{1,5},{5... | collective-permute-start | bytes 786440 | tf_op jit(solution)/shard_map/ppermute | solution.py:34
  181.1 16.9 %collective-permute-start.28 = (bf16[768,256]{1,0:T(8,128)(2,1)S(1)}, bf16[768,256]{1,0:T(8,128)(2,1)S(1)}, u32[]{:S(2)}, u32[]{:S(2)}) collective-permute-start(bf16[768,256]{1,0:T(8,128)(2,1)S(1)} %collective-permute-done.27.refs_2_), channel_id=1, source_target_pairs={{0,1},{1,2},{2,3},{4,5},{5,6},{6,7},{8,9},{9,10},{10,11},{12,13},{... | collective-permute-start | bytes 1179656 | tf_op jit(solution)/shard_map/ppermute | solution.py:22
  185.7 16.9 %collective-permute-start.31 = (bf16[768,256]{1,0:T(8,128)(2,1)S(1)}, bf16[768,256]{1,0:T(8,128)(2,1)S(1)}, u32[]{:S(2)}, u32[]{:S(2)}) collective-permute-start(bf16[768,256]{1,0:T(8,128)(2,1)S(1)} %collective-permute-done.30.refs_5_), channel_id=1, source_target_pairs={{1,0},{2,1},{3,2},{5,4},{6,5},{7,6},{9,8},{10,9},{11,10},{13,12},{... | collective-permute-start | bytes 1179656 | tf_op jit(solution)/shard_map/ppermute | solution.py:23
  189.6 16.9 %collective-permute-start.34 = (bf16[768,256]{1,0:T(8,128)(2,1)S(1)}, bf16[768,256]{1,0:T(8,128)(2,1)S(1)}, u32[]{:S(2)}, u32[]{:S(2)}) collective-permute-start(bf16[768,256]{1,0:T(8,128)(2,1)S(1)} %collective-permute-done.33.refs_9_), channel_id=1, source_target_pairs={{0,1},{1,2},{2,3},{4,5},{5,6},{6,7},{8,9},{9,10},{10,11},{12,13},{... | collective-permute-start | bytes 1179656 | tf_op jit(solution)/shard_map/ppermute | solution.py:22
  194.1 16.8 %collective-permute-start.37 = (bf16[768,256]{1,0:T(8,128)(2,1)S(1)}, bf16[768,256]{1,0:T(8,128)(2,1)}, u32[]{:S(2)}, u32[]{:S(2)}) collective-permute-start(bf16[768,256]{1,0:T(8,128)(2,1)S(1)} %collective-permute-done.36.refs_12_), channel_id=1, source_target_pairs={{1,0},{2,1},{3,2},{5,4},{6,5},{7,6},{9,8},{10,9},{11,10},{13,12},{... | collective-permute-start | bytes 1179656 | tf_op jit(solution)/shard_map/ppermute | solution.py:23
  195.4 1.8 collective-permute-start.44
  (36 other events, 724.0 us)

commit v2 on v0

v2 whole, which is shorter than its diff:
```python
import functools

import jax
import jax.numpy as jnp
from jax import lax
from jax.experimental import pallas as pl
from jax.experimental.pallas import tpu as pltpu
from jax.sharding import PartitionSpec as P

HEAD_WIDTH = 128
BLK = 64
NEIGH = 9
MIB = 1024 * 1024
LOG2E = 1.4426950408889634
HBM = pl.BlockSpec(memory_space=pltpu.HBM)
SMEM = pl.BlockSpec(memory_space=pltpu.SMEM)
VMEM_LIMIT = 60 * MIB


def line_step(parts, axis, size):
    to_right = [(i, i + 1) for i in range(size - 1)]
    to_left = [(i + 1, i) for i in range(size - 1)]
    own, from_left, from_right = parts
    left = lax.ppermute((from_left or [own])[-1], axis, to_right)
    right = lax.ppermute((from_right or [own])[-1], axis, to_left)
    return own, from_left + [left], from_right + [right]


def swap(x, s, axis, size):
    return lax.ppermute(x, axis, [(i, i ^ s) for i in range(size)])


def tile_of(columns):
    return 256 if columns % 256 == 0 else 128


def accumulate_kernel(place, *refs, reach, hid_size, cut):
    chunks = len(reach)
    refs = list(refs)
    parts = []
    for c in range(chunks):
        own = refs.pop(0)
        from_left = [refs.pop(0) for _ in range(reach[c])]
        from_right = [refs.pop(0) for _ in range(reach[c])]
        parts.append((own, from_left, from_right))
    panel = refs.pop(0)
    total, last_rows, rows, weights, sums, row_sem, weight_sem, last_sem, sum_sem = refs
    at_hid = place[0]
    width = cut * chunks
    columns = total.shape[1]

    def each(act):
        for c, (own, from_left, from_right) in enumerate(parts):
            def copy(ref, source, k, c=c):
                at = pl.multiple_of(source * width + c * cut, cut)
                return pltpu.make_async_copy(ref, rows.at[:, pl.ds(at, cut)], row_sem.at[c, k])

            act(copy(own, at_hid, 0))
            for k in range(1, reach[c] + 1):
                @pl.when(at_hid >= k)
                def _():
                    act(copy(from_left[k - 1], at_hid - k, k))

                @pl.when(at_hid + k < hid_size)
                def _():
                    act(copy(from_right[k - 1], at_hid + k, hid_size - 1 + k))

    weight_copy = pltpu.make_async_copy(panel, weights, weight_sem)
    each(lambda d: d.start())
    weight_copy.start()
    for c in range(chunks):
        if reach[c] < hid_size - 1:
            for end, source in ((0, hid_size - 1), (hid_size - 1, 0)):
                @pl.when(at_hid == end)
                def _():
                    at = source * width + c * cut
                    rows[:, at : at + cut] = jnp.zeros((rows.shape[0], cut), rows.dtype)
    weight_copy.wait()
    source = jnp.where(at_hid == 0, hid_size - 1, 0)
    lasts = []
    for c in range(chunks):
        if reach[c] < hid_size - 1:
            at = pl.multiple_of(source * width + c * cut, cut)
            n = len(lasts)
            lasts.append(pltpu.make_async_copy(
                weights.at[pl.ds(at, cut), :], last_rows.at[pl.ds(n * cut, cut), :], last_sem.at[n]
            ))
    for copy in lasts:
        copy.start()
    each(lambda d: d.wait())
    step = tile_of(columns)
    for n in range(0, columns, step):
        sums[:, n : n + step] = jnp.dot(
            rows[...], weights[:, n : n + step], preferred_element_type=jnp.float32
        )
        lasts.append(pltpu.make_async_copy(
            sums.at[:, pl.ds(n, step)], total.at[:, pl.ds(n, step)], sum_sem.at[n // step]
        ))
        lasts[-1].start()
    for copy in lasts:
        copy.wait()


def accumulate(place, parts, panel, reach, hid_size):
    columns = panel.shape[1]
    chunks = len(parts)
    tok_rows, cut = parts[0][0].shape
    full = cut * chunks * hid_size
    flat = []
    for c, (own, from_left, from_right) in enumerate(parts):
        flat += [own, *from_left[: reach[c]], *from_right[: reach[c]]]
    deferred = sum(r < hid_size - 1 for r in reach)
    return pl.pallas_call(
        functools.partial(
            accumulate_kernel, reach=reach, hid_size=hid_size, cut=cut
        ),
        out_shape=[
            jax.ShapeDtypeStruct((tok_rows, columns), jnp.float32),
            jax.ShapeDtypeStruct((deferred * cut, columns), jnp.bfloat16),
        ],
        in_specs=[SMEM] + [HBM] * (len(flat) + 1),
        out_specs=[HBM, HBM],
        scratch_shapes=[
            pltpu.VMEM((tok_rows, full), jnp.bfloat16),
            pltpu.VMEM((full, columns), jnp.bfloat16),
            pltpu.VMEM((tok_rows, columns), jnp.float32),
            pltpu.SemaphoreType.DMA((chunks, 2 * hid_size - 1)),
            pltpu.SemaphoreType.DMA,
            pltpu.SemaphoreType.DMA((deferred,)),
            pltpu.SemaphoreType.DMA((columns // tile_of(columns),)),
        ],
        compiler_params=pltpu.CompilerParams(vmem_limit_bytes=VMEM_LIMIT),
        cost_estimate=pl.CostEstimate(
            flops=2 * tok_rows * full * columns, bytes_accessed=2 * full * (tok_rows + columns), transcendentals=0
        ),
    )(place, *flat, panel)


def finish_kernel(place, send_ids, *refs, deferred, hid_size, cut, begin, columns, n_sends):
    refs = list(refs)
    total = refs.pop(0)
    lasts = [(refs.pop(0), refs.pop(0)) for _ in range(deferred)]
    last_rows = refs.pop(0)
    n_outs = 2 + n_sends if n_sends else 1
    targets, outs, scratch = refs[:n_outs], refs[n_outs:-7], refs[-7:]
    sums, rows, weights, sum_sem, row_sem, weight_sem, out_sem = scratch
    at_hid = place[0]
    at_end = (at_hid == 0) | (at_hid == hid_size - 1)
    sum_copy = pltpu.make_async_copy(total.at[:, pl.ds(begin, columns)], sums, sum_sem)
    weight_copy = pltpu.make_async_copy(last_rows.at[:, pl.ds(begin, columns)], weights, weight_sem)
    sum_copy.start()

    def row_copies(side):
        return [
            pltpu.make_async_copy(lasts[c][side], rows.at[:, pl.ds(c * cut, cut)], row_sem.at[c])
            for c in range(deferred)
        ]

    for end, side in ((0, 1), (hid_size - 1, 0)):
        @pl.when(at_hid == end)
        def _():
            for copy in row_copies(side):
                copy.start()
            weight_copy.start()

    heads = columns // (3 * HEAD_WIDTH)

    def emit(n, value):
        if not n_sends:
            outs[0][:, n : n + value.shape[1]] = value
            return
        for g in range(n // HEAD_WIDTH, (n + value.shape[1]) // HEAD_WIDTH):
            piece = value[:, g * HEAD_WIDTH - n : (g + 1) * HEAD_WIDTH - n]
            head, kind = g // 3, g % 3
            target = outs[min(kind, 1)]
            at = ((kind == 2) * heads + head) * HEAD_WIDTH
            target[:, at : at + HEAD_WIDTH] = piece

    step = tile_of(columns)
    sum_copy.wait()

    @pl.when(at_end)
    def _():
        for copy in row_copies(0):
            copy.wait()
        weight_copy.wait()
        for n in range(0, columns, step):
            more = jnp.dot(rows[...], weights[:, n : n + step], preferred_element_type=jnp.float32)
            emit(n, (sums[:, n : n + step] + more).astype(jnp.bfloat16))

    @pl.when(jnp.logical_not(at_end))
    def _():
        for n in range(0, columns, step):
            emit(n, sums[:, n : n + step].astype(jnp.bfloat16))

    copies = []
    for s in range(n_sends):
        for slot in range(2):
            at = pl.multiple_of(send_ids[s + 1, slot] * BLK, BLK)
            copies.append(pltpu.make_async_copy(
                outs[1].at[pl.ds(at, BLK), :], targets[2 + s].at[pl.ds(slot * BLK, BLK), :],
                out_sem.at[2 + 2 * s + slot],
            ))
    for n, value in enumerate(outs):
        copies.append(pltpu.make_async_copy(value, targets[n], out_sem.at[n]))
    for copy in copies:
        copy.start()
    for copy in copies:
        copy.wait()


def finish(place, send_ids, total, lasts, last_rows, begin, columns, hid_size, n_sends):
    tok_rows = total.shape[0]
    deferred = len(lasts)
    cut = last_rows.shape[0] // deferred
    bf16 = lambda *shape: jax.ShapeDtypeStruct(shape, jnp.bfloat16)
    if n_sends:
        wide = columns // 3
        shapes = [bf16(tok_rows, wide), bf16(tok_rows, 2 * wide)] + [bf16(2 * BLK, 2 * wide)] * n_sends
    else:
        shapes = [bf16(tok_rows, columns)]
    flat = [x for pair in lasts for x in pair]
    return pl.pallas_call(
        functools.partial(
            finish_kernel, deferred=deferred, hid_size=hid_size, cut=cut, begin=begin, columns=columns,
            n_sends=n_sends,
        ),
        out_shape=shapes,
        in_specs=[SMEM] * 2 + [HBM] * (2 + len(flat)),
        out_specs=[HBM] * len(shapes),
        scratch_shapes=[pltpu.VMEM(x.shape, x.dtype) for x in shapes[:2]] + [
            pltpu.VMEM((tok_rows, columns), jnp.float32),
            pltpu.VMEM((tok_rows, deferred * cut), jnp.bfloat16),
            pltpu.VMEM((deferred * cut, columns), jnp.bfloat16),
            pltpu.SemaphoreType.DMA,
            pltpu.SemaphoreType.DMA((deferred,)),
            pltpu.SemaphoreType.DMA,
            pltpu.SemaphoreType.DMA((2 + 2 * n_sends,)),
        ],
        compiler_params=pltpu.CompilerParams(vmem_limit_bytes=VMEM_LIMIT),
        cost_estimate=pl.CostEstimate(
            flops=2 * tok_rows * deferred * cut * columns, bytes_accessed=8 * tok_rows * columns, transcendentals=0
        ),
    )(place, send_ids, total, *flat, last_rows)


def attend_kernel(lists, counts, query_all, key_values, *refs, tok_size, heads):
    remote = refs[: tok_size - 1]
    target, pool, queries, result, sem = refs[tok_size - 1 :]
    tok_rows = queries.shape[0]
    blocks = tok_rows // BLK
    wide = heads * HEAD_WIDTH
    copies = [
        pltpu.make_async_copy(key_values, pool.at[pl.ds(0, tok_rows), :], sem.at[tok_size - 1]),
        pltpu.make_async_copy(query_all, queries, sem.at[tok_size]),
    ]
    for s in range(tok_size - 1):
        copies.append(pltpu.make_async_copy(
            remote[s], pool.at[pl.ds(tok_rows + s * 2 * BLK, 2 * BLK), :], sem.at[s]
        ))
    for copy in copies:
        copy.start()
    for copy in copies:
        copy.wait()
    scale = HEAD_WIDTH ** (-0.5) * LOG2E
    diagonal = (
        lax.broadcasted_iota(jnp.int32, (heads * BLK, wide), 0) // BLK
        == lax.broadcasted_iota(jnp.int32, (heads * BLK, wide), 1) // HEAD_WIDTH
    )
    column = lax.broadcasted_iota(jnp.int32, (heads * BLK, NEIGH * BLK), 1)

    def block(b):
        at = pl.multiple_of(b * BLK, BLK)
        starts = [pl.multiple_of(lists[b, j] * BLK, BLK) for j in range(NEIGH)]
        query = jnp.concatenate([queries[pl.ds(at, BLK), :]] * heads, axis=0)
        query = jnp.where(diagonal, query, jnp.zeros_like(query))
        keys = jnp.concatenate([pool[pl.ds(i, BLK), :wide] for i in starts], axis=0)
        logits = lax.dot_general(query, keys, (((1,), (1,)), ((), ())), preferred_element_type=jnp.float32)
        logits = jnp.where(column < counts[b] * BLK, logits, -1e30)
        highest = jnp.max(logits, axis=1, keepdims=True)
        expon = jnp.exp2((logits - highest) * scale)
        total = jnp.sum(expon, axis=1, keepdims=True)
        values = jnp.concatenate([pool[pl.ds(i, BLK), wide:] for i in starts], axis=0)
        blended = jnp.dot(expon.astype(jnp.bfloat16), values, preferred_element_type=jnp.float32) / total
        for h in range(heads):
            own = slice(h * HEAD_WIDTH, (h + 1) * HEAD_WIDTH)
            result[pl.ds(at, BLK), own] = blended[h * BLK : (h + 1) * BLK, own].astype(result.dtype)

    unroll = next(u for u in (6, 4, 3, 2, 1) if blocks % u == 0)

    def body(i, carry):
        for u in range(unroll):
            block(i * unroll + u)
        return carry

    lax.fori_loop(0, blocks // unroll, body, 0)
    copy = pltpu.make_async_copy(result, target, sem.at[0])
    copy.start()
    copy.wait()


def attend(lists, counts, query, key_values, remote, tok_size):
    tok_rows, wide = query.shape
    heads = wide // HEAD_WIDTH
    return pl.pallas_call(
        functools.partial(attend_kernel, tok_size=tok_size, heads=heads),
        out_shape=jax.ShapeDtypeStruct((tok_rows, wide), jnp.bfloat16),
        in_specs=[SMEM] * 2 + [HBM] * (tok_size + 1),
        out_specs=HBM,
        scratch_shapes=[
            pltpu.VMEM((tok_rows + (tok_size - 1) * 2 * BLK, 2 * wide), jnp.bfloat16),
            pltpu.VMEM((tok_rows, wide), jnp.bfloat16),
            pltpu.VMEM((tok_rows, wide), jnp.bfloat16),
            pltpu.SemaphoreType.DMA((tok_size + 1,)),
        ],
        compiler_params=pltpu.CompilerParams(vmem_limit_bytes=VMEM_LIMIT),
        cost_estimate=pl.CostEstimate(
            flops=8 * tok_rows * NEIGH * BLK * wide,
            bytes_accessed=2 * tok_rows * wide * 10,
            transcendentals=tok_rows * NEIGH * BLK * heads,
        ),
    )(lists, counts, query, key_values, *remote)


def routes(neighbours, counts, at_tok, tok_size, blocks):
    lists = neighbours.reshape(tok_size, blocks * NEIGH)
    valid = (jnp.arange(NEIGH)[None, :] < counts[:, None]).reshape(tok_size, blocks * NEIGH)
    owner = lists // blocks
    peers = jnp.arange(tok_size) ^ at_tok
    named = valid & (owner == at_tok)
    low = jnp.min(jnp.where(named, lists, tok_size * blocks), axis=1)
    high = jnp.max(jnp.where(named, lists, -1), axis=1)
    base = at_tok * blocks
    sends = jnp.clip(jnp.stack([low, high], axis=1) - base, 0, blocks - 1)
    send_ids = sends[peers]
    mine = lax.dynamic_slice_in_dim(lists, at_tok, 1, 0)[0]
    mine_valid = lax.dynamic_slice_in_dim(valid, at_tok, 1, 0)[0]
    mine_owner = mine // blocks
    same = (mine_owner[:, None] == mine_owner[None, :]) & mine_valid[None, :]
    first = jnp.min(jnp.where(same, mine[None, :], tok_size * blocks), axis=1)
    slot = (mine != first).astype(jnp.int32)
    there = blocks + ((mine_owner ^ at_tok) - 1) * 2 + slot
    pool_at = jnp.where(mine_owner == at_tok, mine - base, there)
    pool_at = jnp.where(mine_valid, pool_at, 0).reshape(blocks, NEIGH)
    my_counts = lax.dynamic_slice_in_dim(counts, at_tok * blocks, blocks, 0)
    return send_ids.astype(jnp.int32), pool_at.astype(jnp.int32), my_counts


def shards(tokens, qkv_weight, out_weight, neighbours, counts, *, tok_size, hid_size):
    at_tok, at_hid = lax.axis_index("tok"), lax.axis_index("hid")
    blocks = tokens.shape[0] // BLK
    place = jnp.stack([at_hid, at_tok]).astype(jnp.int32)
    heads_here = qkv_weight.shape[1] // (3 * HEAD_WIDTH)
    group = 2 if heads_here % 2 == 0 else 1
    chunks = heads_here // group
    cut = group * HEAD_WIDTH
    far = hid_size - 1
    out_columns = out_weight.shape[1]

    qkv_panel = lax.all_gather(qkv_weight, "tok", axis=0, tiled=True)
    out_panel = lax.all_gather(out_weight, "tok", axis=0, tiled=True)
    parts = [(tokens[:, c * cut : (c + 1) * cut], [], []) for c in range(chunks)]
    parts = [line_step(p, "hid", hid_size) for p in parts]
    parts[-1], ids = lax.optimization_barrier(
        (parts[-1], routes(neighbours, counts, at_tok, tok_size, blocks))
    )
    send_ids, pool_at, my_counts = ids
    for _ in range(far - 1):
        parts = [line_step(p, "hid", hid_size) for p in parts]

    total, last_rows = accumulate(place, parts, qkv_panel, [far - 1] * chunks, hid_size)
    lasts = [(from_left[-1], from_right[-1]) for _, from_left, from_right in parts]
    parts, remote = [], []
    for c in range(chunks):
        columns = 3 * cut
        query, key_values, *sends = finish(
            place, send_ids, total, lasts, last_rows, c * columns, columns, hid_size, tok_size - 1
        )
        sends, remote = lax.optimization_barrier((sends, remote))
        remote = [swap(sends[s - 1], s, "tok", tok_size) for s in range(1, tok_size)]
        if parts:
            remote, _ = lax.optimization_barrier((remote, parts[-1][0]))
        mixed = attend(pool_at, my_counts, query, key_values, remote, tok_size)
        part = (mixed, [], [])
        for _ in range(far):
            part = line_step(part, "hid", hid_size)
        parts.append(part)
    total, last_rows = accumulate(place, parts, out_panel, [far - 1] * chunks, hid_size)
    lasts = [(from_left[-1], from_right[-1]) for _, from_left, from_right in parts]
    (result,) = finish(place, send_ids, total, lasts, last_rows, 0, out_columns, hid_size, 0)
    return result


def solution(mesh):
    placed = (P("tok", "hid"), P("tok", "hid"), P("tok", "hid"), P(), P())
    return jax.shard_map(
        functools.partial(shards, tok_size=mesh.shape["tok"], hid_size=mesh.shape["hid"]),
        mesh=mesh, in_specs=placed, out_specs=P("tok", "hid"), check_vma=False,
    )
```

time: 407 us -> 188 us (0.46)
  waiting for transfers between devices: 248 us -> 36 us
  local copies, waits for them, and re-layouts: 90.2 us -> 5.97 us
  starting transfers between devices: 0.16 us -> 82.5 us
  Pallas kernels: 0 us -> 46.1 us
  matrix products: 36.5 us -> 0 us
  other arithmetic: 18.2 us -> 2.35 us
    all_gather x5 -> x2, waiting for transfers between devices: 246 us -> 0.04 us  [the longest x1 0.02 us: shards(): out_panel = lax.all_gather(out_weight, 'tok', axis=0, tiled=True)]
    ppermute x0 -> x38, starting transfers between devices: none -> 82.4 us  [the longest x12 55.2 us: line_step(): left = lax.ppermute((from_left or [own])[-1], axis, to_right)]
    pallas_call x0 -> x7, Pallas kernels: none -> 46.1 us  [the longest x2 16.7 us: accumulate(): pl.pallas_call(functools.partial(accumulate_kernel, reach=reach, hid_size...]
    ppermute x0 -> x38, waiting for transfers between devices: none -> 35.2 us  [the longest x12 16 us: line_step(): left = lax.ppermute((from_left or [own])[-1], axis, to_right)]
    slice x3 -> x1, local copies, waits for them, and re-layouts: 33.8 us -> 1.17 us  [shards(): parts = [(tokens[:, c * cut:(c + 1) * cut], [], []) for c in range(chunks)]]
    reshape x3 -> x1, local copies, waits for them, and re-layouts: 32.2 us -> 0.07 us  [routes(): lists = neighbours.reshape(tok_size, blocks * NEIGH)]
    dot_general x3 -> x0, matrix products: 26.5 us -> none  [the longest x1 12.1 us: shards(): jnp.einsum('bhqjk,bjkhd->bqhd', attention_probs, gathered[..., 1, :], pre...]
    gather x1, local copies, waits for them, and re-layouts: 12.1 us -> 1.13 us  [routes(): send_ids = sends[peers]]
  transfers between devices with their start and end apart: 5 -> 40, of which waited for: 4 -> 17; matrix products, arithmetic and copies ran while one was open for 29% -> 4% of each run, Pallas kernels for 0% -> 22%
where the time goes in v2:
time: 188 us; the launch traced here: 187 us
  starting transfers between devices  82.5 us (44%)
  Pallas kernels  46.1 us (25%)
  waiting for transfers between devices  36 us (19%)
  between operations  14.2 us (8%)
  local copies, waits for them, and re-layouts  5.97 us (3%)
  other arithmetic  2.35 us (1%)
    ppermute x12, starting transfers between devices, line_step(): left = lax.ppermute((from_left or [own])[-1], axis, to_right)  55.2 us
    pallas_call x2, Pallas kernels, accumulate(): pl.pallas_call(functools.partial(accumulate_kernel, reach=reach, hid_size...  16.7 us
    ppermute x12, waiting for transfers between devices, line_step(): left = lax.ppermute((from_left or [own])[-1], axis, to_right)  16 us
    ppermute x12, starting transfers between devices, line_step(): right = lax.ppermute((from_right or [own])[-1], axis, to_left)  15.4 us
    pallas_call x2, Pallas kernels, attend(): pl.pallas_call(functools.partial(attend_kernel, tok_size=tok_size, heads=...  15 us
    pallas_call x3, Pallas kernels, finish(): pl.pallas_call(functools.partial(finish_kernel, deferred=deferred, hid_si...  14.5 us
    ppermute x14, starting transfers between devices, swap(): return lax.ppermute(x, axis, [(i, i ^ s) for i in range(size)])  11.8 us
    ppermute x12, waiting for transfers between devices, line_step(): right = lax.ppermute((from_right or [own])[-1], axis, to_left)  10.2 us
  transfers between devices with their start and end apart: 40, of which 17 were waited for; matrix products, arithmetic and copies ran while one was open for 4% of the time, Pallas kernels for 22%

profile of v2, /device:TPU:0, one launch (start us, length us, event | category | flops | bytes accessed | tf_op | source)
XLA Modules:
  0.0 187.1 jit_solution(5389263221962046846)
XLA Ops:
  8.5 5.0 %collective-permute-start = (bf16[768,256]{1,0:T(8,128)(2,1)S(1)}, bf16[768,256]{1,0:T(8,128)(2,1)S(1)}, u32[]{:S(2)}, u32[]{:S(2)}) collective-permute-start(bf16[768,256]{1,0:T(8,128)(2,1)S(1)} %get-tuple-element.57.refs_5_), channel_id=1, source_target_pairs={{0,1},{1,2},{2,3},{4,5},{5,6},{6,7},{8,9},{9,10},{10,11},{12,13},{... | collective-permute-start | bytes 1179656 | tf_op jit(solution)/shard_map/ppermute | solution.py:24
  13.5 1.3 collective-permute-start.1
  14.8 4.6 %collective-permute-start.2 = (bf16[768,256]{1,0:T(8,128)(2,1)S(1)}, bf16[768,256]{1,0:T(8,128)(2,1)S(1)}, u32[]{:S(2)}, u32[]{:S(2)}) collective-permute-start(bf16[768,256]{1,0:T(8,128)(2,1)S(1)} %get-tuple-element.107.refs_0_), channel_id=1, source_target_pairs={{0,1},{1,2},{2,3},{4,5},{5,6},{6,7},{8,9},{9,10},{10,11},{12,13},{... | collective-permute-start | bytes 1179656 | tf_op jit(solution)/shard_map/ppermute | solution.py:24
  19.3 1.3 collective-permute-start.4
  25.7 1.7 collective-permute-done.1.refs_8_
  27.4 2.8 %collective-permute-done.2.refs_1_ = bf16[768,256]{1,0:T(8,128)(2,1)S(1)} collective-permute-done((bf16[768,256]{1,0:T(8,128)(2,1)S(1)}, bf16[768,256]{1,0:T(8,128)(2,1)S(1)}, u32[]{:S(2)}, u32[]{:S(2)}) %collective-permute-start.2) | collective-permute-done | bytes 393248 | tf_op jit(solution)/shard_map/ppermute | solution.py:24
  30.2 5.1 %collective-permute-start.3 = (bf16[768,256]{1,0:T(8,128)(2,1)S(1)}, bf16[768,256]{1,0:T(8,128)(2,1)}, u32[]{:S(2)}, u32[]{:S(2)}) collective-permute-start(bf16[768,256]{1,0:T(8,128)(2,1)S(1)} %collective-permute-done.2.refs_1_), channel_id=1, source_target_pairs={{0,1},{1,2},{2,3},{4,5},{5,6},{6,7},{8,9},{9,10},{10,11},{12,13},{... | collective-permute-start | bytes 1179656 | tf_op jit(solution)/shard_map/ppermute | solution.py:24
  35.4 1.3 collective-permute-start.5
  36.6 5.3 %collective-permute-start.6 = (bf16[768,256]{1,0:T(8,128)(2,1)S(1)}, bf16[768,256]{1,0:T(8,128)(2,1)}, u32[]{:S(2)}, u32[]{:S(2)}) collective-permute-start(bf16[768,256]{1,0:T(8,128)(2,1)S(1)} %collective-permute-done.refs_6_), channel_id=1, source_target_pairs={{0,1},{1,2},{2,3},{4,5},{5,6},{6,7},{8,9},{9,10},{10,11},{12,13},{... | collective-permute-start | bytes 1179656 | tf_op jit(solution)/shard_map/ppermute | solution.py:24
  42.0 1.3 collective-permute-start.7
  44.2 4.5 %collective-permute-start.8 = (bf16[768,256]{1,0:T(8,128)(2,1)}, bf16[768,256]{1,0:T(8,128)(2,1)S(1)}, u32[]{:S(2)}, u32[]{:S(2)}) collective-permute-start(bf16[768,256]{1,0:T(8,128)(2,1)} %collective-permute-done.3.refs_2_), channel_id=1, source_target_pairs={{0,1},{1,2},{2,3},{4,5},{5,6},{6,7},{8,9},{9,10},{10,11},{12,13},{... | collective-permute-start | bytes 1179656 | tf_op jit(solution)/shard_map/ppermute | solution.py:24
  49.4 1.3 collective-permute-start.9
  50.7 1.9 %collective-permute-done.6.refs_7_ = bf16[768,256]{1,0:T(8,128)(2,1)} collective-permute-done((bf16[768,256]{1,0:T(8,128)(2,1)S(1)}, bf16[768,256]{1,0:T(8,128)(2,1)}, u32[]{:S(2)}, u32[]{:S(2)}) %collective-permute-start.6) | collective-permute-done | bytes 393248 | tf_op jit(solution)/shard_map/ppermute | solution.py:24
  52.6 4.5 %collective-permute-start.10 = (bf16[768,256]{1,0:T(8,128)(2,1)}, bf16[768,256]{1,0:T(8,128)(2,1)S(1)}, u32[]{:S(2)}, u32[]{:S(2)}) collective-permute-start(bf16[768,256]{1,0:T(8,128)(2,1)} %collective-permute-done.6.refs_7_), channel_id=1, source_target_pairs={{0,1},{1,2},{2,3},{4,5},{5,6},{6,7},{8,9},{9,10},{10,11},{12,13},{... | collective-permute-start | bytes 1179656 | tf_op jit(solution)/shard_map/ppermute | solution.py:24
  57.8 1.3 collective-permute-start.11
  59.2 10.6 %shard_map.55 = (f32[768,1536]{1,0:T(8,128)}, bf16[512,1536]{1,0:T(8,128)(2,1)}) custom-call(s32[2]{0:T(128)} %pad_add_fusion.1.place, bf16[768,256]{1,0:T(8,128)(2,1)} %copy-done.12, bf16[768,256]{1,0:T(8,128)(2,1)} %copy-done.19, bf16[768,256]{1,0:T(8,128)(2,1)} %collective-permute-done.3.refs_2_, bf16[768,256]{1,0:T(8,128)(2,1)} %copy-done.20, ...), custom_call_target="tpu_custom_call" | custom-call | flops 4831838208 | bytes 9437184 | tf_op jit(solution)/shard_map/pallas_call | solution.py:113
  69.9 2.4 %collective-permute-done.11.refs_4_ = bf16[768,256]{1,0:T(8,128)(2,1)S(1)} collective-permute-done((bf16[768,256]{1,0:T(8,128)(2,1)}, bf16[768,256]{1,0:T(8,128)(2,1)S(1)}, u32[]{:S(2)}, u32[]{:S(2)}) %collective-permute-start.11) | collective-permute-done | bytes 393248 | tf_op jit(solution)/shard_map/ppermute | solution.py:25
  73.1 5.2 %shard_map.56 = (bf16[768,256]{1,0:T(8,128)(2,1)}, bf16[768,512]{1,0:T(8,128)(2,1)}, bf16[128,512]{1,0:T(8,128)(2,1)}, bf16[128,512]{1,0:T(8,128)(2,1)}, bf16[12...) custom-call(s32[2]{0:T(128)} %pad_add_fusion.1.place, ...), custom_call_target="tpu_custom_call" | custom-call | flops 603979776 | bytes 4718592 | tf_op jit(solution)/shard_map/pallas_call | solution.py:223
  78.3 1.6 collective-permute-start.13
  80.2 1.5 collective-permute-start.15
  81.9 2.4 %collective-permute-start.17 = (bf16[128,512]{1,0:T(8,128)(2,1)}, bf16[128,512]{1,0:T(8,128)(2,1)S(1)}, u32[]{:S(2)}, u32[]{:S(2)}) collective-permute-start(bf16[128,512]{1,0:T(8,128)(2,1)} %get-tuple-element.76), channel_id=1, source_target_pairs={{0,24},{4,28},{8,16},{12,20},{16,8},{20,12},{24,0},{28,4},{1,25},{... | collective-permute-start | bytes 393224 | tf_op jit(solution)/shard_map/ppermute | solution.py:30
  84.3 3.4 %collective-permute-done.13.refs_1_ = bf16[128,512]{1,0:T(8,128)(2,1)S(1)} collective-permute-done((bf16[128,512]{1,0:T(8,128)(2,1)}, bf16[128,512]{1,0:T(8,128)(2,1)S(1)}, u32[]{:S(2)}, u32[]{:S(2)}) %collective-permute-start.13) | collective-permute-done | bytes 131104 | tf_op jit(solution)/shard_map/ppermute | solution.py:30
  87.7 1.6 collective-permute-start.18
  89.3 5.2 %shard_map.58 = (bf16[768,256]{1,0:T(8,128)(2,1)}, bf16[768,512]{1,0:T(8,128)(2,1)}, bf16[128,512]{1,0:T(8,128)(2,1)}, bf16[128,512]{1,0:T(8,128)(2,1)}, bf16[12...) custom-call(s32[2]{0:T(128)} %pad_add_fusion.1.place, ...), custom_call_target="tpu_custom_call" | custom-call | flops 603979776 | bytes 4718592 | tf_op jit(solution)/shard_map/pallas_call | solution.py:223
  95.3 2.4 %collective-permute-done.18.refs_6_ = bf16[128,512]{1,0:T(8,128)(2,1)S(1)} collective-permute-done((bf16[128,512]{1,0:T(8,128)(2,1)}, bf16[128,512]{1,0:T(8,128)(2,1)S(1)}, u32[]{:S(2)}, u32[]{:S(2)}) %collective-permute-start.18) | collective-permute-done | bytes 131104 | tf_op jit(solution)/shard_map/ppermute | solution.py:30
  100.1 1.3 collective-permute-start.27
  101.8 2.5 %collective-permute-done.24.refs_1_ = bf16[128,512]{1,0:T(8,128)(2,1)S(1)} collective-permute-done((bf16[128,512]{1,0:T(8,128)(2,1)}, bf16[128,512]{1,0:T(8,128)(2,1)S(1)}, u32[]{:S(2)}, u32[]{:S(2)}) %collective-permute-start.24) | collective-permute-done | bytes 131104 | tf_op jit(solution)/shard_map/ppermute | solution.py:30
  104.4 7.5 %shard_map.57.refs_0_ = bf16[768,256]{1,0:T(8,128)(2,1)} custom-call(s32[12,9]{1,0:T(8,128)} %select_select_fusion.lists, s32[12]{0:T(128)} %dynamic_slice.11.counts, bf16[768,256]{1,0:T(8,128)(2,1)} %get-tuple-element.62.query_all, bf16[768,512]{1,0:T(8,128)(2,1)} %get-tuple-element.63.key_values, bf16[128,512]{1,0:T(8,128)(2,1)} %copy-done.21, ...), custom_call_target="tpu_custom_call" | custom-call | flops 905969664 | bytes 3932160 | tf_op jit(solution)/shard_map/pallas_call | solution.py:305
  111.9 3.3 %collective-permute-start.19 = (bf16[768,256]{1,0:T(8,128)(2,1)}, bf16[768,256]{1,0:T(8,128)(2,1)S(1)}, u32[]{:S(2)}, u32[]{:S(2)}) collective-permute-start(bf16[768,256]{1,0:T(8,128)(2,1)} %shard_map.57.refs_0_), channel_id=1, source_target_pairs={{0,1},{1,2},{2,3},{4,5},{5,6},{6,7},{8,9},{9,10},{10,11},{12,13},{... | collective-permute-start | bytes 1179656 | tf_op jit(solution)/shard_map/ppermute | solution.py:24
  115.2 1.3 collective-permute-start.21
  117.3 7.5 %shard_map.59.refs_5_ = bf16[768,256]{1,0:T(8,128)(2,1)} custom-call(s32[12,9]{1,0:T(8,128)} %select_select_fusion.lists, s32[12]{0:T(128)} %dynamic_slice.11.counts, bf16[768,256]{1,0:T(8,128)(2,1)} %get-tuple-element.78.query_all, bf16[768,512]{1,0:T(8,128)(2,1)} %get-tuple-element.79.key_values, bf16[128,512]{1,0:T(8,128)(2,1)} %copy-done.28, ...), custom_call_target="tpu_custom_call" | custom-call | flops 905969664 | bytes 3932160 | tf_op jit(solution)/shard_map/pallas_call | solution.py:305
  124.8 4.6 %collective-permute-start.30 = (bf16[768,256]{1,0:T(8,128)(2,1)}, bf16[768,256]{1,0:T(8,128)(2,1)S(1)}, u32[]{:S(2)}, u32[]{:S(2)}) collective-permute-start(bf16[768,256]{1,0:T(8,128)(2,1)} %shard_map.59.refs_5_), channel_id=1, source_target_pairs={{0,1},{1,2},{2,3},{4,5},{5,6},{6,7},{8,9},{9,10},{10,11},{12,13},{... | collective-permute-start | bytes 1179656 | tf_op jit(solution)/shard_map/ppermute | solution.py:24
  129.3 1.3 collective-permute-start.32
  130.7 4.6 %collective-permute-start.20 = (bf16[768,256]{1,0:T(8,128)(2,1)S(1)}, bf16[768,256]{1,0:T(8,128)(2,1)S(1)}, u32[]{:S(2)}, u32[]{:S(2)}) collective-permute-start(bf16[768,256]{1,0:T(8,128)(2,1)S(1)} %collective-permute-done.19.refs_1_), channel_id=1, source_target_pairs={{0,1},{1,2},{2,3},{4,5},{5,6},{6,7},{8,9},{9,10},{10,11},{12,13},{... | collective-permute-start | bytes 1179656 | tf_op jit(solution)/shard_map/ppermute | solution.py:24
  135.3 1.3 collective-permute-start.22
  136.6 2.5 %collective-permute-done.30.refs_6_ = bf16[768,256]{1,0:T(8,128)(2,1)S(1)} collective-permute-done((bf16[768,256]{1,0:T(8,128)(2,1)}, bf16[768,256]{1,0:T(8,128)(2,1)S(1)}, u32[]{:S(2)}, u32[]{:S(2)}) %collective-permute-start.30) | collective-permute-done | bytes 393248 | tf_op jit(solution)/shard_map/ppermute | solution.py:24
  139.1 4.3 %collective-permute-start.31 = (bf16[768,256]{1,0:T(8,128)(2,1)S(1)}, bf16[768,256]{1,0:T(8,128)(2,1)S(1)}, u32[]{:S(2)}, u32[]{:S(2)}) collective-permute-start(bf16[768,256]{1,0:T(8,128)(2,1)S(1)} %collective-permute-done.30.refs_6_), channel_id=1, source_target_pairs={{0,1},{1,2},{2,3},{4,5},{5,6},{6,7},{8,9},{9,10},{10,11},{12,13},{... | collective-permute-start | bytes 1179656 | tf_op jit(solution)/shard_map/ppermute | solution.py:24
  143.4 1.3 collective-permute-start.33
  144.7 2.7 %collective-permute-done.20.refs_2_ = bf16[768,256]{1,0:T(8,128)(2,1)S(1)} collective-permute-done((bf16[768,256]{1,0:T(8,128)(2,1)S(1)}, bf16[768,256]{1,0:T(8,128)(2,1)S(1)}, u32[]{:S(2)}, u32[]{:S(2)}) %collective-permute-start.20) | collective-permute-done | bytes 393248 | tf_op jit(solution)/shard_map/ppermute | solution.py:24
  147.4 4.4 %collective-permute-start.34 = (bf16[768,256]{1,0:T(8,128)(2,1)S(1)}, bf16[768,256]{1,0:T(8,128)(2,1)S(1)}, u32[]{:S(2)}, u32[]{:S(2)}) collective-permute-start(bf16[768,256]{1,0:T(8,128)(2,1)S(1)} %collective-permute-done.20.refs_2_), channel_id=1, source_target_pairs={{0,1},{1,2},{2,3},{4,5},{5,6},{6,7},{8,9},{9,10},{10,11},{12,13},{... | collective-permute-start | bytes 1179656 | tf_op jit(solution)/shard_map/ppermute | solution.py:24
  151.9 1.3 collective-permute-start.35
  153.2 2.7 %collective-permute-done.31.refs_7_ = bf16[768,256]{1,0:T(8,128)(2,1)S(1)} collective-permute-done((bf16[768,256]{1,0:T(8,128)(2,1)S(1)}, bf16[768,256]{1,0:T(8,128)(2,1)S(1)}, u32[]{:S(2)}, u32[]{:S(2)}) %collective-permute-start.31) | collective-permute-done | bytes 393248 | tf_op jit(solution)/shard_map/ppermute | solution.py:24
  155.8 5.1 %collective-permute-start.36 = (bf16[768,256]{1,0:T(8,128)(2,1)S(1)}, bf16[768,256]{1,0:T(8,128)(2,1)}, u32[]{:S(2)}, u32[]{:S(2)}) collective-permute-start(bf16[768,256]{1,0:T(8,128)(2,1)S(1)} %collective-permute-done.31.refs_7_), channel_id=1, source_target_pairs={{0,1},{1,2},{2,3},{4,5},{5,6},{6,7},{8,9},{9,10},{10,11},{12,13},{... | collective-permute-start | bytes 1179656 | tf_op jit(solution)/shard_map/ppermute | solution.py:24
  161.0 1.3 collective-permute-start.37
  162.4 6.1 %shard_map.60 = (f32[768,512]{1,0:T(8,128)}, bf16[512,512]{1,0:T(8,128)(2,1)}) custom-call(s32[2]{0:T(128)} %pad_add_fusion.1.place, bf16[768,256]{1,0:T(8,128)(2,1)} %shard_map.57.refs_0_, bf16[768,256]{1,0:T(8,128)(2,1)} %copy-done.4, bf16[768,256]{1,0:T(8,128)(2,1)} %copy-done.8, bf16[768,256]{1,0:T(8,128)(2,1)} %copy-done.5, bf16[768,256]{1,0:T(8,128)(2,1)} %copy-done.9, ...), custom_call_target="tpu_custom_call" | custom-call | flops 1610612736 | bytes 5242880 | tf_op jit(solution)/shard_map/pallas_call | solution.py:113
  168.8 3.2 %collective-permute-done.36.refs_3_ = bf16[768,256]{1,0:T(8,128)(2,1)} collective-permute-done((bf16[768,256]{1,0:T(8,128)(2,1)S(1)}, bf16[768,256]{1,0:T(8,128)(2,1)}, u32[]{:S(2)}, u32[]{:S(2)}) %collective-permute-start.36) | collective-permute-done | bytes 393248 | tf_op jit(solution)/shard_map/ppermute | solution.py:24
  172.0 4.2 %collective-permute-done.37.refs_4_ = bf16[768,256]{1,0:T(8,128)(2,1)} collective-permute-done((bf16[768,256]{1,0:T(8,128)(2,1)S(1)}, bf16[768,256]{1,0:T(8,128)(2,1)}, u32[]{:S(2)}, u32[]{:S(2)}) %collective-permute-start.37) | collective-permute-done | bytes 393248 | tf_op jit(solution)/shard_map/ppermute | solution.py:25
  176.2 4.1 %shard_map.61 = bf16[768,512]{1,0:T(8,128)(2,1)} custom-call(s32[2]{0:T(128)} %pad_add_fusion.1.place, s32[8,2]{1,0:T(8,128)} %gather_fusion, f32[768,512]{1,0:T(8,128)} %get-tuple-element.101.refs_0_, bf16[768,256]{1,0:T(8,128)(2,1)} %copy-done.14, bf16[768,256]{1,0:T(8,128)(2,1)} %collective-permute-done.35.refs_2_, ...), custom_call_target="tpu_custom_call" | custom-call | flops 402653184 | bytes 3145728 | tf_op jit(solution)/shard_map/pallas_call | solution.py:223
  (142 shorter events, 15.4 us)
Async XLA Ops:
  6.5 52.6 %all-gather.3.cloned.1.call-start = ((), (), s32[]{:S(2)}) async-start(), calls=%async_computation | async-start | bytes 7077888 | tf_op jit(solution)/shard_map/all_gather | solution.py:360
  7.3 155.0 %all-gather.5.cloned.1.call-start = ((), (), s32[]{:S(2)}) async-start(), calls=%async_computation.1 | async-start | bytes 2359296 | tf_op jit(solution)/shard_map/all_gather | solution.py:361
  8.5 50.7 %copy-start.12 = (bf16[768,256]{1,0:T(8,128)(2,1)}, bf16[768,256]{1,0:T(8,128)(2,1)S(1)}, u32[]{:S(2)}) copy-start(bf16[768,256]{1,0:T(8,128)(2,1)S(1)} %get-tuple-element.107.refs_0_) | copy-start | bytes 1179652
  8.5 50.7 %copy-start.13 = (bf16[768,256]{1,0:T(8,128)(2,1)}, bf16[768,256]{1,0:T(8,128)(2,1)S(1)}, u32[]{:S(2)}) copy-start(bf16[768,256]{1,0:T(8,128)(2,1)S(1)} %get-tuple-element.57.refs_5_) | copy-start | bytes 1179652
  8.5 17.2 %collective-permute-start = (bf16[768,256]{1,0:T(8,128)(2,1)S(1)}, bf16[768,256]{1,0:T(8,128)(2,1)S(1)}, u32[]{:S(2)}, u32[]{:S(2)}) collective-permute-start(bf16[768,256]{1,0:T(8,128)(2,1)S(1)} %get-tuple-element.57.refs_5_), channel_id=1, source_target_pairs={{0,1},{1,2},{2,3},{4,5},{5,6},{6,7},{8,9},{9,10},{10,11},{12,13},{... | collective-permute-start | bytes 1179656 | tf_op jit(solution)/shard_map/ppermute | solution.py:24
  13.5 13.9 %collective-permute-start.1 = (bf16[768,256]{1,0:T(8,128)(2,1)S(1)}, bf16[768,256]{1,0:T(8,128)(2,1)S(1)}, u32[]{:S(2)}, u32[]{:S(2)}) collective-permute-start(bf16[768,256]{1,0:T(8,128)(2,1)S(1)} %get-tuple-element.57.refs_5_), channel_id=1, source_target_pairs={{1,0},{2,1},{3,2},{5,4},{6,5},{7,6},{9,8},{10,9},{11,10},{13,12},{... | collective-permute-start | bytes 1179656 | tf_op jit(solution)/shard_map/ppermute | solution.py:25
  14.8 15.5 %collective-permute-start.2 = (bf16[768,256]{1,0:T(8,128)(2,1)S(1)}, bf16[768,256]{1,0:T(8,128)(2,1)S(1)}, u32[]{:S(2)}, u32[]{:S(2)}) collective-permute-start(bf16[768,256]{1,0:T(8,128)(2,1)S(1)} %get-tuple-element.107.refs_0_), channel_id=1, source_target_pairs={{0,1},{1,2},{2,3},{4,5},{5,6},{6,7},{8,9},{9,10},{10,11},{12,13},{... | collective-permute-start | bytes 1179656 | tf_op jit(solution)/shard_map/ppermute | solution.py:24
  19.3 16.0 %collective-permute-start.4 = (bf16[768,256]{1,0:T(8,128)(2,1)S(1)}, bf16[768,256]{1,0:T(8,128)(2,1)S(1)}, u32[]{:S(2)}, u32[]{:S(2)}) collective-permute-start(bf16[768,256]{1,0:T(8,128)(2,1)S(1)} %get-tuple-element.107.refs_0_), channel_id=1, source_target_pairs={{1,0},{2,1},{3,2},{5,4},{6,5},{7,6},{9,8},{10,9},{11,10},{13,12},{... | collective-permute-start | bytes 1179656 | tf_op jit(solution)/shard_map/ppermute | solution.py:25
  25.7 33.4 %copy-start.17 = (bf16[768,256]{1,0:T(8,128)(2,1)}, bf16[768,256]{1,0:T(8,128)(2,1)S(1)}, u32[]{:S(2)}) copy-start(bf16[768,256]{1,0:T(8,128)(2,1)S(1)} %collective-permute-done.refs_6_) | copy-start | bytes 1179652
  27.4 31.8 %copy-start.18 = (bf16[768,256]{1,0:T(8,128)(2,1)}, bf16[768,256]{1,0:T(8,128)(2,1)S(1)}, u32[]{:S(2)}) copy-start(bf16[768,256]{1,0:T(8,128)(2,1)S(1)} %collective-permute-done.1.refs_8_) | copy-start | bytes 1179652
  30.2 29.0 %copy-start.19 = (bf16[768,256]{1,0:T(8,128)(2,1)}, bf16[768,256]{1,0:T(8,128)(2,1)S(1)}, u32[]{:S(2)}) copy-start(bf16[768,256]{1,0:T(8,128)(2,1)S(1)} %collective-permute-done.2.refs_1_) | copy-start | bytes 1179652
  30.2 13.9 %collective-permute-start.3 = (bf16[768,256]{1,0:T(8,128)(2,1)S(1)}, bf16[768,256]{1,0:T(8,128)(2,1)}, u32[]{:S(2)}, u32[]{:S(2)}) collective-permute-start(bf16[768,256]{1,0:T(8,128)(2,1)S(1)} %collective-permute-done.2.refs_1_), channel_id=1, source_target_pairs={{0,1},{1,2},{2,3},{4,5},{5,6},{6,7},{8,9},{9,10},{10,11},{12,13},{... | collective-permute-start | bytes 1179656 | tf_op jit(solution)/shard_map/ppermute | solution.py:24
  35.4 14.0 %collective-permute-start.5 = (bf16[768,256]{1,0:T(8,128)(2,1)S(1)}, bf16[768,256]{1,0:T(8,128)(2,1)}, u32[]{:S(2)}, u32[]{:S(2)}) collective-permute-start(bf16[768,256]{1,0:T(8,128)(2,1)S(1)} %collective-permute-done.4.refs_3_), channel_id=1, source_target_pairs={{1,0},{2,1},{3,2},{5,4},{6,5},{7,6},{9,8},{10,9},{11,10},{13,12},{... | collective-permute-start | bytes 1179656 | tf_op jit(solution)/shard_map/ppermute | solution.py:25
  36.6 15.9 %collective-permute-start.6 = (bf16[768,256]{1,0:T(8,128)(2,1)S(1)}, bf16[768,256]{1,0:T(8,128)(2,1)}, u32[]{:S(2)}, u32[]{:S(2)}) collective-permute-start(bf16[768,256]{1,0:T(8,128)(2,1)S(1)} %collective-permute-done.refs_6_), channel_id=1, source_target_pairs={{0,1},{1,2},{2,3},{4,5},{5,6},{6,7},{8,9},{9,10},{10,11},{12,13},{... | collective-permute-start | bytes 1179656 | tf_op jit(solution)/shard_map/ppermute | solution.py:24
  42.0 15.9 %collective-permute-start.7 = (bf16[768,256]{1,0:T(8,128)(2,1)S(1)}, bf16[768,256]{1,0:T(8,128)(2,1)}, u32[]{:S(2)}, u32[]{:S(2)}) collective-permute-start(bf16[768,256]{1,0:T(8,128)(2,1)S(1)} %collective-permute-done.1.refs_8_), channel_id=1, source_target_pairs={{1,0},{2,1},{3,2},{5,4},{6,5},{7,6},{9,8},{10,9},{11,10},{13,12},{... | collective-permute-start | bytes 1179656 | tf_op jit(solution)/shard_map/ppermute | solution.py:25
  44.2 25.7 %collective-permute-start.8 = (bf16[768,256]{1,0:T(8,128)(2,1)}, bf16[768,256]{1,0:T(8,128)(2,1)S(1)}, u32[]{:S(2)}, u32[]{:S(2)}) collective-permute-start(bf16[768,256]{1,0:T(8,128)(2,1)} %collective-permute-done.3.refs_2_), channel_id=1, source_target_pairs={{0,1},{1,2},{2,3},{4,5},{5,6},{6,7},{8,9},{9,10},{10,11},{12,13},{... | collective-permute-start | bytes 1179656 | tf_op jit(solution)/shard_map/ppermute | solution.py:24
  49.4 20.5 %collective-permute-start.9 = (bf16[768,256]{1,0:T(8,128)(2,1)}, bf16[768,256]{1,0:T(8,128)(2,1)S(1)}, u32[]{:S(2)}, u32[]{:S(2)}) collective-permute-start(bf16[768,256]{1,0:T(8,128)(2,1)} %collective-permute-done.5.refs_4_), channel_id=1, source_target_pairs={{1,0},{2,1},{3,2},{5,4},{6,5},{7,6},{9,8},{10,9},{11,10},{13,12},{... | collective-permute-start | bytes 1179656 | tf_op jit(solution)/shard_map/ppermute | solution.py:25
  52.6 17.3 %collective-permute-start.10 = (bf16[768,256]{1,0:T(8,128)(2,1)}, bf16[768,256]{1,0:T(8,128)(2,1)S(1)}, u32[]{:S(2)}, u32[]{:S(2)}) collective-permute-start(bf16[768,256]{1,0:T(8,128)(2,1)} %collective-permute-done.6.refs_7_), channel_id=1, source_target_pairs={{0,1},{1,2},{2,3},{4,5},{5,6},{6,7},{8,9},{9,10},{10,11},{12,13},{... | collective-permute-start | bytes 1179656 | tf_op jit(solution)/shard_map/ppermute | solution.py:24
  57.8 14.5 %collective-permute-start.11 = (bf16[768,256]{1,0:T(8,128)(2,1)}, bf16[768,256]{1,0:T(8,128)(2,1)S(1)}, u32[]{:S(2)}, u32[]{:S(2)}) collective-permute-start(bf16[768,256]{1,0:T(8,128)(2,1)} %collective-permute-done.7.refs_9_), channel_id=1, source_target_pairs={{1,0},{2,1},{3,2},{5,4},{6,5},{7,6},{9,8},{10,9},{11,10},{13,12},{... | collective-permute-start | bytes 1179656 | tf_op jit(solution)/shard_map/ppermute | solution.py:25
  78.2 3.6 %collective-permute-start.12 = (bf16[128,512]{1,0:T(8,128)(2,1)}, bf16[128,512]{1,0:T(8,128)(2,1)S(1)}, u32[]{:S(2)}, u32[]{:S(2)}) collective-permute-start(bf16[128,512]{1,0:T(8,128)(2,1)} %get-tuple-element.71), channel_id=1, source_target_pairs={{0,4},{4,0},{8,12},{12,8},{16,20},{20,16},{24,28},{28,24},{1,5},{5... | collective-permute-start | bytes 393224 | tf_op jit(solution)/shard_map/ppermute | solution.py:30
  78.3 9.4 %collective-permute-start.13 = (bf16[128,512]{1,0:T(8,128)(2,1)}, bf16[128,512]{1,0:T(8,128)(2,1)S(1)}, u32[]{:S(2)}, u32[]{:S(2)}) collective-permute-start(bf16[128,512]{1,0:T(8,128)(2,1)} %get-tuple-element.72), channel_id=1, source_target_pairs={{0,8},{4,12},{8,0},{12,4},{16,24},{20,28},{24,16},{28,20},{1,9},{5... | collective-permute-start | bytes 393224 | tf_op jit(solution)/shard_map/ppermute | solution.py:30
  79.9 14.7 %collective-permute-start.14 = (bf16[128,512]{1,0:T(8,128)(2,1)}, bf16[128,512]{1,0:T(8,128)(2,1)S(1)}, u32[]{:S(2)}, u32[]{:S(2)}) collective-permute-start(bf16[128,512]{1,0:T(8,128)(2,1)} %get-tuple-element.73), channel_id=1, source_target_pairs={{0,12},{4,8},{8,4},{12,0},{16,28},{20,24},{24,20},{28,16},{1,13},{... | collective-permute-start | bytes 393224 | tf_op jit(solution)/shard_map/ppermute | solution.py:30
  80.2 14.4 %collective-permute-start.15 = (bf16[128,512]{1,0:T(8,128)(2,1)}, bf16[128,512]{1,0:T(8,128)(2,1)S(1)}, u32[]{:S(2)}, u32[]{:S(2)}) collective-permute-start(bf16[128,512]{1,0:T(8,128)(2,1)} %get-tuple-element.74), channel_id=1, source_target_pairs={{0,16},{4,20},{8,24},{12,28},{16,0},{20,4},{24,8},{28,12},{1,17},{... | collective-permute-start | bytes 393224 | tf_op jit(solution)/shard_map/ppermute | solution.py:30
  81.7 12.9 %collective-permute-start.16 = (bf16[128,512]{1,0:T(8,128)(2,1)}, bf16[128,512]{1,0:T(8,128)(2,1)S(1)}, u32[]{:S(2)}, u32[]{:S(2)}) collective-permute-start(bf16[128,512]{1,0:T(8,128)(2,1)} %get-tuple-element.75), channel_id=1, source_target_pairs={{0,20},{4,16},{8,28},{12,24},{16,4},{20,0},{24,12},{28,8},{1,21},{... | collective-permute-start | bytes 393224 | tf_op jit(solution)/shard_map/ppermute | solution.py:30
  81.9 13.4 %collective-permute-start.17 = (bf16[128,512]{1,0:T(8,128)(2,1)}, bf16[128,512]{1,0:T(8,128)(2,1)S(1)}, u32[]{:S(2)}, u32[]{:S(2)}) collective-permute-start(bf16[128,512]{1,0:T(8,128)(2,1)} %get-tuple-element.76), channel_id=1, source_target_pairs={{0,24},{4,28},{8,16},{12,20},{16,8},{20,12},{24,0},{28,4},{1,25},{... | collective-permute-start | bytes 393224 | tf_op jit(solution)/shard_map/ppermute | solution.py:30
  87.7 9.9 %collective-permute-start.18 = (bf16[128,512]{1,0:T(8,128)(2,1)}, bf16[128,512]{1,0:T(8,128)(2,1)S(1)}, u32[]{:S(2)}, u32[]{:S(2)}) collective-permute-start(bf16[128,512]{1,0:T(8,128)(2,1)} %get-tuple-element.77), channel_id=1, source_target_pairs={{0,28},{4,24},{8,20},{12,16},{16,12},{20,8},{24,4},{28,0},{1,29},{... | collective-permute-start | bytes 393224 | tf_op jit(solution)/shard_map/ppermute | solution.py:30
  97.7 3.7 %collective-permute-start.23 = (bf16[128,512]{1,0:T(8,128)(2,1)}, bf16[128,512]{1,0:T(8,128)(2,1)S(1)}, u32[]{:S(2)}, u32[]{:S(2)}) collective-permute-start(bf16[128,512]{1,0:T(8,128)(2,1)} %get-tuple-element.87), channel_id=1, source_target_pairs={{0,4},{4,0},{8,12},{12,8},{16,20},{20,16},{24,28},{28,24},{1,5},{5... | collective-permute-start | bytes 393224 | tf_op jit(solution)/shard_map/ppermute | solution.py:30
  97.8 6.6 %collective-permute-start.24 = (bf16[128,512]{1,0:T(8,128)(2,1)}, bf16[128,512]{1,0:T(8,128)(2,1)S(1)}, u32[]{:S(2)}, u32[]{:S(2)}) collective-permute-start(bf16[128,512]{1,0:T(8,128)(2,1)} %get-tuple-element.88), channel_id=1, source_target_pairs={{0,8},{4,12},{8,0},{12,4},{16,24},{20,28},{24,16},{28,20},{1,9},{5... | collective-permute-start | bytes 393224 | tf_op jit(solution)/shard_map/ppermute | solution.py:30
  98.4 13.5 %collective-permute-start.25 = (bf16[128,512]{1,0:T(8,128)(2,1)}, bf16[128,512]{1,0:T(8,128)(2,1)S(1)}, u32[]{:S(2)}, u32[]{:S(2)}) collective-permute-start(bf16[128,512]{1,0:T(8,128)(2,1)} %get-tuple-element.89), channel_id=1, source_target_pairs={{0,12},{4,8},{8,4},{12,0},{16,28},{20,24},{24,20},{28,16},{1,13},{... | collective-permute-start | bytes 393224 | tf_op jit(solution)/shard_map/ppermute | solution.py:30
  99.5 15.7 %collective-permute-start.26 = (bf16[128,512]{1,0:T(8,128)(2,1)}, bf16[128,512]{1,0:T(8,128)(2,1)S(1)}, u32[]{:S(2)}, u32[]{:S(2)}) collective-permute-start(bf16[128,512]{1,0:T(8,128)(2,1)} %get-tuple-element.90), channel_id=1, source_target_pairs={{0,16},{4,20},{8,24},{12,28},{16,0},{20,4},{24,8},{28,12},{1,17},{... | collective-permute-start | bytes 393224 | tf_op jit(solution)/shard_map/ppermute | solution.py:30
  100.1 16.5 %collective-permute-start.27 = (bf16[128,512]{1,0:T(8,128)(2,1)}, bf16[128,512]{1,0:T(8,128)(2,1)S(1)}, u32[]{:S(2)}, u32[]{:S(2)}) collective-permute-start(bf16[128,512]{1,0:T(8,128)(2,1)} %get-tuple-element.91), channel_id=1, source_target_pairs={{0,20},{4,16},{8,28},{12,24},{16,4},{20,0},{24,12},{28,8},{1,21},{... | collective-permute-start | bytes 393224 | tf_op jit(solution)/shard_map/ppermute | solution.py:30
  101.3 15.2 %collective-permute-start.28 = (bf16[128,512]{1,0:T(8,128)(2,1)}, bf16[128,512]{1,0:T(8,128)(2,1)S(1)}, u32[]{:S(2)}, u32[]{:S(2)}) collective-permute-start(bf16[128,512]{1,0:T(8,128)(2,1)} %get-tuple-element.92), channel_id=1, source_target_pairs={{0,24},{4,28},{8,16},{12,20},{16,8},{20,12},{24,0},{28,4},{1,25},{... | collective-permute-start | bytes 393224 | tf_op jit(solution)/shard_map/ppermute | solution.py:30
  104.3 12.2 %collective-permute-start.29 = (bf16[128,512]{1,0:T(8,128)(2,1)}, bf16[128,512]{1,0:T(8,128)(2,1)S(1)}, u32[]{:S(2)}, u32[]{:S(2)}) collective-permute-start(bf16[128,512]{1,0:T(8,128)(2,1)} %get-tuple-element.93), channel_id=1, source_target_pairs={{0,28},{4,24},{8,20},{12,16},{16,12},{20,8},{24,4},{28,0},{1,29},{... | collective-permute-start | bytes 393224 | tf_op jit(solution)/shard_map/ppermute | solution.py:30
  111.9 18.7 %collective-permute-start.19 = (bf16[768,256]{1,0:T(8,128)(2,1)}, bf16[768,256]{1,0:T(8,128)(2,1)S(1)}, u32[]{:S(2)}, u32[]{:S(2)}) collective-permute-start(bf16[768,256]{1,0:T(8,128)(2,1)} %shard_map.57.refs_0_), channel_id=1, source_target_pairs={{0,1},{1,2},{2,3},{4,5},{5,6},{6,7},{8,9},{9,10},{10,11},{12,13},{... | collective-permute-start | bytes 1179656 | tf_op jit(solution)/shard_map/ppermute | solution.py:24
  115.2 20.0 %collective-permute-start.21 = (bf16[768,256]{1,0:T(8,128)(2,1)}, bf16[768,256]{1,0:T(8,128)(2,1)S(1)}, u32[]{:S(2)}, u32[]{:S(2)}) collective-permute-start(bf16[768,256]{1,0:T(8,128)(2,1)} %shard_map.57.refs_0_), channel_id=1, source_target_pairs={{1,0},{2,1},{3,2},{5,4},{6,5},{7,6},{9,8},{10,9},{11,10},{13,12},{... | collective-permute-start | bytes 1179656 | tf_op jit(solution)/shard_map/ppermute | solution.py:25
  124.8 14.3 %collective-permute-start.30 = (bf16[768,256]{1,0:T(8,128)(2,1)}, bf16[768,256]{1,0:T(8,128)(2,1)S(1)}, u32[]{:S(2)}, u32[]{:S(2)}) collective-permute-start(bf16[768,256]{1,0:T(8,128)(2,1)} %shard_map.59.refs_5_), channel_id=1, source_target_pairs={{0,1},{1,2},{2,3},{4,5},{5,6},{6,7},{8,9},{9,10},{10,11},{12,13},{... | collective-permute-start | bytes 1179656 | tf_op jit(solution)/shard_map/ppermute | solution.py:24
  129.3 14.1 %collective-permute-start.32 = (bf16[768,256]{1,0:T(8,128)(2,1)}, bf16[768,256]{1,0:T(8,128)(2,1)S(1)}, u32[]{:S(2)}, u32[]{:S(2)}) collective-permute-start(bf16[768,256]{1,0:T(8,128)(2,1)} %shard_map.59.refs_5_), channel_id=1, source_target_pairs={{1,0},{2,1},{3,2},{5,4},{6,5},{7,6},{9,8},{10,9},{11,10},{13,12},{... | collective-permute-start | bytes 1179656 | tf_op jit(solution)/shard_map/ppermute | solution.py:25
  130.7 31.6 %copy-start.4 = (bf16[768,256]{1,0:T(8,128)(2,1)}, bf16[768,256]{1,0:T(8,128)(2,1)S(1)}, u32[]{:S(2)}) copy-start(bf16[768,256]{1,0:T(8,128)(2,1)S(1)} %collective-permute-done.19.refs_1_) | copy-start | bytes 1179652
  130.7 16.7 %collective-permute-start.20 = (bf16[768,256]{1,0:T(8,128)(2,1)S(1)}, bf16[768,256]{1,0:T(8,128)(2,1)S(1)}, u32[]{:S(2)}, u32[]{:S(2)}) collective-permute-start(bf16[768,256]{1,0:T(8,128)(2,1)S(1)} %collective-permute-done.19.refs_1_), channel_id=1, source_target_pairs={{0,1},{1,2},{2,3},{4,5},{5,6},{6,7},{8,9},{9,10},{10,11},{12,13},{... | collective-permute-start | bytes 1179656 | tf_op jit(solution)/shard_map/ppermute | solution.py:24
  135.3 27.1 %copy-start.5 = (bf16[768,256]{1,0:T(8,128)(2,1)}, bf16[768,256]{1,0:T(8,128)(2,1)S(1)}, u32[]{:S(2)}) copy-start(bf16[768,256]{1,0:T(8,128)(2,1)S(1)} %collective-permute-done.21.refs_3_) | copy-start | bytes 1179652
  135.3 16.6 %collective-permute-start.22 = (bf16[768,256]{1,0:T(8,128)(2,1)S(1)}, bf16[768,256]{1,0:T(8,128)(2,1)S(1)}, u32[]{:S(2)}, u32[]{:S(2)}) collective-permute-start(bf16[768,256]{1,0:T(8,128)(2,1)S(1)} %collective-permute-done.21.refs_3_), channel_id=1, source_target_pairs={{1,0},{2,1},{3,2},{5,4},{6,5},{7,6},{9,8},{10,9},{11,10},{13,12},{... | collective-permute-start | bytes 1179656 | tf_op jit(solution)/shard_map/ppermute | solution.py:25
  139.1 23.2 %copy-start.6 = (bf16[768,256]{1,0:T(8,128)(2,1)}, bf16[768,256]{1,0:T(8,128)(2,1)S(1)}, u32[]{:S(2)}) copy-start(bf16[768,256]{1,0:T(8,128)(2,1)S(1)} %collective-permute-done.30.refs_6_) | copy-start | bytes 1179652
  139.1 16.7 %collective-permute-start.31 = (bf16[768,256]{1,0:T(8,128)(2,1)S(1)}, bf16[768,256]{1,0:T(8,128)(2,1)S(1)}, u32[]{:S(2)}, u32[]{:S(2)}) collective-permute-start(bf16[768,256]{1,0:T(8,128)(2,1)S(1)} %collective-permute-done.30.refs_6_), channel_id=1, source_target_pairs={{0,1},{1,2},{2,3},{4,5},{5,6},{6,7},{8,9},{9,10},{10,11},{12,13},{... | collective-permute-start | bytes 1179656 | tf_op jit(solution)/shard_map/ppermute | solution.py:24
  143.4 17.5 %collective-permute-start.33 = (bf16[768,256]{1,0:T(8,128)(2,1)S(1)}, bf16[768,256]{1,0:T(8,128)(2,1)S(1)}, u32[]{:S(2)}, u32[]{:S(2)}) collective-permute-start(bf16[768,256]{1,0:T(8,128)(2,1)S(1)} %collective-permute-done.32.refs_8_), channel_id=1, source_target_pairs={{1,0},{2,1},{3,2},{5,4},{6,5},{7,6},{9,8},{10,9},{11,10},{13,12},{... | collective-permute-start | bytes 1179656 | tf_op jit(solution)/shard_map/ppermute | solution.py:25
  147.4 21.0 %collective-permute-start.34 = (bf16[768,256]{1,0:T(8,128)(2,1)S(1)}, bf16[768,256]{1,0:T(8,128)(2,1)S(1)}, u32[]{:S(2)}, u32[]{:S(2)}) collective-permute-start(bf16[768,256]{1,0:T(8,128)(2,1)S(1)} %collective-permute-done.20.refs_2_), channel_id=1, source_target_pairs={{0,1},{1,2},{2,3},{4,5},{5,6},{6,7},{8,9},{9,10},{10,11},{12,13},{... | collective-permute-start | bytes 1179656 | tf_op jit(solution)/shard_map/ppermute | solution.py:24
  151.9 17.0 %collective-permute-start.35 = (bf16[768,256]{1,0:T(8,128)(2,1)S(1)}, bf16[768,256]{1,0:T(8,128)(2,1)}, u32[]{:S(2)}, u32[]{:S(2)}) collective-permute-start(bf16[768,256]{1,0:T(8,128)(2,1)S(1)} %collective-permute-done.22.refs_4_), channel_id=1, source_target_pairs={{1,0},{2,1},{3,2},{5,4},{6,5},{7,6},{9,8},{10,9},{11,10},{13,12},{... | collective-permute-start | bytes 1179656 | tf_op jit(solution)/shard_map/ppermute | solution.py:25
  155.8 16.2 %collective-permute-start.36 = (bf16[768,256]{1,0:T(8,128)(2,1)S(1)}, bf16[768,256]{1,0:T(8,128)(2,1)}, u32[]{:S(2)}, u32[]{:S(2)}) collective-permute-start(bf16[768,256]{1,0:T(8,128)(2,1)S(1)} %collective-permute-done.31.refs_7_), channel_id=1, source_target_pairs={{0,1},{1,2},{2,3},{4,5},{5,6},{6,7},{8,9},{9,10},{10,11},{12,13},{... | collective-permute-start | bytes 1179656 | tf_op jit(solution)/shard_map/ppermute | solution.py:24
  161.0 15.3 %collective-permute-start.37 = (bf16[768,256]{1,0:T(8,128)(2,1)S(1)}, bf16[768,256]{1,0:T(8,128)(2,1)}, u32[]{:S(2)}, u32[]{:S(2)}) collective-permute-start(bf16[768,256]{1,0:T(8,128)(2,1)S(1)} %collective-permute-done.33.refs_9_), channel_id=1, source_target_pairs={{1,0},{2,1},{3,2},{5,4},{6,5},{7,6},{9,8},{10,9},{11,10},{13,12},{... | collective-permute-start | bytes 1179656 | tf_op jit(solution)/shard_map/ppermute | solution.py:25
  (27 other events, 210.0 us)
Sparse Core Ops, SparseCore 0:
  9.2 48.2 all-gather.2
  59.4 32.0 all-gather.4

commit v3 on v2

--- a/solution.py
+++ b/solution.py
@@ -30,11 +30,24 @@
     return lax.ppermute(x, axis, [(i, i ^ s) for i in range(size)])
 
 
+def halves(x):
+    return [x[: x.shape[0] // 2], x[x.shape[0] // 2 :]]
+
+
+def forward(pieces, s, axis, size):
+    a = s & -s
+    b = s ^ a
+    via_a, via_b = sum(map(halves, pieces[b]), [])[:2], sum(map(halves, pieces[a]), [])[-2:]
+    if len(pieces[b]) > 1 or len(pieces[a]) > 1:
+        return [swap(x, a, axis, size) for x in pieces[b]]
+    return [swap(via_a[0], a, axis, size), swap(via_b[-1], b, axis, size)]
+
+
 def tile_of(columns):
     return 256 if columns % 256 == 0 else 128
 
 
-def accumulate_kernel(place, *refs, reach, hid_size, cut):
+def accumulate_kernel(place, *refs, reach, hid_size, layout, arrays, cut):
     chunks = len(reach)
     refs = list(refs)
     parts = []
@@ -43,10 +56,12 @@
         from_left = [refs.pop(0) for _ in range(reach[c])]
         from_right = [refs.pop(0) for _ in range(reach[c])]
         parts.append((own, from_left, from_right))
-    panel = refs.pop(0)
+    stacks = [refs.pop(0) for _ in range(arrays)]
+    tok_size = len(layout)
     total, last_rows, rows, weights, sums, row_sem, weight_sem, last_sem, sum_sem = refs
-    at_hid = place[0]
+    at_hid, at_tok = place[0], place[1]
     width = cut * chunks
+    depth = sum(n for _, _, n in layout[0])
     columns = total.shape[1]
 
     def each(act):
@@ -65,9 +80,19 @@
                 def _():
                     act(copy(from_right[k - 1], at_hid + k, hid_size - 1 + k))
 
-    weight_copy = pltpu.make_async_copy(panel, weights, weight_sem)
+    weight_copies = []
+    for s in range(tok_size):
+        at = (at_tok ^ s) * depth
+        for array, first, n in layout[s]:
+            here = pl.ds(pl.multiple_of(at, n), n)
+            weight_copies.append(pltpu.make_async_copy(
+                stacks[array].at[pl.ds(first, n), :], weights.at[here, :], weight_sem.at[len(weight_copies)]
+            ))
+            at = at + n
+
     each(lambda d: d.start())
-    weight_copy.start()
+    for copy in weight_copies:
+        copy.start()
     for c in range(chunks):
         if reach[c] < hid_size - 1:
             for end, source in ((0, hid_size - 1), (hid_size - 1, 0)):
@@ -75,7 +100,8 @@
                 def _():
                     at = source * width + c * cut
                     rows[:, at : at + cut] = jnp.zeros((rows.shape[0], cut), rows.dtype)
-    weight_copy.wait()
+    for copy in weight_copies:
+        copy.wait()
     source = jnp.where(at_hid == 0, hid_size - 1, 0)
     lasts = []
     for c in range(chunks):
@@ -101,8 +127,9 @@
         copy.wait()
 
 
-def accumulate(place, parts, panel, reach, hid_size):
-    columns = panel.shape[1]
+def accumulate(place, parts, stacks, layout, reach, hid_size):
+    columns = stacks[0].shape[1]
+    copies = sum(map(len, layout))
     chunks = len(parts)
     tok_rows, cut = parts[0][0].shape
     full = cut * chunks * hid_size
@@ -112,20 +139,21 @@
     deferred = sum(r < hid_size - 1 for r in reach)
     return pl.pallas_call(
         functools.partial(
-            accumulate_kernel, reach=reach, hid_size=hid_size, cut=cut
+            accumulate_kernel, reach=reach, hid_size=hid_size, layout=layout,
+            arrays=len(stacks), cut=cut,
         ),
         out_shape=[
             jax.ShapeDtypeStruct((tok_rows, columns), jnp.float32),
             jax.ShapeDtypeStruct((deferred * cut, columns), jnp.bfloat16),
         ],
-        in_specs=[SMEM] + [HBM] * (len(flat) + 1),
+        in_specs=[SMEM] + [HBM] * (len(flat) + len(stacks)),
         out_specs=[HBM, HBM],
         scratch_shapes=[
             pltpu.VMEM((tok_rows, full), jnp.bfloat16),
             pltpu.VMEM((full, columns), jnp.bfloat16),
             pltpu.VMEM((tok_rows, columns), jnp.float32),
             pltpu.SemaphoreType.DMA((chunks, 2 * hid_size - 1)),
-            pltpu.SemaphoreType.DMA,
+            pltpu.SemaphoreType.DMA((copies,)),
             pltpu.SemaphoreType.DMA((deferred,)),
             pltpu.SemaphoreType.DMA((columns // tile_of(columns),)),
         ],
@@ -133,7 +161,7 @@
         cost_estimate=pl.CostEstimate(
             flops=2 * tok_rows * full * columns, bytes_accessed=2 * full * (tok_rows + columns), transcendentals=0
         ),
-    )(place, *flat, panel)
+    )(place, *flat, *stacks)
 
 
 def finish_kernel(place, send_ids, *refs, deferred, hid_size, cut, begin, columns, n_sends):
@@ -194,12 +222,13 @@
             emit(n, sums[:, n : n + step].astype(jnp.bfloat16))
 
     copies = []
-    for s in range(n_sends):
-        for slot in range(2):
-            at = pl.multiple_of(send_ids[s + 1, slot] * BLK, BLK)
+    for i in range(n_sends):
+        for slot in range(targets[2 + i].shape[0] // BLK):
+            peer = place[1] ^ (1 if i == 0 else 2 * i + slot // 2)
+            at = pl.multiple_of(send_ids[peer, slot % 2] * BLK, BLK)
             copies.append(pltpu.make_async_copy(
-                outs[1].at[pl.ds(at, BLK), :], targets[2 + s].at[pl.ds(slot * BLK, BLK), :],
-                out_sem.at[2 + 2 * s + slot],
+                outs[1].at[pl.ds(at, BLK), :], targets[2 + i].at[pl.ds(slot * BLK, BLK), :],
+                out_sem.at[2 + len(copies)],
             ))
     for n, value in enumerate(outs):
         copies.append(pltpu.make_async_copy(value, targets[n], out_sem.at[n]))
@@ -216,7 +245,7 @@
     bf16 = lambda *shape: jax.ShapeDtypeStruct(shape, jnp.bfloat16)
     if n_sends:
         wide = columns // 3
-        shapes = [bf16(tok_rows, wide), bf16(tok_rows, 2 * wide)] + [bf16(2 * BLK, 2 * wide)] * n_sends
+        shapes = [bf16(tok_rows, wide), bf16(tok_rows, 2 * wide)] + [bf16((2 if i == 0 else 4) * BLK, 2 * wide) for i in range(n_sends)]
     else:
         shapes = [bf16(tok_rows, columns)]
     flat = [x for pair in lasts for x in pair]
@@ -235,7 +264,7 @@
             pltpu.SemaphoreType.DMA,
             pltpu.SemaphoreType.DMA((deferred,)),
             pltpu.SemaphoreType.DMA,
-            pltpu.SemaphoreType.DMA((2 + 2 * n_sends,)),
+            pltpu.SemaphoreType.DMA((2 + 4 * n_sends,)),
         ],
         compiler_params=pltpu.CompilerParams(vmem_limit_bytes=VMEM_LIMIT),
         cost_estimate=pl.CostEstimate(
@@ -244,9 +273,9 @@
     )(place, send_ids, total, *flat, last_rows)
 
 
-def attend_kernel(lists, counts, query_all, key_values, *refs, tok_size, heads):
-    remote = refs[: tok_size - 1]
-    target, pool, queries, result, sem = refs[tok_size - 1 :]
+def attend_kernel(place, lists, counts, query_all, key_values, *refs, tok_size, heads):
+    passed, remote = refs[0], refs[1 : tok_size // 2]
+    target, pool, queries, result, sem = refs[tok_size // 2 :]
     tok_rows = queries.shape[0]
     blocks = tok_rows // BLK
     wide = heads * HEAD_WIDTH
@@ -254,9 +283,10 @@
         pltpu.make_async_copy(key_values, pool.at[pl.ds(0, tok_rows), :], sem.at[tok_size - 1]),
         pltpu.make_async_copy(query_all, queries, sem.at[tok_size]),
     ]
-    for s in range(tok_size - 1):
+    for s in range(1, tok_size):
+        ref = passed.at[pl.ds((s // 2) * 2 * BLK, 2 * BLK), :] if s % 2 else remote[s // 2 - 1].at[pl.ds(0, 2 * BLK), :]
         copies.append(pltpu.make_async_copy(
-            remote[s], pool.at[pl.ds(tok_rows + s * 2 * BLK, 2 * BLK), :], sem.at[s]
+            ref, pool.at[pl.ds(tok_rows + (s - 1) * 2 * BLK, 2 * BLK), :], sem.at[s - 1]
         ))
     for copy in copies:
         copy.start()
@@ -271,12 +301,12 @@
 
     def block(b):
         at = pl.multiple_of(b * BLK, BLK)
-        starts = [pl.multiple_of(lists[b, j] * BLK, BLK) for j in range(NEIGH)]
+        starts = [pl.multiple_of(lists[0, b * NEIGH + j] * BLK, BLK) for j in range(NEIGH)]
         query = jnp.concatenate([queries[pl.ds(at, BLK), :]] * heads, axis=0)
         query = jnp.where(diagonal, query, jnp.zeros_like(query))
         keys = jnp.concatenate([pool[pl.ds(i, BLK), :wide] for i in starts], axis=0)
         logits = lax.dot_general(query, keys, (((1,), (1,)), ((), ())), preferred_element_type=jnp.float32)
-        logits = jnp.where(column < counts[b] * BLK, logits, -1e30)
+        logits = jnp.where(column < counts[place[1] * blocks + b] * BLK, logits, -1e30)
         highest = jnp.max(logits, axis=1, keepdims=True)
         expon = jnp.exp2((logits - highest) * scale)
         total = jnp.sum(expon, axis=1, keepdims=True)
@@ -299,13 +329,13 @@
     copy.wait()
 
 
-def attend(lists, counts, query, key_values, remote, tok_size):
+def attend(place, lists, counts, query, key_values, remote, tok_size):
     tok_rows, wide = query.shape
     heads = wide // HEAD_WIDTH
     return pl.pallas_call(
         functools.partial(attend_kernel, tok_size=tok_size, heads=heads),
         out_shape=jax.ShapeDtypeStruct((tok_rows, wide), jnp.bfloat16),
-        in_specs=[SMEM] * 2 + [HBM] * (tok_size + 1),
+        in_specs=[SMEM] * 3 + [HBM] * (2 + tok_size // 2),
         out_specs=HBM,
         scratch_shapes=[
             pltpu.VMEM((tok_rows + (tok_size - 1) * 2 * BLK, 2 * wide), jnp.bfloat16),
@@ -319,31 +349,42 @@
             bytes_accessed=2 * tok_rows * wide * 10,
             transcendentals=tok_rows * NEIGH * BLK * heads,
         ),
-    )(lists, counts, query, key_values, *remote)
-
-
-def routes(neighbours, counts, at_tok, tok_size, blocks):
-    lists = neighbours.reshape(tok_size, blocks * NEIGH)
-    valid = (jnp.arange(NEIGH)[None, :] < counts[:, None]).reshape(tok_size, blocks * NEIGH)
-    owner = lists // blocks
-    peers = jnp.arange(tok_size) ^ at_tok
-    named = valid & (owner == at_tok)
-    low = jnp.min(jnp.where(named, lists, tok_size * blocks), axis=1)
-    high = jnp.max(jnp.where(named, lists, -1), axis=1)
+    )(place, lists, counts, query, key_values, *remote)
+
+
+def routes_kernel(place, lists_ref, send_ids, pool_at, *, blocks):
+    at_tok = place[1]
+    tok_size = lists_ref.shape[0]
+    lists = lists_ref[...]
     base = at_tok * blocks
-    sends = jnp.clip(jnp.stack([low, high], axis=1) - base, 0, blocks - 1)
-    send_ids = sends[peers]
-    mine = lax.dynamic_slice_in_dim(lists, at_tok, 1, 0)[0]
-    mine_valid = lax.dynamic_slice_in_dim(valid, at_tok, 1, 0)[0]
-    mine_owner = mine // blocks
-    same = (mine_owner[:, None] == mine_owner[None, :]) & mine_valid[None, :]
-    first = jnp.min(jnp.where(same, mine[None, :], tok_size * blocks), axis=1)
-    slot = (mine != first).astype(jnp.int32)
-    there = blocks + ((mine_owner ^ at_tok) - 1) * 2 + slot
-    pool_at = jnp.where(mine_owner == at_tok, mine - base, there)
-    pool_at = jnp.where(mine_valid, pool_at, 0).reshape(blocks, NEIGH)
-    my_counts = lax.dynamic_slice_in_dim(counts, at_tok * blocks, blocks, 0)
-    return send_ids.astype(jnp.int32), pool_at.astype(jnp.int32), my_counts
+    named = (lists >= base) & (lists < base + blocks)
+    low = jnp.min(jnp.where(named, lists - base, blocks - 1), axis=1, keepdims=True)
+    high = jnp.max(jnp.where(named, lists - base, 0), axis=1, keepdims=True)
+    side = lax.broadcasted_iota(jnp.int32, send_ids.shape, 1)
+    send_ids[...] = jnp.where(side == 0, low, high)
+    mine = lists_ref[pl.ds(at_tok, 1), :]
+    at = jnp.where((mine >= base) & (mine < base + blocks), mine - base, 0)
+    for p in range(tok_size):
+        here = (mine >= p * blocks) & (mine < (p + 1) * blocks)
+        first = jnp.min(jnp.where(here, mine, tok_size * blocks), axis=1, keepdims=True)
+        there = blocks + ((at_tok ^ p) - 1) * 2 + (mine != first).astype(jnp.int32)
+        at = jnp.where(here & (p != at_tok), there, at)
+    pool_at[...] = at
+
+
+def routes(place, neighbours, counts, tok_size, blocks):
+    usable = jnp.arange(NEIGH)[None, :] < counts[:, None]
+    lists = jnp.where(usable, neighbours, -1).reshape(tok_size, blocks * NEIGH)
+    vmem = pl.BlockSpec(memory_space=pltpu.VMEM)
+    return pl.pallas_call(
+        functools.partial(routes_kernel, blocks=blocks),
+        out_shape=[
+            jax.ShapeDtypeStruct((tok_size, 128), jnp.int32),
+            jax.ShapeDtypeStruct((1, blocks * NEIGH), jnp.int32),
+        ],
+        in_specs=[SMEM, vmem],
+        out_specs=[vmem, vmem],
+    )(place, lists)
 
 
 def shards(tokens, qkv_weight, out_weight, neighbours, counts, *, tok_size, hid_size):
@@ -357,35 +398,66 @@
     far = hid_size - 1
     out_columns = out_weight.shape[1]
 
-    qkv_panel = lax.all_gather(qkv_weight, "tok", axis=0, tiled=True)
-    out_panel = lax.all_gather(out_weight, "tok", axis=0, tiled=True)
-    parts = [(tokens[:, c * cut : (c + 1) * cut], [], []) for c in range(chunks)]
-    parts = [line_step(p, "hid", hid_size) for p in parts]
-    parts[-1], ids = lax.optimization_barrier(
-        (parts[-1], routes(neighbours, counts, at_tok, tok_size, blocks))
+    weight = qkv_weight
+    near = [s for s in range(2, tok_size) if s & (s - 1) == 0]
+    even = range(0, tok_size, 2)
+    pieces = [[weight]] + [None] * (tok_size - 1)
+    part = line_step((tokens, [], []), "hid", hid_size)
+    for s in near:
+        pieces[s] = [swap(weight, s, "tok", tok_size)]
+    part, (send_ids, pool_at) = lax.optimization_barrier(
+        (part, routes(place, neighbours, counts, tok_size, blocks))
     )
-    send_ids, pool_at, my_counts = ids
+    bits = [1 << i for i in reversed(range(tok_size.bit_length() - 1))]
+    out_rows, out_ids = out_weight, [0]
+    for bit in bits[:-2]:
+        came = swap(out_rows, bit, "tok", tok_size)
+        came, held = lax.optimization_barrier((came, [pieces[s] for s in near]))
+        for s, piece in zip(near, held):
+            pieces[s] = piece
+        out_rows, out_ids = jnp.concatenate([out_rows, came], axis=0), out_ids + [s ^ bit for s in out_ids]
+    came = swap(out_rows, 2, "tok", tok_size)
     for _ in range(far - 1):
-        parts = [line_step(p, "hid", hid_size) for p in parts]
-
-    total, last_rows = accumulate(place, parts, qkv_panel, [far - 1] * chunks, hid_size)
+        part = line_step(part, "hid", hid_size)
+    for s in even:
+        if pieces[s] is None:
+            pieces[s] = forward(pieces, s, "tok", tok_size)
+    held = lax.optimization_barrier([pieces[s] for s in even])
+    for s, piece in zip(even, held):
+        pieces[s + 1] = [swap(x, 1, "tok", tok_size) for x in piece]
+    parts = [part]
+
+    stacks, layout = [], []
+    for piece in pieces:
+        layout.append([(len(stacks) + i, 0, x.shape[0]) for i, x in enumerate(piece)])
+        stacks += piece
+    total, last_rows = accumulate(place, parts, stacks, layout, [far - 1], hid_size)
+    total, came = lax.optimization_barrier((total, came))
+    out_rows, out_ids = jnp.concatenate([out_rows, came], axis=0), out_ids + [s ^ 2 for s in out_ids]
+    came = swap(out_rows, 1, "tok", tok_size)
     lasts = [(from_left[-1], from_right[-1]) for _, from_left, from_right in parts]
-    parts, remote = [], []
+    groups = [
+        finish(place, send_ids, total, lasts, last_rows, c * 3 * cut, 3 * cut, hid_size, tok_size // 2)
+        for c in range(chunks)
+    ]
+    parts = []
     for c in range(chunks):
-        columns = 3 * cut
-        query, key_values, *sends = finish(
-            place, send_ids, total, lasts, last_rows, c * columns, columns, hid_size, tok_size - 1
+        query, key_values, *sends = groups[c]
+        remote = [swap(sends[i], 2 * i, "tok", tok_size) for i in range(1, tok_size // 2)]
+        remote, groups[c + 1 :], _ = lax.optimization_barrier(
+            (remote, groups[c + 1 :], [p[0] for p in parts])
         )
-        sends, remote = lax.optimization_barrier((sends, remote))
-        remote = [swap(sends[s - 1], s, "tok", tok_size) for s in range(1, tok_size)]
-        if parts:
-            remote, _ = lax.optimization_barrier((remote, parts[-1][0]))
-        mixed = attend(pool_at, my_counts, query, key_values, remote, tok_size)
+        passed = jnp.concatenate([sends[0]] + [x[2 * BLK :] for x in remote], axis=0)
+        remote = [swap(passed, 1, "tok", tok_size)] + remote
+        mixed = attend(place, pool_at, counts, query, key_values, remote, tok_size)
         part = (mixed, [], [])
         for _ in range(far):
             part = line_step(part, "hid", hid_size)
         parts.append(part)
-    total, last_rows = accumulate(place, parts, out_panel, [far - 1] * chunks, hid_size)
+    depth = out_weight.shape[0]
+    layout = [[(s not in out_ids, out_ids.index(s if s in out_ids else s ^ 1) * depth, depth)] for s in range(tok_size)]
+    layout = [[(int(a), first, n)] for ((a, first, n),) in layout]
+    total, last_rows = accumulate(place, parts, [out_rows, came], layout, [far - 1] * chunks, hid_size)
     lasts = [(from_left[-1], from_right[-1]) for _, from_left, from_right in parts]
     (result,) = finish(place, send_ids, total, lasts, last_rows, 0, out_columns, hid_size, 0)
     return result

time: 188 us -> 180 us (0.957)
  waiting for transfers between devices: 36 us -> 55.5 us
  starting transfers between devices: 82.5 us -> 65.9 us
  between operations: 14.2 us -> 0.59 us
    ppermute x12 -> x9, starting transfers between devices: 55.2 us -> 38.8 us  [line_step(): left = lax.ppermute((from_left or [own])[-1], axis, to_right)]
    ppermute x14 -> x20, waiting for transfers between devices: 8.95 us -> 18.8 us  [swap(): return lax.ppermute(x, axis, [(i, i ^ s) for i in range(size)])]
    ppermute x12 -> x9, waiting for transfers between devices: 10.2 us -> 18.1 us  [line_step(): right = lax.ppermute((from_right or [own])[-1], axis, to_left)]
    ppermute x12 -> x9, starting transfers between devices: 15.4 us -> 11.6 us  [line_step(): right = lax.ppermute((from_right or [own])[-1], axis, to_left)]
    ppermute x14 -> x20, starting transfers between devices: 11.8 us -> 15.6 us  [swap(): return lax.ppermute(x, axis, [(i, i ^ s) for i in range(size)])]
    unnamed x71 -> x64, local copies, waits for them, and re-layouts: 1.62 us -> 5.08 us
    ppermute x12 -> x9, waiting for transfers between devices: 16 us -> 18.6 us  [line_step(): left = lax.ppermute((from_left or [own])[-1], axis, to_right)]
  transfers between devices with their start and end apart: 40 -> 38, of which waited for: 17 -> 18; matrix products, arithmetic and copies ran while one was open for 4% -> 2% of each run, Pallas kernels for 22% -> 22%
where the time goes in v3:
time: 180 us; the launch traced here: 179 us
  starting transfers between devices  65.9 us (37%)
  waiting for transfers between devices  55.5 us (31%)
  Pallas kernels  47.8 us (27%)
  local copies, waits for them, and re-layouts  7.26 us (4%)
    ppermute x9, starting transfers between devices, line_step(): left = lax.ppermute((from_left or [own])[-1], axis, to_right)  38.8 us
    ppermute x20, waiting for transfers between devices, swap(): return lax.ppermute(x, axis, [(i, i ^ s) for i in range(size)])  18.8 us
    ppermute x9, waiting for transfers between devices, line_step(): left = lax.ppermute((from_left or [own])[-1], axis, to_right)  18.6 us
    ppermute x9, waiting for transfers between devices, line_step(): right = lax.ppermute((from_right or [own])[-1], axis, to_left)  18.1 us
    pallas_call x2, Pallas kernels, accumulate(): pl.pallas_call(functools.partial(accumulate_kernel, reach=reach, hid_size...  16.9 us
    ppermute x20, starting transfers between devices, swap(): return lax.ppermute(x, axis, [(i, i ^ s) for i in range(size)])  15.6 us
    pallas_call x2, Pallas kernels, attend(): pl.pallas_call(functools.partial(attend_kernel, tok_size=tok_size, heads=...  15 us
    pallas_call x3, Pallas kernels, finish(): pl.pallas_call(functools.partial(finish_kernel, deferred=deferred, hid_si...  14.5 us
  transfers between devices with their start and end apart: 38, of which 18 were waited for; matrix products, arithmetic and copies ran while one was open for 2% of the time, Pallas kernels for 22%

profile of v3, /device:TPU:0, one launch (start us, length us, event | category | flops | bytes accessed | tf_op | source)
XLA Modules:
  0.0 178.5 jit_solution(12644250816089431686)
XLA Ops:
  0.0 5.1 %collective-permute-start = (bf16[768,512]{1,0:T(8,128)(2,1)}, bf16[768,512]{1,0:T(8,128)(2,1)S(1)}, u32[]{:S(2)}, u32[]{:S(2)}) collective-permute-start(bf16[768,512]{1,0:T(8,128)(2,1)} %refs_0_), channel_id=1, source_target_pairs={{0,1},{1,2},{2,3},{4,5},{5,6},{6,7},{8,9},{9,10},{10,11},{12,13},{... | collective-permute-start | bytes 2359304 | tf_op jit(solution)/shard_map/ppermute | solution.py:24
  5.1 1.3 collective-permute-start.1
  6.4 1.6 collective-permute-start.5
  8.0 1.5 collective-permute-start.6
  12.1 1.5 shard_map.55
  13.6 8.6 %collective-permute-done.refs_1_ = bf16[768,512]{1,0:T(8,128)(2,1)S(1)} collective-permute-done((bf16[768,512]{1,0:T(8,128)(2,1)}, bf16[768,512]{1,0:T(8,128)(2,1)S(1)}, u32[]{:S(2)}, u32[]{:S(2)}) %collective-permute-start) | collective-permute-done | bytes 786464 | tf_op jit(solution)/shard_map/ppermute | solution.py:24
  22.2 4.1 %collective-permute-done.1.refs_3_ = bf16[768,512]{1,0:T(8,128)(2,1)S(1)} collective-permute-done((bf16[768,512]{1,0:T(8,128)(2,1)}, bf16[768,512]{1,0:T(8,128)(2,1)S(1)}, u32[]{:S(2)}, u32[]{:S(2)}) %collective-permute-start.1) | collective-permute-done | bytes 786464 | tf_op jit(solution)/shard_map/ppermute | solution.py:25
  26.2 4.3 %collective-permute-start.2 = (bf16[768,512]{1,0:T(8,128)(2,1)S(1)}, bf16[768,512]{1,0:T(8,128)(2,1)}, u32[]{:S(2)}, u32[]{:S(2)}) collective-permute-start(bf16[768,512]{1,0:T(8,128)(2,1)S(1)} %collective-permute-done.refs_1_), channel_id=1, source_target_pairs={{0,1},{1,2},{2,3},{4,5},{5,6},{6,7},{8,9},{9,10},{10,11},{12,13},{... | collective-permute-start | bytes 2359304 | tf_op jit(solution)/shard_map/ppermute | solution.py:24
  30.5 1.3 collective-permute-start.3
  32.5 1.3 slice.24
  34.8 1.6 collective-permute-start.8
  36.3 6.9 %collective-permute-done.7.refs_11_ = bf16[128,1536]{1,0:T(8,128)(2,1)S(1)} collective-permute-done((bf16[128,1536]{1,0:T(8,128)(2,1)S(1)}, bf16[128,1536]{1,0:T(8,128)(2,1)S(1)}, u32[]{:S(2)}, u32[]{:S(2)}) %collective-permute-start.7) | collective-permute-done | bytes 393248 | tf_op jit(solution)/shard_map/ppermute | solution.py:30
  45.4 5.1 %collective-permute-done.3.refs_4_ = bf16[768,512]{1,0:T(8,128)(2,1)} collective-permute-done((bf16[768,512]{1,0:T(8,128)(2,1)S(1)}, bf16[768,512]{1,0:T(8,128)(2,1)}, u32[]{:S(2)}, u32[]{:S(2)}) %collective-permute-start.3) | collective-permute-done | bytes 786464 | tf_op jit(solution)/shard_map/ppermute | solution.py:25
  50.5 2.7 %collective-permute-start.15 = (bf16[768,512]{1,0:T(8,128)(2,1)}, bf16[768,512]{1,0:T(8,128)(2,1)S(1)}, u32[]{:S(2)}, u32[]{:S(2)}) collective-permute-start(bf16[768,512]{1,0:T(8,128)(2,1)} %collective-permute-done.2.refs_2_), channel_id=1, source_target_pairs={{0,1},{1,2},{2,3},{4,5},{5,6},{6,7},{8,9},{9,10},{10,11},{12,13},{... | collective-permute-start | bytes 2359304 | tf_op jit(solution)/shard_map/ppermute | solution.py:24
  53.9 1.3 collective-permute-start.16
  55.3 1.6 collective-permute-start.14
  57.7 10.8 %shard_map.56 = (f32[768,1536]{1,0:T(8,128)}, bf16[512,1536]{1,0:T(8,128)(2,1)}) custom-call(s32[2]{0:T(128)} %pad_add_fusion.place, bf16[768,512]{1,0:T(8,128)(2,1)} %refs_0_, bf16[768,512]{1,0:T(8,128)(2,1)} %copy-done.20, bf16[768,512]{1,0:T(8,128)(2,1)} %collective-permute-done.2.refs_2_, bf16[768,512]{1,0:T(8,128)(2,1)} %copy-done.21, ...), custom_call_target="tpu_custom_call" | custom-call | flops 4831838208 | bytes 9437184 | tf_op jit(solution)/shard_map/pallas_call | solution.py:140
  69.4 1.4 collective-permute-done.15.refs_1_
  70.8 4.8 %collective-permute-done.16.refs_2_ = bf16[768,512]{1,0:T(8,128)(2,1)S(1)} collective-permute-done((bf16[768,512]{1,0:T(8,128)(2,1)}, bf16[768,512]{1,0:T(8,128)(2,1)S(1)}, u32[]{:S(2)}, u32[]{:S(2)}) %collective-permute-start.16) | collective-permute-done | bytes 786464 | tf_op jit(solution)/shard_map/ppermute | solution.py:25
  76.6 5.2 %shard_map.57 = (bf16[768,256]{1,0:T(8,128)(2,1)}, bf16[768,512]{1,0:T(8,128)(2,1)}, bf16[128,512]{1,0:T(8,128)(2,1)}, bf16[256,512]{1,0:T(8,128)(2,1)}, bf16[25...) custom-call(s32[2]{0:T(128)} %pad_add_fusion.place, s32[8,128]{1,0:T(8,128)} %get-tuple-element.52.send_ids, ...), custom_call_target="tpu_custom_call" | custom-call | flops 603979776 | bytes 4718592 | tf_op jit(solution)/shard_map/pallas_call | solution.py:252
  81.8 1.6 collective-permute-start.17
  83.4 1.5 collective-permute-start.18
  85.4 5.2 %shard_map.58 = (bf16[768,256]{1,0:T(8,128)(2,1)}, bf16[768,512]{1,0:T(8,128)(2,1)}, bf16[128,512]{1,0:T(8,128)(2,1)}, bf16[256,512]{1,0:T(8,128)(2,1)}, bf16[25...) custom-call(s32[2]{0:T(128)} %pad_add_fusion.place, s32[8,128]{1,0:T(8,128)} %get-tuple-element.52.send_ids, ...), custom_call_target="tpu_custom_call" | custom-call | flops 603979776 | bytes 4718592 | tf_op jit(solution)/shard_map/pallas_call | solution.py:252
  91.3 5.2 %collective-permute-done.18.refs_2_ = bf16[256,512]{1,0:T(8,128)(2,1)S(1)} collective-permute-done((bf16[256,512]{1,0:T(8,128)(2,1)}, bf16[256,512]{1,0:T(8,128)(2,1)S(1)}, u32[]{:S(2)}, u32[]{:S(2)}) %collective-permute-start.18) | collective-permute-done | bytes 262176 | tf_op jit(solution)/shard_map/ppermute | solution.py:30
  96.7 1.3 collective-permute-start.25
  98.8 1.4 collective-permute-start.27
  101.1 7.5 %shard_map.59.refs_0_ = bf16[768,256]{1,0:T(8,128)(2,1)} custom-call(s32[2]{0:T(128)} %pad_add_fusion.place, s32[1,108]{1,0:T(1,128)} %get-tuple-element.53.lists, s32[96]{0:T(128)} %counts.3, bf16[768,256]{1,0:T(8,128)(2,1)} %get-tuple-element.68.query_all, bf16[768,512]{1,0:T(8,128)(2,1)} %get-tuple-element.69.key_values, bf16[512,512]{1,0:T(8,128)(2,1)} %copy-done.24, ...), custom_call_target="tpu_custom_call" | custom-call | flops 905969664 | bytes 3932160 | tf_op jit(solution)/shard_map/pallas_call | solution.py:335
  108.7 3.6 %collective-permute-done.27.refs_3_ = bf16[256,512]{1,0:T(8,128)(2,1)S(1)} collective-permute-done((bf16[256,512]{1,0:T(8,128)(2,1)S(1)}, bf16[256,512]{1,0:T(8,128)(2,1)S(1)}, u32[]{:S(2)}, u32[]{:S(2)}) %collective-permute-start.27) | collective-permute-done | bytes 262176 | tf_op jit(solution)/shard_map/ppermute | solution.py:30
  113.3 1.3 collective-permute-start.21
  114.6 1.3 collective-permute-start.23
  116.0 7.4 %shard_map.60.refs_5_ = bf16[768,256]{1,0:T(8,128)(2,1)} custom-call(s32[2]{0:T(128)} %pad_add_fusion.place, s32[1,108]{1,0:T(1,128)} %get-tuple-element.53.lists, s32[96]{0:T(128)} %counts.3, bf16[768,256]{1,0:T(8,128)(2,1)} %get-tuple-element.83.query_all, bf16[768,512]{1,0:T(8,128)(2,1)} %get-tuple-element.84.key_values, ...), custom_call_target="tpu_custom_call" | custom-call | flops 905969664 | bytes 3932160 | tf_op jit(solution)/shard_map/pallas_call | solution.py:335
  123.4 4.6 %collective-permute-start.29 = (bf16[768,256]{1,0:T(8,128)(2,1)}, bf16[768,256]{1,0:T(8,128)(2,1)S(1)}, u32[]{:S(2)}, u32[]{:S(2)}) collective-permute-start(bf16[768,256]{1,0:T(8,128)(2,1)} %shard_map.60.refs_5_), channel_id=1, source_target_pairs={{0,1},{1,2},{2,3},{4,5},{5,6},{6,7},{8,9},{9,10},{10,11},{12,13},{... | collective-permute-start | bytes 1179656 | tf_op jit(solution)/shard_map/ppermute | solution.py:24
  128.0 1.3 collective-permute-start.31
  129.3 5.3 %collective-permute-start.22 = (bf16[768,256]{1,0:T(8,128)(2,1)S(1)}, bf16[768,256]{1,0:T(8,128)(2,1)}, u32[]{:S(2)}, u32[]{:S(2)}) collective-permute-start(bf16[768,256]{1,0:T(8,128)(2,1)S(1)} %collective-permute-done.21.refs_1_), channel_id=1, source_target_pairs={{0,1},{1,2},{2,3},{4,5},{5,6},{6,7},{8,9},{9,10},{10,11},{12,13},{... | collective-permute-start | bytes 1179656 | tf_op jit(solution)/shard_map/ppermute | solution.py:24
  134.6 1.3 collective-permute-start.24
  135.9 1.9 %collective-permute-done.29.refs_6_ = bf16[768,256]{1,0:T(8,128)(2,1)S(1)} collective-permute-done((bf16[768,256]{1,0:T(8,128)(2,1)}, bf16[768,256]{1,0:T(8,128)(2,1)S(1)}, u32[]{:S(2)}, u32[]{:S(2)}) %collective-permute-start.29) | collective-permute-done | bytes 393248 | tf_op jit(solution)/shard_map/ppermute | solution.py:24
  137.8 5.1 %collective-permute-start.30 = (bf16[768,256]{1,0:T(8,128)(2,1)S(1)}, bf16[768,256]{1,0:T(8,128)(2,1)}, u32[]{:S(2)}, u32[]{:S(2)}) collective-permute-start(bf16[768,256]{1,0:T(8,128)(2,1)S(1)} %collective-permute-done.29.refs_6_), channel_id=1, source_target_pairs={{0,1},{1,2},{2,3},{4,5},{5,6},{6,7},{8,9},{9,10},{10,11},{12,13},{... | collective-permute-start | bytes 1179656 | tf_op jit(solution)/shard_map/ppermute | solution.py:24
  142.8 1.3 collective-permute-start.32
  144.1 2.0 %collective-permute-done.22.refs_2_ = bf16[768,256]{1,0:T(8,128)(2,1)} collective-permute-done((bf16[768,256]{1,0:T(8,128)(2,1)S(1)}, bf16[768,256]{1,0:T(8,128)(2,1)}, u32[]{:S(2)}, u32[]{:S(2)}) %collective-permute-start.22) | collective-permute-done | bytes 393248 | tf_op jit(solution)/shard_map/ppermute | solution.py:24
  146.1 5.2 %collective-permute-start.34 = (bf16[768,256]{1,0:T(8,128)(2,1)}, bf16[768,256]{1,0:T(8,128)(2,1)}, u32[]{:S(2)}, u32[]{:S(2)}) collective-permute-start(bf16[768,256]{1,0:T(8,128)(2,1)} %collective-permute-done.22.refs_2_), channel_id=1, source_target_pairs={{0,1},{1,2},{2,3},{4,5},{5,6},{6,7},{8,9},{9,10},{10,11},{12,13},{... | collective-permute-start | bytes 1179656 | tf_op jit(solution)/shard_map/ppermute | solution.py:24
  151.3 1.3 collective-permute-start.35
  152.6 1.9 %collective-permute-done.30.refs_7_ = bf16[768,256]{1,0:T(8,128)(2,1)} collective-permute-done((bf16[768,256]{1,0:T(8,128)(2,1)S(1)}, bf16[768,256]{1,0:T(8,128)(2,1)}, u32[]{:S(2)}, u32[]{:S(2)}) %collective-permute-start.30) | collective-permute-done | bytes 393248 | tf_op jit(solution)/shard_map/ppermute | solution.py:24
  154.5 5.2 %collective-permute-start.36 = (bf16[768,256]{1,0:T(8,128)(2,1)}, bf16[768,256]{1,0:T(8,128)(2,1)}, u32[]{:S(2)}, u32[]{:S(2)}) collective-permute-start(bf16[768,256]{1,0:T(8,128)(2,1)} %collective-permute-done.30.refs_7_), channel_id=1, source_target_pairs={{0,1},{1,2},{2,3},{4,5},{5,6},{6,7},{8,9},{9,10},{10,11},{12,13},{... | collective-permute-start | bytes 1179656 | tf_op jit(solution)/shard_map/ppermute | solution.py:24
  159.8 1.3 collective-permute-start.37
  162.1 6.1 %shard_map.61 = (f32[768,512]{1,0:T(8,128)}, bf16[512,512]{1,0:T(8,128)(2,1)}) custom-call(s32[2]{0:T(128)} %pad_add_fusion.place, bf16[768,256]{1,0:T(8,128)(2,1)} %shard_map.59.refs_0_, bf16[768,256]{1,0:T(8,128)(2,1)} %copy-done.6, bf16[768,256]{1,0:T(8,128)(2,1)} %collective-permute-done.22.refs_2_, bf16[768,256]{1,0:T(8,128)(2,1)} %copy-done.7, ...), custom_call_target="tpu_custom_call" | custom-call | flops 1610612736 | bytes 5242880 | tf_op jit(solution)/shard_map/pallas_call | solution.py:140
  168.3 2.1 %collective-permute-done.36.refs_3_ = bf16[768,256]{1,0:T(8,128)(2,1)} collective-permute-done((bf16[768,256]{1,0:T(8,128)(2,1)}, bf16[768,256]{1,0:T(8,128)(2,1)}, u32[]{:S(2)}, u32[]{:S(2)}) %collective-permute-start.36) | collective-permute-done | bytes 393248 | tf_op jit(solution)/shard_map/ppermute | solution.py:24
  170.3 4.1 %collective-permute-done.37.refs_4_ = bf16[768,256]{1,0:T(8,128)(2,1)} collective-permute-done((bf16[768,256]{1,0:T(8,128)(2,1)}, bf16[768,256]{1,0:T(8,128)(2,1)}, u32[]{:S(2)}, u32[]{:S(2)}) %collective-permute-start.37) | collective-permute-done | bytes 393248 | tf_op jit(solution)/shard_map/ppermute | solution.py:25
  174.5 4.1 %shard_map.62 = bf16[768,512]{1,0:T(8,128)(2,1)} custom-call(s32[2]{0:T(128)} %pad_add_fusion.place, s32[8,128]{1,0:T(8,128)} %get-tuple-element.52.send_ids, f32[768,512]{1,0:T(8,128)} %get-tuple-element.93.refs_0_, bf16[768,256]{1,0:T(8,128)(2,1)} %collective-permute-done.34.refs_1_, bf16[768,256]{1,0:T(8,128)(2,1)} %collective-permute-done.35.refs_2_, ...), custom_call_target="tpu_custom_call" | custom-call | flops 402653184 | bytes 3145728 | tf_op jit(solution)/shard_map/pallas_call | solution.py:252
  (116 shorter events, 14.9 us)
Async XLA Ops:
  0.0 55.2 %copy-start.3 = (bf16[256,512]{1,0:T(8,128)(2,1)S(1)}, bf16[256,512]{1,0:T(8,128)(2,1)}, u32[]{:S(2)}) copy-start(bf16[256,512]{1,0:T(8,128)(2,1)} %param.7) | copy-start | bytes 786436
  0.0 22.2 %collective-permute-start = (bf16[768,512]{1,0:T(8,128)(2,1)}, bf16[768,512]{1,0:T(8,128)(2,1)S(1)}, u32[]{:S(2)}, u32[]{:S(2)}) collective-permute-start(bf16[768,512]{1,0:T(8,128)(2,1)} %refs_0_), channel_id=1, source_target_pairs={{0,1},{1,2},{2,3},{4,5},{5,6},{6,7},{8,9},{9,10},{10,11},{12,13},{... | collective-permute-start | bytes 2359304 | tf_op jit(solution)/shard_map/ppermute | solution.py:24
  5.1 21.1 %collective-permute-start.1 = (bf16[768,512]{1,0:T(8,128)(2,1)}, bf16[768,512]{1,0:T(8,128)(2,1)S(1)}, u32[]{:S(2)}, u32[]{:S(2)}) collective-permute-start(bf16[768,512]{1,0:T(8,128)(2,1)} %refs_0_), channel_id=1, source_target_pairs={{1,0},{2,1},{3,2},{5,4},{6,5},{7,6},{9,8},{10,9},{11,10},{13,12},{... | collective-permute-start | bytes 2359304 | tf_op jit(solution)/shard_map/ppermute | solution.py:25
  6.4 26.1 %collective-permute-start.5 = (bf16[256,1536]{1,0:T(8,128)(2,1)}, bf16[256,1536]{1,0:T(8,128)(2,1)S(1)}, u32[]{:S(2)}, u32[]{:S(2)}) collective-permute-start(bf16[256,1536]{1,0:T(8,128)(2,1)} %refs_5_.1), channel_id=1, source_target_pairs={{0,8},{4,12},{8,0},{12,4},{16,24},{20,28},{24,16},{28,20},{1,9},{5... | collective-permute-start | bytes 2359304 | tf_op jit(solution)/shard_map/ppermute | solution.py:30
  8.0 24.6 %collective-permute-start.6 = (bf16[256,1536]{1,0:T(8,128)(2,1)}, bf16[256,1536]{1,0:T(8,128)(2,1)}, u32[]{:S(2)}, u32[]{:S(2)}) collective-permute-start(bf16[256,1536]{1,0:T(8,128)(2,1)} %refs_5_.1), channel_id=1, source_target_pairs={{0,16},{4,20},{8,24},{12,28},{16,0},{20,4},{24,8},{28,12},{1,17},{... | collective-permute-start | bytes 2359304 | tf_op jit(solution)/shard_map/ppermute | solution.py:30
  9.5 23.0 %collective-permute-start.4 = (bf16[256,512]{1,0:T(8,128)(2,1)}, bf16[256,512]{1,0:T(8,128)(2,1)S(1)}, u32[]{:S(2)}, u32[]{:S(2)}) collective-permute-start(bf16[256,512]{1,0:T(8,128)(2,1)} %param.7), channel_id=1, source_target_pairs={{0,16},{4,20},{8,24},{12,28},{16,0},{20,4},{24,8},{28,12},{1,17},{... | collective-permute-start | bytes 786440 | tf_op jit(solution)/shard_map/ppermute | solution.py:30
  22.2 28.3 %copy-start.20 = (bf16[768,512]{1,0:T(8,128)(2,1)}, bf16[768,512]{1,0:T(8,128)(2,1)S(1)}, u32[]{:S(2)}) copy-start(bf16[768,512]{1,0:T(8,128)(2,1)S(1)} %collective-permute-done.refs_1_) | copy-start | bytes 2359300
  26.2 26.9 %copy-start.21 = (bf16[768,512]{1,0:T(8,128)(2,1)}, bf16[768,512]{1,0:T(8,128)(2,1)S(1)}, u32[]{:S(2)}) copy-start(bf16[768,512]{1,0:T(8,128)(2,1)S(1)} %collective-permute-done.1.refs_3_) | copy-start | bytes 2359300
  26.2 19.1 %collective-permute-start.2 = (bf16[768,512]{1,0:T(8,128)(2,1)S(1)}, bf16[768,512]{1,0:T(8,128)(2,1)}, u32[]{:S(2)}, u32[]{:S(2)}) collective-permute-start(bf16[768,512]{1,0:T(8,128)(2,1)S(1)} %collective-permute-done.refs_1_), channel_id=1, source_target_pairs={{0,1},{1,2},{2,3},{4,5},{5,6},{6,7},{8,9},{9,10},{10,11},{12,13},{... | collective-permute-start | bytes 2359304 | tf_op jit(solution)/shard_map/ppermute | solution.py:24
  30.5 19.9 %collective-permute-start.3 = (bf16[768,512]{1,0:T(8,128)(2,1)S(1)}, bf16[768,512]{1,0:T(8,128)(2,1)}, u32[]{:S(2)}, u32[]{:S(2)}) collective-permute-start(bf16[768,512]{1,0:T(8,128)(2,1)S(1)} %collective-permute-done.1.refs_3_), channel_id=1, source_target_pairs={{1,0},{2,1},{3,2},{5,4},{6,5},{7,6},{9,8},{10,9},{11,10},{13,12},{... | collective-permute-start | bytes 2359304 | tf_op jit(solution)/shard_map/ppermute | solution.py:25
  32.5 25.2 %copy-start.11 = (bf16[256,1536]{1,0:T(8,128)(2,1)}, bf16[256,1536]{1,0:T(8,128)(2,1)S(1)}, u32[]{:S(2)}) copy-start(bf16[256,1536]{1,0:T(8,128)(2,1)S(1)} %collective-permute-done.5.refs_7_) | copy-start | bytes 2359300
  33.8 9.4 %collective-permute-start.7 = (bf16[128,1536]{1,0:T(8,128)(2,1)S(1)}, bf16[128,1536]{1,0:T(8,128)(2,1)S(1)}, u32[]{:S(2)}, u32[]{:S(2)}) collective-permute-start(bf16[128,1536]{1,0:T(8,128)(2,1)S(1)} %slice.24), channel_id=1, source_target_pairs={{0,8},{4,12},{8,0},{12,4},{16,24},{20,28},{24,16},{28,20},{1,9},{5... | collective-permute-start | bytes 1179656 | tf_op jit(solution)/shard_map/ppermute | solution.py:30
  34.8 9.3 %collective-permute-start.8 = (bf16[128,1536]{1,0:T(8,128)(2,1)S(1)}, bf16[128,1536]{1,0:T(8,128)(2,1)S(1)}, u32[]{:S(2)}, u32[]{:S(2)}) collective-permute-start(bf16[128,1536]{1,0:T(8,128)(2,1)S(1)} %slice.25), channel_id=1, source_target_pairs={{0,16},{4,20},{8,24},{12,28},{16,0},{20,4},{24,8},{28,12},{1,17},{... | collective-permute-start | bytes 1179656 | tf_op jit(solution)/shard_map/ppermute | solution.py:30
  44.0 11.2 %collective-permute-start.9 = (bf16[256,1536]{1,0:T(8,128)(2,1)}, bf16[256,1536]{1,0:T(8,128)(2,1)S(1)}, u32[]{:S(2)}, u32[]{:S(2)}) collective-permute-start(bf16[256,1536]{1,0:T(8,128)(2,1)} %refs_5_.1), channel_id=1, source_target_pairs={{0,4},{4,0},{8,12},{12,8},{16,20},{20,16},{24,28},{28,24},{1,5},{5... | collective-permute-start | bytes 2359304 | tf_op jit(solution)/shard_map/ppermute | solution.py:30
  44.0 12.8 %collective-permute-start.10 = (bf16[256,1536]{1,0:T(8,128)(2,1)S(1)}, bf16[256,1536]{1,0:T(8,128)(2,1)S(1)}, u32[]{:S(2)}, u32[]{:S(2)}) collective-permute-start(bf16[256,1536]{1,0:T(8,128)(2,1)S(1)} %collective-permute-done.5.refs_7_), channel_id=1, source_target_pairs={{0,4},{4,0},{8,12},{12,8},{16,20},{20,16},{24,28},{28,24},{1,5},{5... | collective-permute-start | bytes 2359304 | tf_op jit(solution)/shard_map/ppermute | solution.py:30
  44.5 13.2 %collective-permute-start.11 = (bf16[256,1536]{1,0:T(8,128)(2,1)}, bf16[256,1536]{1,0:T(8,128)(2,1)}, u32[]{:S(2)}, u32[]{:S(2)}) collective-permute-start(bf16[256,1536]{1,0:T(8,128)(2,1)} %collective-permute-done.6.refs_9_), channel_id=1, source_target_pairs={{0,4},{4,0},{8,12},{12,8},{16,20},{20,16},{24,28},{28,24},{1,5},{5... | collective-permute-start | bytes 2359304 | tf_op jit(solution)/shard_map/ppermute | solution.py:30
  45.4 5.1 %collective-permute-start.12 = (bf16[128,1536]{1,0:T(8,128)(2,1)S(1)}, bf16[128,1536]{1,0:T(8,128)(2,1)S(1)}, u32[]{:S(2)}, u32[]{:S(2)}) collective-permute-start(bf16[128,1536]{1,0:T(8,128)(2,1)S(1)} %collective-permute-done.7.refs_11_), channel_id=1, source_target_pairs={{0,4},{4,0},{8,12},{12,8},{16,20},{20,16},{24,28},{28,24},{1,5},{5... | collective-permute-start | bytes 1179656 | tf_op jit(solution)/shard_map/ppermute | solution.py:30
  50.4 2.7 %collective-permute-start.13 = (bf16[128,1536]{1,0:T(8,128)(2,1)S(1)}, bf16[128,1536]{1,0:T(8,128)(2,1)S(1)}, u32[]{:S(2)}, u32[]{:S(2)}) collective-permute-start(bf16[128,1536]{1,0:T(8,128)(2,1)S(1)} %collective-permute-done.8.refs_12_), channel_id=1, source_target_pairs={{0,4},{4,0},{8,12},{12,8},{16,20},{20,16},{24,28},{28,24},{1,5},{5... | collective-permute-start | bytes 1179656 | tf_op jit(solution)/shard_map/ppermute | solution.py:30
  50.5 20.4 %collective-permute-start.15 = (bf16[768,512]{1,0:T(8,128)(2,1)}, bf16[768,512]{1,0:T(8,128)(2,1)S(1)}, u32[]{:S(2)}, u32[]{:S(2)}) collective-permute-start(bf16[768,512]{1,0:T(8,128)(2,1)} %collective-permute-done.2.refs_2_), channel_id=1, source_target_pairs={{0,1},{1,2},{2,3},{4,5},{5,6},{6,7},{8,9},{9,10},{10,11},{12,13},{... | collective-permute-start | bytes 2359304 | tf_op jit(solution)/shard_map/ppermute | solution.py:24
  53.9 21.7 %collective-permute-start.16 = (bf16[768,512]{1,0:T(8,128)(2,1)}, bf16[768,512]{1,0:T(8,128)(2,1)S(1)}, u32[]{:S(2)}, u32[]{:S(2)}) collective-permute-start(bf16[768,512]{1,0:T(8,128)(2,1)} %collective-permute-done.3.refs_4_), channel_id=1, source_target_pairs={{1,0},{2,1},{3,2},{5,4},{6,5},{7,6},{9,8},{10,9},{11,10},{13,12},{... | collective-permute-start | bytes 2359304 | tf_op jit(solution)/shard_map/ppermute | solution.py:25
  55.3 14.1 %collective-permute-start.14 = (bf16[512,512]{1,0:T(8,128)(2,1)S(1)}, bf16[512,512]{1,0:T(8,128)(2,1)S(1)}, u32[]{:S(2)}, u32[]{:S(2)}) collective-permute-start(bf16[512,512]{1,0:T(8,128)(2,1)S(1)} %pad_maximum_fusion), channel_id=1, source_target_pairs={{0,8},{4,12},{8,0},{12,4},{16,24},{20,28},{24,16},{28,20},{1,9},{5... | collective-permute-start | bytes 1572872 | tf_op jit(solution)/shard_map/ppermute | solution.py:30
  81.8 9.5 %collective-permute-start.17 = (bf16[256,512]{1,0:T(8,128)(2,1)}, bf16[256,512]{1,0:T(8,128)(2,1)S(1)}, u32[]{:S(2)}, u32[]{:S(2)}) collective-permute-start(bf16[256,512]{1,0:T(8,128)(2,1)} %get-tuple-element.71), channel_id=1, source_target_pairs={{0,8},{4,12},{8,0},{12,4},{16,24},{20,28},{24,16},{28,20},{1,9},{5... | collective-permute-start | bytes 786440 | tf_op jit(solution)/shard_map/ppermute | solution.py:30
  83.4 13.1 %collective-permute-start.18 = (bf16[256,512]{1,0:T(8,128)(2,1)}, bf16[256,512]{1,0:T(8,128)(2,1)S(1)}, u32[]{:S(2)}, u32[]{:S(2)}) collective-permute-start(bf16[256,512]{1,0:T(8,128)(2,1)} %get-tuple-element.72), channel_id=1, source_target_pairs={{0,16},{4,20},{8,24},{12,28},{16,0},{20,4},{24,8},{28,12},{1,17},{... | collective-permute-start | bytes 786440 | tf_op jit(solution)/shard_map/ppermute | solution.py:30
  84.9 11.7 %copy-start.13 = (bf16[128,512]{1,0:T(8,128)(2,1)S(1)}, bf16[128,512]{1,0:T(8,128)(2,1)}, u32[]{:S(2)}) copy-start(bf16[128,512]{1,0:T(8,128)(2,1)} %get-tuple-element.70) | copy-start | bytes 393220
  84.9 11.6 %collective-permute-start.19 = (bf16[256,512]{1,0:T(8,128)(2,1)}, bf16[256,512]{1,0:T(8,128)(2,1)S(1)}, u32[]{:S(2)}, u32[]{:S(2)}) collective-permute-start(bf16[256,512]{1,0:T(8,128)(2,1)} %get-tuple-element.73), channel_id=1, source_target_pairs={{0,24},{4,28},{8,16},{12,20},{16,8},{20,12},{24,0},{28,4},{1,25},{... | collective-permute-start | bytes 786440 | tf_op jit(solution)/shard_map/ppermute | solution.py:30
  96.6 3.6 %collective-permute-start.20 = (bf16[512,512]{1,0:T(8,128)(2,1)S(1)}, bf16[512,512]{1,0:T(8,128)(2,1)S(1)}, u32[]{:S(2)}, u32[]{:S(2)}) collective-permute-start(bf16[512,512]{1,0:T(8,128)(2,1)S(1)} %pad_maximum_fusion.1), channel_id=1, source_target_pairs={{0,4},{4,0},{8,12},{12,8},{16,20},{20,16},{24,28},{28,24},{1,5},{5... | collective-permute-start | bytes 1572872 | tf_op jit(solution)/shard_map/ppermute | solution.py:30
  96.7 11.9 %collective-permute-start.25 = (bf16[256,512]{1,0:T(8,128)(2,1)}, bf16[256,512]{1,0:T(8,128)(2,1)S(1)}, u32[]{:S(2)}, u32[]{:S(2)}) collective-permute-start(bf16[256,512]{1,0:T(8,128)(2,1)} %get-tuple-element.86), channel_id=1, source_target_pairs={{0,8},{4,12},{8,0},{12,4},{16,24},{20,28},{24,16},{28,20},{1,9},{5... | collective-permute-start | bytes 786440 | tf_op jit(solution)/shard_map/ppermute | solution.py:30
  98.0 10.6 %collective-permute-start.26 = (bf16[256,512]{1,0:T(8,128)(2,1)S(1)}, bf16[256,512]{1,0:T(8,128)(2,1)S(1)}, u32[]{:S(2)}, u32[]{:S(2)}) collective-permute-start(bf16[256,512]{1,0:T(8,128)(2,1)S(1)} %copy-done.30), channel_id=1, source_target_pairs={{0,16},{4,20},{8,24},{12,28},{16,0},{20,4},{24,8},{28,12},{1,17},{... | collective-permute-start | bytes 786440 | tf_op jit(solution)/shard_map/ppermute | solution.py:30
  98.8 13.4 %collective-permute-start.27 = (bf16[256,512]{1,0:T(8,128)(2,1)S(1)}, bf16[256,512]{1,0:T(8,128)(2,1)S(1)}, u32[]{:S(2)}, u32[]{:S(2)}) collective-permute-start(bf16[256,512]{1,0:T(8,128)(2,1)S(1)} %copy-done.29), channel_id=1, source_target_pairs={{0,24},{4,28},{8,16},{12,20},{16,8},{20,12},{24,0},{28,4},{1,25},{... | collective-permute-start | bytes 786440 | tf_op jit(solution)/shard_map/ppermute | solution.py:30
  101.1 11.2 %copy-start.12 = (bf16[128,512]{1,0:T(8,128)(2,1)S(1)}, bf16[128,512]{1,0:T(8,128)(2,1)}, u32[]{:S(2)}) copy-start(bf16[128,512]{1,0:T(8,128)(2,1)} %get-tuple-element.85) | copy-start | bytes 393220
  112.3 3.6 %collective-permute-start.28 = (bf16[512,512]{1,0:T(8,128)(2,1)S(1)}, bf16[512,512]{1,0:T(8,128)(2,1)}, u32[]{:S(2)}, u32[]{:S(2)}) collective-permute-start(bf16[512,512]{1,0:T(8,128)(2,1)S(1)} %pad_maximum_fusion.2), channel_id=1, source_target_pairs={{0,4},{4,0},{8,12},{12,8},{16,20},{20,16},{24,28},{28,24},{1,5},{5... | collective-permute-start | bytes 1572872 | tf_op jit(solution)/shard_map/ppermute | solution.py:30
  112.9 48.1 %collective-permute-start.33 = (bf16[1024,512]{1,0:T(8,128)(2,1)S(1)}, bf16[1024,512]{1,0:T(8,128)(2,1)S(1)}, u32[]{:S(2)}, u32[]{:S(2)}) collective-permute-start(bf16[1024,512]{1,0:T(8,128)(2,1)S(1)} %constant_dynamic-update-slice_fusion.refs_10_), channel_id=1, source_target_pairs={{0,4},{4,0},{8,12},{12,8},{16,20},{20,16},{24,28},{28,24},{1,5},{5... | collective-permute-start | bytes 3145736 | tf_op jit(solution)/shard_map/ppermute | solution.py:30
  113.3 15.9 %collective-permute-start.21 = (bf16[768,256]{1,0:T(8,128)(2,1)S(1)}, bf16[768,256]{1,0:T(8,128)(2,1)S(1)}, u32[]{:S(2)}, u32[]{:S(2)}) collective-permute-start(bf16[768,256]{1,0:T(8,128)(2,1)S(1)} %copy-done.5), channel_id=1, source_target_pairs={{0,1},{1,2},{2,3},{4,5},{5,6},{6,7},{8,9},{9,10},{10,11},{12,13},{... | collective-permute-start | bytes 1179656 | tf_op jit(solution)/shard_map/ppermute | solution.py:24
  114.6 20.0 %collective-permute-start.23 = (bf16[768,256]{1,0:T(8,128)(2,1)S(1)}, bf16[768,256]{1,0:T(8,128)(2,1)S(1)}, u32[]{:S(2)}, u32[]{:S(2)}) collective-permute-start(bf16[768,256]{1,0:T(8,128)(2,1)S(1)} %copy-done.5), channel_id=1, source_target_pairs={{1,0},{2,1},{3,2},{5,4},{6,5},{7,6},{9,8},{10,9},{11,10},{13,12},{... | collective-permute-start | bytes 1179656 | tf_op jit(solution)/shard_map/ppermute | solution.py:25
  123.4 14.4 %collective-permute-start.29 = (bf16[768,256]{1,0:T(8,128)(2,1)}, bf16[768,256]{1,0:T(8,128)(2,1)S(1)}, u32[]{:S(2)}, u32[]{:S(2)}) collective-permute-start(bf16[768,256]{1,0:T(8,128)(2,1)} %shard_map.60.refs_5_), channel_id=1, source_target_pairs={{0,1},{1,2},{2,3},{4,5},{5,6},{6,7},{8,9},{9,10},{10,11},{12,13},{... | collective-permute-start | bytes 1179656 | tf_op jit(solution)/shard_map/ppermute | solution.py:24
  128.0 14.9 %collective-permute-start.31 = (bf16[768,256]{1,0:T(8,128)(2,1)}, bf16[768,256]{1,0:T(8,128)(2,1)S(1)}, u32[]{:S(2)}, u32[]{:S(2)}) collective-permute-start(bf16[768,256]{1,0:T(8,128)(2,1)} %shard_map.60.refs_5_), channel_id=1, source_target_pairs={{1,0},{2,1},{3,2},{5,4},{6,5},{7,6},{9,8},{10,9},{11,10},{13,12},{... | collective-permute-start | bytes 1179656 | tf_op jit(solution)/shard_map/ppermute | solution.py:25
  129.3 31.8 %copy-start.6 = (bf16[768,256]{1,0:T(8,128)(2,1)}, bf16[768,256]{1,0:T(8,128)(2,1)S(1)}, u32[]{:S(2)}) copy-start(bf16[768,256]{1,0:T(8,128)(2,1)S(1)} %collective-permute-done.21.refs_1_) | copy-start | bytes 1179652
  129.3 16.8 %collective-permute-start.22 = (bf16[768,256]{1,0:T(8,128)(2,1)S(1)}, bf16[768,256]{1,0:T(8,128)(2,1)}, u32[]{:S(2)}, u32[]{:S(2)}) collective-permute-start(bf16[768,256]{1,0:T(8,128)(2,1)S(1)} %collective-permute-done.21.refs_1_), channel_id=1, source_target_pairs={{0,1},{1,2},{2,3},{4,5},{5,6},{6,7},{8,9},{9,10},{10,11},{12,13},{... | collective-permute-start | bytes 1179656 | tf_op jit(solution)/shard_map/ppermute | solution.py:24
  134.6 26.5 %copy-start.7 = (bf16[768,256]{1,0:T(8,128)(2,1)}, bf16[768,256]{1,0:T(8,128)(2,1)S(1)}, u32[]{:S(2)}) copy-start(bf16[768,256]{1,0:T(8,128)(2,1)S(1)} %collective-permute-done.23.refs_3_) | copy-start | bytes 1179652
  134.6 16.7 %collective-permute-start.24 = (bf16[768,256]{1,0:T(8,128)(2,1)S(1)}, bf16[768,256]{1,0:T(8,128)(2,1)S(1)}, u32[]{:S(2)}, u32[]{:S(2)}) collective-permute-start(bf16[768,256]{1,0:T(8,128)(2,1)S(1)} %collective-permute-done.23.refs_3_), channel_id=1, source_target_pairs={{1,0},{2,1},{3,2},{5,4},{6,5},{7,6},{9,8},{10,9},{11,10},{13,12},{... | collective-permute-start | bytes 1179656 | tf_op jit(solution)/shard_map/ppermute | solution.py:25
  137.8 23.3 %copy-start.8 = (bf16[768,256]{1,0:T(8,128)(2,1)}, bf16[768,256]{1,0:T(8,128)(2,1)S(1)}, u32[]{:S(2)}) copy-start(bf16[768,256]{1,0:T(8,128)(2,1)S(1)} %collective-permute-done.29.refs_6_) | copy-start | bytes 1179652
  137.8 16.7 %collective-permute-start.30 = (bf16[768,256]{1,0:T(8,128)(2,1)S(1)}, bf16[768,256]{1,0:T(8,128)(2,1)}, u32[]{:S(2)}, u32[]{:S(2)}) collective-permute-start(bf16[768,256]{1,0:T(8,128)(2,1)S(1)} %collective-permute-done.29.refs_6_), channel_id=1, source_target_pairs={{0,1},{1,2},{2,3},{4,5},{5,6},{6,7},{8,9},{9,10},{10,11},{12,13},{... | collective-permute-start | bytes 1179656 | tf_op jit(solution)/shard_map/ppermute | solution.py:24
  142.8 18.3 %copy-start.9 = (bf16[768,256]{1,0:T(8,128)(2,1)}, bf16[768,256]{1,0:T(8,128)(2,1)S(1)}, u32[]{:S(2)}) copy-start(bf16[768,256]{1,0:T(8,128)(2,1)S(1)} %collective-permute-done.31.refs_8_) | copy-start | bytes 1179652
  142.8 16.9 %collective-permute-start.32 = (bf16[768,256]{1,0:T(8,128)(2,1)S(1)}, bf16[768,256]{1,0:T(8,128)(2,1)}, u32[]{:S(2)}, u32[]{:S(2)}) collective-permute-start(bf16[768,256]{1,0:T(8,128)(2,1)S(1)} %collective-permute-done.31.refs_8_), channel_id=1, source_target_pairs={{1,0},{2,1},{3,2},{5,4},{6,5},{7,6},{9,8},{10,9},{11,10},{13,12},{... | collective-permute-start | bytes 1179656 | tf_op jit(solution)/shard_map/ppermute | solution.py:25
  146.1 22.2 %collective-permute-start.34 = (bf16[768,256]{1,0:T(8,128)(2,1)}, bf16[768,256]{1,0:T(8,128)(2,1)}, u32[]{:S(2)}, u32[]{:S(2)}) collective-permute-start(bf16[768,256]{1,0:T(8,128)(2,1)} %collective-permute-done.22.refs_2_), channel_id=1, source_target_pairs={{0,1},{1,2},{2,3},{4,5},{5,6},{6,7},{8,9},{9,10},{10,11},{12,13},{... | collective-permute-start | bytes 1179656 | tf_op jit(solution)/shard_map/ppermute | solution.py:24
  151.3 16.9 %collective-permute-start.35 = (bf16[768,256]{1,0:T(8,128)(2,1)S(1)}, bf16[768,256]{1,0:T(8,128)(2,1)}, u32[]{:S(2)}, u32[]{:S(2)}) collective-permute-start(bf16[768,256]{1,0:T(8,128)(2,1)S(1)} %collective-permute-done.24.refs_4_), channel_id=1, source_target_pairs={{1,0},{2,1},{3,2},{5,4},{6,5},{7,6},{9,8},{10,9},{11,10},{13,12},{... | collective-permute-start | bytes 1179656 | tf_op jit(solution)/shard_map/ppermute | solution.py:25
  154.5 15.8 %collective-permute-start.36 = (bf16[768,256]{1,0:T(8,128)(2,1)}, bf16[768,256]{1,0:T(8,128)(2,1)}, u32[]{:S(2)}, u32[]{:S(2)}) collective-permute-start(bf16[768,256]{1,0:T(8,128)(2,1)} %collective-permute-done.30.refs_7_), channel_id=1, source_target_pairs={{0,1},{1,2},{2,3},{4,5},{5,6},{6,7},{8,9},{9,10},{10,11},{12,13},{... | collective-permute-start | bytes 1179656 | tf_op jit(solution)/shard_map/ppermute | solution.py:24
  159.8 14.7 %collective-permute-start.37 = (bf16[768,256]{1,0:T(8,128)(2,1)}, bf16[768,256]{1,0:T(8,128)(2,1)}, u32[]{:S(2)}, u32[]{:S(2)}) collective-permute-start(bf16[768,256]{1,0:T(8,128)(2,1)} %collective-permute-done.32.refs_9_), channel_id=1, source_target_pairs={{1,0},{2,1},{3,2},{5,4},{6,5},{7,6},{9,8},{10,9},{11,10},{13,12},{... | collective-permute-start | bytes 1179656 | tf_op jit(solution)/shard_map/ppermute | solution.py:25
  (21 other events, 94.4 us)

commit v4 on v3

--- a/solution.py
+++ b/solution.py
@@ -405,16 +405,11 @@
     part = line_step((tokens, [], []), "hid", hid_size)
     for s in near:
         pieces[s] = [swap(weight, s, "tok", tok_size)]
-    part, (send_ids, pool_at) = lax.optimization_barrier(
-        (part, routes(place, neighbours, counts, tok_size, blocks))
-    )
+    send_ids, pool_at = routes(place, neighbours, counts, tok_size, blocks)
     bits = [1 << i for i in reversed(range(tok_size.bit_length() - 1))]
     out_rows, out_ids = out_weight, [0]
     for bit in bits[:-2]:
         came = swap(out_rows, bit, "tok", tok_size)
-        came, held = lax.optimization_barrier((came, [pieces[s] for s in near]))
-        for s, piece in zip(near, held):
-            pieces[s] = piece
         out_rows, out_ids = jnp.concatenate([out_rows, came], axis=0), out_ids + [s ^ bit for s in out_ids]
     came = swap(out_rows, 2, "tok", tok_size)
     for _ in range(far - 1):
@@ -422,9 +417,8 @@
     for s in even:
         if pieces[s] is None:
             pieces[s] = forward(pieces, s, "tok", tok_size)
-    held = lax.optimization_barrier([pieces[s] for s in even])
-    for s, piece in zip(even, held):
-        pieces[s + 1] = [swap(x, 1, "tok", tok_size) for x in piece]
+    for s in even:
+        pieces[s + 1] = [swap(x, 1, "tok", tok_size) for x in pieces[s]]
     parts = [part]
 
     stacks, layout = [], []
@@ -432,7 +426,7 @@
         layout.append([(len(stacks) + i, 0, x.shape[0]) for i, x in enumerate(piece)])
         stacks += piece
     total, last_rows = accumulate(place, parts, stacks, layout, [far - 1], hid_size)
-    total, came = lax.optimization_barrier((total, came))
+    total, came, send_ids, pool_at = lax.optimization_barrier((total, came, send_ids, pool_at))
     out_rows, out_ids = jnp.concatenate([out_rows, came], axis=0), out_ids + [s ^ 2 for s in out_ids]
     came = swap(out_rows, 1, "tok", tok_size)
     lasts = [(from_left[-1], from_right[-1]) for _, from_left, from_right in parts]

time: 180 us -> 168 us (0.933)
  waiting for transfers between devices: 55.5 us -> 43 us
  starting transfers between devices: 65.9 us -> 68.9 us
    ppermute x9, waiting for transfers between devices: 18.1 us -> 7.81 us  [line_step(): right = lax.ppermute((from_right or [own])[-1], axis, to_left)]
    ppermute x9, waiting for transfers between devices: 18.6 us -> 10 us  [line_step(): left = lax.ppermute((from_left or [own])[-1], axis, to_right)]
    ppermute x20, waiting for transfers between devices: 18.8 us -> 25.1 us  [swap(): return lax.ppermute(x, axis, [(i, i ^ s) for i in range(size)])]
    ppermute x20, starting transfers between devices: 15.6 us -> 17.4 us  [swap(): return lax.ppermute(x, axis, [(i, i ^ s) for i in range(size)])]
    unnamed x64 -> x60, local copies, waits for them, and re-layouts: 5.08 us -> 3.6 us
  transfers between devices with their start and end apart: 38 -> 38, of which waited for: 18 -> 13; matrix products, arithmetic and copies ran while one was open for 2% -> 2% of each run, Pallas kernels for 22% -> 23%
where the time goes in v4:
time: 168 us; the launch traced here: 167 us
  starting transfers between devices  68.9 us (41%)
  Pallas kernels  47.6 us (28%)
  waiting for transfers between devices  43 us (26%)
  local copies, waits for them, and re-layouts  6.52 us (4%)
    ppermute x9, starting transfers between devices, line_step(): left = lax.ppermute((from_left or [own])[-1], axis, to_right)  39.9 us
    ppermute x20, waiting for transfers between devices, swap(): return lax.ppermute(x, axis, [(i, i ^ s) for i in range(size)])  25.1 us
    ppermute x20, starting transfers between devices, swap(): return lax.ppermute(x, axis, [(i, i ^ s) for i in range(size)])  17.4 us
    pallas_call x2, Pallas kernels, accumulate(): pl.pallas_call(functools.partial(accumulate_kernel, reach=reach, hid_size...  16.9 us
    pallas_call x2, Pallas kernels, attend(): pl.pallas_call(functools.partial(attend_kernel, tok_size=tok_size, heads=...  14.9 us
    pallas_call x3, Pallas kernels, finish(): pl.pallas_call(functools.partial(finish_kernel, deferred=deferred, hid_si...  14.4 us
    ppermute x9, starting transfers between devices, line_step(): right = lax.ppermute((from_right or [own])[-1], axis, to_left)  11.6 us
    ppermute x9, waiting for transfers between devices, line_step(): left = lax.ppermute((from_left or [own])[-1], axis, to_right)  10 us
  transfers between devices with their start and end apart: 38, of which 13 were waited for; matrix products, arithmetic and copies ran while one was open for 2% of the time, Pallas kernels for 23%

profile of v4, /device:TPU:0, one launch (start us, length us, event | category | flops | bytes accessed | tf_op | source)
XLA Modules:
  0.0 167.3 jit_solution(3051829636395964653)
XLA Ops:
  0.0 3.0 %collective-permute-start.7 = (bf16[256,1536]{1,0:T(8,128)(2,1)}, bf16[256,1536]{1,0:T(8,128)(2,1)}, u32[]{:S(2)}, u32[]{:S(2)}) collective-permute-start(bf16[256,1536]{1,0:T(8,128)(2,1)} %refs_5_.1), channel_id=1, source_target_pairs={{0,16},{4,20},{8,24},{12,28},{16,0},{20,4},{24,8},{28,12},{1,17},{... | collective-permute-start | bytes 2359304 | tf_op jit(solution)/shard_map/ppermute | solution.py:30
  3.0 1.5 collective-permute-start.5
  4.5 3.5 %collective-permute-start = (bf16[768,512]{1,0:T(8,128)(2,1)}, bf16[768,512]{1,0:T(8,128)(2,1)S(1)}, u32[]{:S(2)}, u32[]{:S(2)}) collective-permute-start(bf16[768,512]{1,0:T(8,128)(2,1)} %refs_0_.1), channel_id=1, source_target_pairs={{0,1},{1,2},{2,3},{4,5},{5,6},{6,7},{8,9},{9,10},{10,11},{12,13},{... | collective-permute-start | bytes 2359304 | tf_op jit(solution)/shard_map/ppermute | solution.py:24
  8.1 1.3 collective-permute-start.2
  9.4 11.5 %collective-permute-done.7.refs_9_ = bf16[256,1536]{1,0:T(8,128)(2,1)} collective-permute-done((bf16[256,1536]{1,0:T(8,128)(2,1)}, bf16[256,1536]{1,0:T(8,128)(2,1)}, u32[]{:S(2)}, u32[]{:S(2)}) %collective-permute-start.7) | collective-permute-done | bytes 786464 | tf_op jit(solution)/shard_map/ppermute | solution.py:30
  20.9 1.7 %collective-permute-start.13 = (bf16[256,512]{1,0:T(8,128)(2,1)}, bf16[256,512]{1,0:T(8,128)(2,1)S(1)}, u32[]{:S(2)}, u32[]{:S(2)}) collective-permute-start(bf16[256,512]{1,0:T(8,128)(2,1)} %param.7), channel_id=1, source_target_pairs={{0,16},{4,20},{8,24},{12,28},{16,0},{20,4},{24,8},{28,12},{1,17},{... | collective-permute-start | bytes 786440 | tf_op jit(solution)/shard_map/ppermute | solution.py:30
  22.6 1.0 slice.32
  23.7 1.6 collective-permute-start.9
  25.2 4.5 %collective-permute-start.1 = (bf16[768,512]{1,0:T(8,128)(2,1)S(1)}, bf16[768,512]{1,0:T(8,128)(2,1)}, u32[]{:S(2)}, u32[]{:S(2)}) collective-permute-start(bf16[768,512]{1,0:T(8,128)(2,1)S(1)} %collective-permute-done.refs_1_), channel_id=1, source_target_pairs={{0,1},{1,2},{2,3},{4,5},{5,6},{6,7},{8,9},{9,10},{10,11},{12,13},{... | collective-permute-start | bytes 2359304 | tf_op jit(solution)/shard_map/ppermute | solution.py:24
  29.7 1.3 collective-permute-start.3
  31.0 1.0 slice.33
  34.0 7.3 %collective-permute-done.10.refs_12_ = bf16[128,1536]{1,0:T(8,128)(2,1)} collective-permute-done((bf16[128,1536]{1,0:T(8,128)(2,1)S(1)}, bf16[128,1536]{1,0:T(8,128)(2,1)}, u32[]{:S(2)}, u32[]{:S(2)}) %collective-permute-start.10) | collective-permute-done | bytes 393248 | tf_op jit(solution)/shard_map/ppermute | solution.py:30
  41.8 2.3 %collective-permute-done.1.refs_2_ = bf16[768,512]{1,0:T(8,128)(2,1)} collective-permute-done((bf16[768,512]{1,0:T(8,128)(2,1)S(1)}, bf16[768,512]{1,0:T(8,128)(2,1)}, u32[]{:S(2)}, u32[]{:S(2)}) %collective-permute-start.1) | collective-permute-done | bytes 786464 | tf_op jit(solution)/shard_map/ppermute | solution.py:24
  44.1 4.5 %collective-permute-start.15 = (bf16[768,512]{1,0:T(8,128)(2,1)}, bf16[768,512]{1,0:T(8,128)(2,1)S(1)}, u32[]{:S(2)}, u32[]{:S(2)}) collective-permute-start(bf16[768,512]{1,0:T(8,128)(2,1)} %collective-permute-done.1.refs_2_), channel_id=1, source_target_pairs={{0,1},{1,2},{2,3},{4,5},{5,6},{6,7},{8,9},{9,10},{10,11},{12,13},{... | collective-permute-start | bytes 2359304 | tf_op jit(solution)/shard_map/ppermute | solution.py:24
  49.2 1.3 collective-permute-start.16
  52.6 1.4 shard_map.56
  54.0 10.7 %shard_map.55 = (f32[768,1536]{1,0:T(8,128)}, bf16[512,1536]{1,0:T(8,128)(2,1)}) custom-call(s32[2]{0:T(128)} %pad_add_fusion.place, bf16[768,512]{1,0:T(8,128)(2,1)} %refs_0_.1, bf16[768,512]{1,0:T(8,128)(2,1)} %copy-done.21, bf16[768,512]{1,0:T(8,128)(2,1)} %collective-permute-done.1.refs_2_, bf16[768,512]{1,0:T(8,128)(2,1)} %copy-done.22, ...), custom_call_target="tpu_custom_call" | custom-call | flops 4831838208 | bytes 9437184 | tf_op jit(solution)/shard_map/pallas_call | solution.py:140
  64.8 3.1 %collective-permute-done.16.refs_2_ = bf16[768,512]{1,0:T(8,128)(2,1)S(1)} collective-permute-done((bf16[768,512]{1,0:T(8,128)(2,1)}, bf16[768,512]{1,0:T(8,128)(2,1)S(1)}, u32[]{:S(2)}, u32[]{:S(2)}) %collective-permute-start.16) | collective-permute-done | bytes 786464 | tf_op jit(solution)/shard_map/ppermute | solution.py:25
  67.9 0.9 copy-done.1
  68.8 5.1 %shard_map.57 = (bf16[768,256]{1,0:T(8,128)(2,1)}, bf16[768,512]{1,0:T(8,128)(2,1)}, bf16[128,512]{1,0:T(8,128)(2,1)}, bf16[256,512]{1,0:T(8,128)(2,1)}, bf16[25...) custom-call(s32[2]{0:T(128)} %pad_add_fusion.place, s32[8,128]{1,0:T(8,128)} %get-tuple-element.42.send_ids, ...), custom_call_target="tpu_custom_call" | custom-call | flops 603979776 | bytes 4718592 | tf_op jit(solution)/shard_map/pallas_call | solution.py:252
  75.1 2.4 %collective-permute-start.19 = (bf16[256,512]{1,0:T(8,128)(2,1)}, bf16[256,512]{1,0:T(8,128)(2,1)S(1)}, u32[]{:S(2)}, u32[]{:S(2)}) collective-permute-start(bf16[256,512]{1,0:T(8,128)(2,1)} %get-tuple-element.51), channel_id=1, source_target_pairs={{0,24},{4,28},{8,16},{12,20},{16,8},{20,12},{24,0},{28,4},{1,25},{... | collective-permute-start | bytes 786440 | tf_op jit(solution)/shard_map/ppermute | solution.py:30
  77.5 5.2 %shard_map.58 = (bf16[768,256]{1,0:T(8,128)(2,1)}, bf16[768,512]{1,0:T(8,128)(2,1)}, bf16[128,512]{1,0:T(8,128)(2,1)}, bf16[256,512]{1,0:T(8,128)(2,1)}, bf16[25...) custom-call(s32[2]{0:T(128)} %pad_add_fusion.place, s32[8,128]{1,0:T(8,128)} %get-tuple-element.42.send_ids, ...), custom_call_target="tpu_custom_call" | custom-call | flops 603979776 | bytes 4718592 | tf_op jit(solution)/shard_map/pallas_call | solution.py:252
  82.8 1.8 %collective-permute-done.18.refs_2_ = bf16[256,512]{1,0:T(8,128)(2,1)S(1)} collective-permute-done((bf16[256,512]{1,0:T(8,128)(2,1)}, bf16[256,512]{1,0:T(8,128)(2,1)S(1)}, u32[]{:S(2)}, u32[]{:S(2)}) %collective-permute-start.18) | collective-permute-done | bytes 262176 | tf_op jit(solution)/shard_map/ppermute | solution.py:30
  84.8 1.6 collective-permute-start.25
  86.9 1.5 collective-permute-start.27
  89.1 7.5 %shard_map.59.refs_0_ = bf16[768,256]{1,0:T(8,128)(2,1)} custom-call(s32[2]{0:T(128)} %pad_add_fusion.place, s32[1,108]{1,0:T(1,128)} %get-tuple-element.43.lists, s32[96]{0:T(128)} %counts.3, bf16[768,256]{1,0:T(8,128)(2,1)} %get-tuple-element.46.query_all, bf16[768,512]{1,0:T(8,128)(2,1)} %get-tuple-element.47.key_values, bf16[512,512]{1,0:T(8,128)(2,1)} %copy-done.24, ...), custom_call_target="tpu_custom_call" | custom-call | flops 905969664 | bytes 3932160 | tf_op jit(solution)/shard_map/pallas_call | solution.py:335
  96.7 3.6 %collective-permute-done.26.refs_2_ = bf16[256,512]{1,0:T(8,128)(2,1)S(1)} collective-permute-done((bf16[256,512]{1,0:T(8,128)(2,1)S(1)}, bf16[256,512]{1,0:T(8,128)(2,1)S(1)}, u32[]{:S(2)}, u32[]{:S(2)}) %collective-permute-start.26) | collective-permute-done | bytes 262176 | tf_op jit(solution)/shard_map/ppermute | solution.py:30
  101.5 2.0 %collective-permute-start.21 = (bf16[768,256]{1,0:T(8,128)(2,1)S(1)}, bf16[768,256]{1,0:T(8,128)(2,1)S(1)}, u32[]{:S(2)}, u32[]{:S(2)}) collective-permute-start(bf16[768,256]{1,0:T(8,128)(2,1)S(1)} %copy-done.5), channel_id=1, source_target_pairs={{0,1},{1,2},{2,3},{4,5},{5,6},{6,7},{8,9},{9,10},{10,11},{12,13},{... | collective-permute-start | bytes 1179656 | tf_op jit(solution)/shard_map/ppermute | solution.py:24
  103.6 1.3 collective-permute-start.23
  104.9 7.4 %shard_map.60.refs_5_ = bf16[768,256]{1,0:T(8,128)(2,1)} custom-call(s32[2]{0:T(128)} %pad_add_fusion.place, s32[1,108]{1,0:T(1,128)} %get-tuple-element.43.lists, s32[96]{0:T(128)} %counts.3, bf16[768,256]{1,0:T(8,128)(2,1)} %get-tuple-element.61.query_all, bf16[768,512]{1,0:T(8,128)(2,1)} %get-tuple-element.62.key_values, ...), custom_call_target="tpu_custom_call" | custom-call | flops 905969664 | bytes 3932160 | tf_op jit(solution)/shard_map/pallas_call | solution.py:335
  112.3 4.6 %collective-permute-start.29 = (bf16[768,256]{1,0:T(8,128)(2,1)}, bf16[768,256]{1,0:T(8,128)(2,1)S(1)}, u32[]{:S(2)}, u32[]{:S(2)}) collective-permute-start(bf16[768,256]{1,0:T(8,128)(2,1)} %shard_map.60.refs_5_), channel_id=1, source_target_pairs={{0,1},{1,2},{2,3},{4,5},{5,6},{6,7},{8,9},{9,10},{10,11},{12,13},{... | collective-permute-start | bytes 1179656 | tf_op jit(solution)/shard_map/ppermute | solution.py:24
  116.9 1.3 collective-permute-start.31
  118.2 5.3 %collective-permute-start.22 = (bf16[768,256]{1,0:T(8,128)(2,1)S(1)}, bf16[768,256]{1,0:T(8,128)(2,1)}, u32[]{:S(2)}, u32[]{:S(2)}) collective-permute-start(bf16[768,256]{1,0:T(8,128)(2,1)S(1)} %collective-permute-done.21.refs_1_), channel_id=1, source_target_pairs={{0,1},{1,2},{2,3},{4,5},{5,6},{6,7},{8,9},{9,10},{10,11},{12,13},{... | collective-permute-start | bytes 1179656 | tf_op jit(solution)/shard_map/ppermute | solution.py:24
  123.5 1.3 collective-permute-start.24
  124.8 1.9 %collective-permute-done.29.refs_6_ = bf16[768,256]{1,0:T(8,128)(2,1)S(1)} collective-permute-done((bf16[768,256]{1,0:T(8,128)(2,1)}, bf16[768,256]{1,0:T(8,128)(2,1)S(1)}, u32[]{:S(2)}, u32[]{:S(2)}) %collective-permute-start.29) | collective-permute-done | bytes 393248 | tf_op jit(solution)/shard_map/ppermute | solution.py:24
  126.7 5.0 %collective-permute-start.30 = (bf16[768,256]{1,0:T(8,128)(2,1)S(1)}, bf16[768,256]{1,0:T(8,128)(2,1)}, u32[]{:S(2)}, u32[]{:S(2)}) collective-permute-start(bf16[768,256]{1,0:T(8,128)(2,1)S(1)} %collective-permute-done.29.refs_6_), channel_id=1, source_target_pairs={{0,1},{1,2},{2,3},{4,5},{5,6},{6,7},{8,9},{9,10},{10,11},{12,13},{... | collective-permute-start | bytes 1179656 | tf_op jit(solution)/shard_map/ppermute | solution.py:24
  131.7 1.3 collective-permute-start.32
  133.0 2.0 %collective-permute-done.22.refs_2_ = bf16[768,256]{1,0:T(8,128)(2,1)} collective-permute-done((bf16[768,256]{1,0:T(8,128)(2,1)S(1)}, bf16[768,256]{1,0:T(8,128)(2,1)}, u32[]{:S(2)}, u32[]{:S(2)}) %collective-permute-start.22) | collective-permute-done | bytes 393248 | tf_op jit(solution)/shard_map/ppermute | solution.py:24
  135.0 5.2 %collective-permute-start.34 = (bf16[768,256]{1,0:T(8,128)(2,1)}, bf16[768,256]{1,0:T(8,128)(2,1)}, u32[]{:S(2)}, u32[]{:S(2)}) collective-permute-start(bf16[768,256]{1,0:T(8,128)(2,1)} %collective-permute-done.22.refs_2_), channel_id=1, source_target_pairs={{0,1},{1,2},{2,3},{4,5},{5,6},{6,7},{8,9},{9,10},{10,11},{12,13},{... | collective-permute-start | bytes 1179656 | tf_op jit(solution)/shard_map/ppermute | solution.py:24
  140.3 1.3 collective-permute-start.35
  141.5 1.9 %collective-permute-done.30.refs_7_ = bf16[768,256]{1,0:T(8,128)(2,1)} collective-permute-done((bf16[768,256]{1,0:T(8,128)(2,1)S(1)}, bf16[768,256]{1,0:T(8,128)(2,1)}, u32[]{:S(2)}, u32[]{:S(2)}) %collective-permute-start.30) | collective-permute-done | bytes 393248 | tf_op jit(solution)/shard_map/ppermute | solution.py:24
  143.4 5.2 %collective-permute-start.36 = (bf16[768,256]{1,0:T(8,128)(2,1)}, bf16[768,256]{1,0:T(8,128)(2,1)}, u32[]{:S(2)}, u32[]{:S(2)}) collective-permute-start(bf16[768,256]{1,0:T(8,128)(2,1)} %collective-permute-done.30.refs_7_), channel_id=1, source_target_pairs={{0,1},{1,2},{2,3},{4,5},{5,6},{6,7},{8,9},{9,10},{10,11},{12,13},{... | collective-permute-start | bytes 1179656 | tf_op jit(solution)/shard_map/ppermute | solution.py:24
  148.7 1.3 collective-permute-start.37
  150.0 1.0 copy-done.4
  151.0 6.1 %shard_map.61 = (f32[768,512]{1,0:T(8,128)}, bf16[512,512]{1,0:T(8,128)(2,1)}) custom-call(s32[2]{0:T(128)} %pad_add_fusion.place, bf16[768,256]{1,0:T(8,128)(2,1)} %shard_map.59.refs_0_, bf16[768,256]{1,0:T(8,128)(2,1)} %copy-done.6, bf16[768,256]{1,0:T(8,128)(2,1)} %collective-permute-done.22.refs_2_, bf16[768,256]{1,0:T(8,128)(2,1)} %copy-done.7, ...), custom_call_target="tpu_custom_call" | custom-call | flops 1610612736 | bytes 5242880 | tf_op jit(solution)/shard_map/pallas_call | solution.py:140
  157.2 2.0 %collective-permute-done.36.refs_3_ = bf16[768,256]{1,0:T(8,128)(2,1)} collective-permute-done((bf16[768,256]{1,0:T(8,128)(2,1)}, bf16[768,256]{1,0:T(8,128)(2,1)}, u32[]{:S(2)}, u32[]{:S(2)}) %collective-permute-start.36) | collective-permute-done | bytes 393248 | tf_op jit(solution)/shard_map/ppermute | solution.py:24
  159.2 4.1 %collective-permute-done.37.refs_4_ = bf16[768,256]{1,0:T(8,128)(2,1)} collective-permute-done((bf16[768,256]{1,0:T(8,128)(2,1)}, bf16[768,256]{1,0:T(8,128)(2,1)}, u32[]{:S(2)}, u32[]{:S(2)}) %collective-permute-start.37) | collective-permute-done | bytes 393248 | tf_op jit(solution)/shard_map/ppermute | solution.py:25
  163.3 4.1 %shard_map.62 = bf16[768,512]{1,0:T(8,128)(2,1)} custom-call(s32[2]{0:T(128)} %pad_add_fusion.place, s32[8,128]{1,0:T(8,128)} %get-tuple-element.42.send_ids, f32[768,512]{1,0:T(8,128)} %get-tuple-element.71.refs_0_, bf16[768,256]{1,0:T(8,128)(2,1)} %collective-permute-done.34.refs_1_, bf16[768,256]{1,0:T(8,128)(2,1)} %collective-permute-done.35.refs_2_, ...), custom_call_target="tpu_custom_call" | custom-call | flops 402653184 | bytes 3145728 | tf_op jit(solution)/shard_map/pallas_call | solution.py:252
  (112 shorter events, 8.9 us)
Async XLA Ops:
  0.0 51.3 %copy-start.3 = (bf16[256,512]{1,0:T(8,128)(2,1)S(1)}, bf16[256,512]{1,0:T(8,128)(2,1)}, u32[]{:S(2)}) copy-start(bf16[256,512]{1,0:T(8,128)(2,1)} %param.7) | copy-start | bytes 786436
  0.0 50.5 %copy-start.19 = (s32[96,9]{0,1:T(8,128)S(1)}, s32[96,9]{0,1:T(8,128)}, u32[]{:S(2)}) copy-start(s32[96,9]{0,1:T(8,128)} %param.8) | copy-start | bytes 10372
  0.0 50.5 %copy-start.20 = (s32[96]{0:T(128)S(1)}, s32[96]{0:T(128)}, u32[]{:S(2)}) copy-start(s32[96]{0:T(128)} %counts.3) | copy-start | bytes 1156
  0.0 20.9 %collective-permute-start.7 = (bf16[256,1536]{1,0:T(8,128)(2,1)}, bf16[256,1536]{1,0:T(8,128)(2,1)}, u32[]{:S(2)}, u32[]{:S(2)}) collective-permute-start(bf16[256,1536]{1,0:T(8,128)(2,1)} %refs_5_.1), channel_id=1, source_target_pairs={{0,16},{4,20},{8,24},{12,28},{16,0},{20,4},{24,8},{28,12},{1,17},{... | collective-permute-start | bytes 2359304 | tf_op jit(solution)/shard_map/ppermute | solution.py:30
  3.0 20.6 %collective-permute-start.5 = (bf16[256,1536]{1,0:T(8,128)(2,1)}, bf16[256,1536]{1,0:T(8,128)(2,1)}, u32[]{:S(2)}, u32[]{:S(2)}) collective-permute-start(bf16[256,1536]{1,0:T(8,128)(2,1)} %refs_5_.1), channel_id=1, source_target_pairs={{0,8},{4,12},{8,0},{12,4},{16,24},{20,28},{24,16},{28,20},{1,9},{5... | collective-permute-start | bytes 2359304 | tf_op jit(solution)/shard_map/ppermute | solution.py:30
  4.5 20.7 %collective-permute-start = (bf16[768,512]{1,0:T(8,128)(2,1)}, bf16[768,512]{1,0:T(8,128)(2,1)S(1)}, u32[]{:S(2)}, u32[]{:S(2)}) collective-permute-start(bf16[768,512]{1,0:T(8,128)(2,1)} %refs_0_.1), channel_id=1, source_target_pairs={{0,1},{1,2},{2,3},{4,5},{5,6},{6,7},{8,9},{9,10},{10,11},{12,13},{... | collective-permute-start | bytes 2359304 | tf_op jit(solution)/shard_map/ppermute | solution.py:24
  8.1 21.7 %collective-permute-start.2 = (bf16[768,512]{1,0:T(8,128)(2,1)}, bf16[768,512]{1,0:T(8,128)(2,1)S(1)}, u32[]{:S(2)}, u32[]{:S(2)}) collective-permute-start(bf16[768,512]{1,0:T(8,128)(2,1)} %refs_0_.1), channel_id=1, source_target_pairs={{1,0},{2,1},{3,2},{5,4},{6,5},{7,6},{9,8},{10,9},{11,10},{13,12},{... | collective-permute-start | bytes 2359304 | tf_op jit(solution)/shard_map/ppermute | solution.py:25
  9.4 24.1 %collective-permute-start.4 = (bf16[256,1536]{1,0:T(8,128)(2,1)}, bf16[256,1536]{1,0:T(8,128)(2,1)S(1)}, u32[]{:S(2)}, u32[]{:S(2)}) collective-permute-start(bf16[256,1536]{1,0:T(8,128)(2,1)} %refs_5_.1), channel_id=1, source_target_pairs={{0,4},{4,0},{8,12},{12,8},{16,20},{20,16},{24,28},{28,24},{1,5},{5... | collective-permute-start | bytes 2359304 | tf_op jit(solution)/shard_map/ppermute | solution.py:30
  20.9 11.1 %collective-permute-start.13 = (bf16[256,512]{1,0:T(8,128)(2,1)}, bf16[256,512]{1,0:T(8,128)(2,1)S(1)}, u32[]{:S(2)}, u32[]{:S(2)}) collective-permute-start(bf16[256,512]{1,0:T(8,128)(2,1)} %param.7), channel_id=1, source_target_pairs={{0,16},{4,20},{8,24},{12,28},{16,0},{20,4},{24,8},{28,12},{1,17},{... | collective-permute-start | bytes 786440 | tf_op jit(solution)/shard_map/ppermute | solution.py:30
  23.7 9.8 %collective-permute-start.9 = (bf16[128,1536]{1,0:T(8,128)(2,1)S(1)}, bf16[128,1536]{1,0:T(8,128)(2,1)S(1)}, u32[]{:S(2)}, u32[]{:S(2)}) collective-permute-start(bf16[128,1536]{1,0:T(8,128)(2,1)S(1)} %slice.32), channel_id=1, source_target_pairs={{0,8},{4,12},{8,0},{12,4},{16,24},{20,28},{24,16},{28,20},{1,9},{5... | collective-permute-start | bytes 1179656 | tf_op jit(solution)/shard_map/ppermute | solution.py:30
  25.2 16.6 %copy-start.21 = (bf16[768,512]{1,0:T(8,128)(2,1)}, bf16[768,512]{1,0:T(8,128)(2,1)S(1)}, u32[]{:S(2)}) copy-start(bf16[768,512]{1,0:T(8,128)(2,1)S(1)} %collective-permute-done.refs_1_) | copy-start | bytes 2359300
  25.2 18.9 %collective-permute-start.1 = (bf16[768,512]{1,0:T(8,128)(2,1)S(1)}, bf16[768,512]{1,0:T(8,128)(2,1)}, u32[]{:S(2)}, u32[]{:S(2)}) collective-permute-start(bf16[768,512]{1,0:T(8,128)(2,1)S(1)} %collective-permute-done.refs_1_), channel_id=1, source_target_pairs={{0,1},{1,2},{2,3},{4,5},{5,6},{6,7},{8,9},{9,10},{10,11},{12,13},{... | collective-permute-start | bytes 2359304 | tf_op jit(solution)/shard_map/ppermute | solution.py:24
  29.7 18.9 %copy-start.22 = (bf16[768,512]{1,0:T(8,128)(2,1)}, bf16[768,512]{1,0:T(8,128)(2,1)S(1)}, u32[]{:S(2)}) copy-start(bf16[768,512]{1,0:T(8,128)(2,1)S(1)} %collective-permute-done.2.refs_3_) | copy-start | bytes 2359300
  29.7 19.5 %collective-permute-start.3 = (bf16[768,512]{1,0:T(8,128)(2,1)S(1)}, bf16[768,512]{1,0:T(8,128)(2,1)}, u32[]{:S(2)}, u32[]{:S(2)}) collective-permute-start(bf16[768,512]{1,0:T(8,128)(2,1)S(1)} %collective-permute-done.2.refs_3_), channel_id=1, source_target_pairs={{1,0},{2,1},{3,2},{5,4},{6,5},{7,6},{9,8},{10,9},{11,10},{13,12},{... | collective-permute-start | bytes 2359304 | tf_op jit(solution)/shard_map/ppermute | solution.py:25
  32.0 9.3 %collective-permute-start.10 = (bf16[128,1536]{1,0:T(8,128)(2,1)S(1)}, bf16[128,1536]{1,0:T(8,128)(2,1)}, u32[]{:S(2)}, u32[]{:S(2)}) collective-permute-start(bf16[128,1536]{1,0:T(8,128)(2,1)S(1)} %slice.33), channel_id=1, source_target_pairs={{0,16},{4,20},{8,24},{12,28},{16,0},{20,4},{24,8},{28,12},{1,17},{... | collective-permute-start | bytes 1179656 | tf_op jit(solution)/shard_map/ppermute | solution.py:30
  33.4 7.9 %collective-permute-start.11 = (bf16[128,1536]{1,0:T(8,128)(2,1)S(1)}, bf16[128,1536]{1,0:T(8,128)(2,1)S(1)}, u32[]{:S(2)}, u32[]{:S(2)}) collective-permute-start(bf16[128,1536]{1,0:T(8,128)(2,1)S(1)} %collective-permute-done.9.refs_11_), channel_id=1, source_target_pairs={{0,4},{4,0},{8,12},{12,8},{16,20},{20,16},{24,28},{28,24},{1,5},{5... | collective-permute-start | bytes 1179656 | tf_op jit(solution)/shard_map/ppermute | solution.py:30
  33.5 17.2 %copy-start.23 = (bf16[256,1536]{1,0:T(8,128)(2,1)}, bf16[256,1536]{1,0:T(8,128)(2,1)S(1)}, u32[]{:S(2)}) copy-start(bf16[256,1536]{1,0:T(8,128)(2,1)S(1)} %collective-permute-done.4.refs_6_) | copy-start | bytes 2359300
  33.5 20.6 %collective-permute-start.6 = (bf16[256,1536]{1,0:T(8,128)(2,1)}, bf16[256,1536]{1,0:T(8,128)(2,1)}, u32[]{:S(2)}, u32[]{:S(2)}) collective-permute-start(bf16[256,1536]{1,0:T(8,128)(2,1)} %collective-permute-done.5.refs_7_), channel_id=1, source_target_pairs={{0,4},{4,0},{8,12},{12,8},{16,20},{20,16},{24,28},{28,24},{1,5},{5... | collective-permute-start | bytes 2359304 | tf_op jit(solution)/shard_map/ppermute | solution.py:30
  41.3 12.7 %collective-permute-start.8 = (bf16[256,1536]{1,0:T(8,128)(2,1)}, bf16[256,1536]{1,0:T(8,128)(2,1)}, u32[]{:S(2)}, u32[]{:S(2)}) collective-permute-start(bf16[256,1536]{1,0:T(8,128)(2,1)} %collective-permute-done.7.refs_9_), channel_id=1, source_target_pairs={{0,4},{4,0},{8,12},{12,8},{16,20},{20,16},{24,28},{28,24},{1,5},{5... | collective-permute-start | bytes 2359304 | tf_op jit(solution)/shard_map/ppermute | solution.py:30
  41.3 10.1 %collective-permute-start.12 = (bf16[128,1536]{1,0:T(8,128)(2,1)}, bf16[128,1536]{1,0:T(8,128)(2,1)}, u32[]{:S(2)}, u32[]{:S(2)}) collective-permute-start(bf16[128,1536]{1,0:T(8,128)(2,1)} %collective-permute-done.10.refs_12_), channel_id=1, source_target_pairs={{0,4},{4,0},{8,12},{12,8},{16,20},{20,16},{24,28},{28,24},{1,5},{5... | collective-permute-start | bytes 1179656 | tf_op jit(solution)/shard_map/ppermute | solution.py:30
  44.1 20.7 %collective-permute-start.15 = (bf16[768,512]{1,0:T(8,128)(2,1)}, bf16[768,512]{1,0:T(8,128)(2,1)S(1)}, u32[]{:S(2)}, u32[]{:S(2)}) collective-permute-start(bf16[768,512]{1,0:T(8,128)(2,1)} %collective-permute-done.1.refs_2_), channel_id=1, source_target_pairs={{0,1},{1,2},{2,3},{4,5},{5,6},{6,7},{8,9},{9,10},{10,11},{12,13},{... | collective-permute-start | bytes 2359304 | tf_op jit(solution)/shard_map/ppermute | solution.py:24
  49.2 18.7 %collective-permute-start.16 = (bf16[768,512]{1,0:T(8,128)(2,1)}, bf16[768,512]{1,0:T(8,128)(2,1)S(1)}, u32[]{:S(2)}, u32[]{:S(2)}) collective-permute-start(bf16[768,512]{1,0:T(8,128)(2,1)} %collective-permute-done.3.refs_4_), channel_id=1, source_target_pairs={{1,0},{2,1},{3,2},{5,4},{6,5},{7,6},{9,8},{10,9},{11,10},{13,12},{... | collective-permute-start | bytes 2359304 | tf_op jit(solution)/shard_map/ppermute | solution.py:25
  51.4 13.4 %collective-permute-start.14 = (bf16[512,512]{1,0:T(8,128)(2,1)S(1)}, bf16[512,512]{1,0:T(8,128)(2,1)S(1)}, u32[]{:S(2)}, u32[]{:S(2)}) collective-permute-start(bf16[512,512]{1,0:T(8,128)(2,1)S(1)} %pad_maximum_fusion), channel_id=1, source_target_pairs={{0,8},{4,12},{8,0},{12,4},{16,24},{20,28},{24,16},{28,20},{1,9},{5... | collective-permute-start | bytes 1572872 | tf_op jit(solution)/shard_map/ppermute | solution.py:30
  74.0 8.8 %collective-permute-start.17 = (bf16[256,512]{1,0:T(8,128)(2,1)}, bf16[256,512]{1,0:T(8,128)(2,1)S(1)}, u32[]{:S(2)}, u32[]{:S(2)}) collective-permute-start(bf16[256,512]{1,0:T(8,128)(2,1)} %get-tuple-element.49), channel_id=1, source_target_pairs={{0,8},{4,12},{8,0},{12,4},{16,24},{20,28},{24,16},{28,20},{1,9},{5... | collective-permute-start | bytes 786440 | tf_op jit(solution)/shard_map/ppermute | solution.py:30
  74.6 10.0 %collective-permute-start.18 = (bf16[256,512]{1,0:T(8,128)(2,1)}, bf16[256,512]{1,0:T(8,128)(2,1)S(1)}, u32[]{:S(2)}, u32[]{:S(2)}) collective-permute-start(bf16[256,512]{1,0:T(8,128)(2,1)} %get-tuple-element.50), channel_id=1, source_target_pairs={{0,16},{4,20},{8,24},{12,28},{16,0},{20,4},{24,8},{28,12},{1,17},{... | collective-permute-start | bytes 786440 | tf_op jit(solution)/shard_map/ppermute | solution.py:30
  75.1 9.5 %collective-permute-start.19 = (bf16[256,512]{1,0:T(8,128)(2,1)}, bf16[256,512]{1,0:T(8,128)(2,1)S(1)}, u32[]{:S(2)}, u32[]{:S(2)}) collective-permute-start(bf16[256,512]{1,0:T(8,128)(2,1)} %get-tuple-element.51), channel_id=1, source_target_pairs={{0,24},{4,28},{8,16},{12,20},{16,8},{20,12},{24,0},{28,4},{1,25},{... | collective-permute-start | bytes 786440 | tf_op jit(solution)/shard_map/ppermute | solution.py:30
  84.7 3.6 %collective-permute-start.20 = (bf16[512,512]{1,0:T(8,128)(2,1)S(1)}, bf16[512,512]{1,0:T(8,128)(2,1)S(1)}, u32[]{:S(2)}, u32[]{:S(2)}) collective-permute-start(bf16[512,512]{1,0:T(8,128)(2,1)S(1)} %pad_maximum_fusion.1), channel_id=1, source_target_pairs={{0,4},{4,0},{8,12},{12,8},{16,20},{20,16},{24,28},{28,24},{1,5},{5... | collective-permute-start | bytes 1572872 | tf_op jit(solution)/shard_map/ppermute | solution.py:30
  84.8 11.9 %collective-permute-start.25 = (bf16[256,512]{1,0:T(8,128)(2,1)}, bf16[256,512]{1,0:T(8,128)(2,1)S(1)}, u32[]{:S(2)}, u32[]{:S(2)}) collective-permute-start(bf16[256,512]{1,0:T(8,128)(2,1)} %get-tuple-element.64), channel_id=1, source_target_pairs={{0,8},{4,12},{8,0},{12,4},{16,24},{20,28},{24,16},{28,20},{1,9},{5... | collective-permute-start | bytes 786440 | tf_op jit(solution)/shard_map/ppermute | solution.py:30
  86.3 14.0 %collective-permute-start.26 = (bf16[256,512]{1,0:T(8,128)(2,1)S(1)}, bf16[256,512]{1,0:T(8,128)(2,1)S(1)}, u32[]{:S(2)}, u32[]{:S(2)}) collective-permute-start(bf16[256,512]{1,0:T(8,128)(2,1)S(1)} %copy-done.28), channel_id=1, source_target_pairs={{0,16},{4,20},{8,24},{12,28},{16,0},{20,4},{24,8},{28,12},{1,17},{... | collective-permute-start | bytes 786440 | tf_op jit(solution)/shard_map/ppermute | solution.py:30
  86.9 13.5 %collective-permute-start.27 = (bf16[256,512]{1,0:T(8,128)(2,1)S(1)}, bf16[256,512]{1,0:T(8,128)(2,1)S(1)}, u32[]{:S(2)}, u32[]{:S(2)}) collective-permute-start(bf16[256,512]{1,0:T(8,128)(2,1)S(1)} %copy-done.27), channel_id=1, source_target_pairs={{0,24},{4,28},{8,16},{12,20},{16,8},{20,12},{24,0},{28,4},{1,25},{... | collective-permute-start | bytes 786440 | tf_op jit(solution)/shard_map/ppermute | solution.py:30
  100.4 4.4 %collective-permute-start.28 = (bf16[512,512]{1,0:T(8,128)(2,1)S(1)}, bf16[512,512]{1,0:T(8,128)(2,1)}, u32[]{:S(2)}, u32[]{:S(2)}) collective-permute-start(bf16[512,512]{1,0:T(8,128)(2,1)S(1)} %pad_maximum_fusion.2), channel_id=1, source_target_pairs={{0,4},{4,0},{8,12},{12,8},{16,20},{20,16},{24,28},{28,24},{1,5},{5... | collective-permute-start | bytes 1572872 | tf_op jit(solution)/shard_map/ppermute | solution.py:30
  101.1 48.9 %collective-permute-start.33 = (bf16[1024,512]{1,0:T(8,128)(2,1)S(1)}, bf16[1024,512]{1,0:T(8,128)(2,1)S(1)}, u32[]{:S(2)}, u32[]{:S(2)}) collective-permute-start(bf16[1024,512]{1,0:T(8,128)(2,1)S(1)} %constant_dynamic-update-slice_fusion.refs_10_), channel_id=1, source_target_pairs={{0,4},{4,0},{8,12},{12,8},{16,20},{20,16},{24,28},{28,24},{1,5},{5... | collective-permute-start | bytes 3145736 | tf_op jit(solution)/shard_map/ppermute | solution.py:30
  101.5 16.7 %collective-permute-start.21 = (bf16[768,256]{1,0:T(8,128)(2,1)S(1)}, bf16[768,256]{1,0:T(8,128)(2,1)S(1)}, u32[]{:S(2)}, u32[]{:S(2)}) collective-permute-start(bf16[768,256]{1,0:T(8,128)(2,1)S(1)} %copy-done.5), channel_id=1, source_target_pairs={{0,1},{1,2},{2,3},{4,5},{5,6},{6,7},{8,9},{9,10},{10,11},{12,13},{... | collective-permute-start | bytes 1179656 | tf_op jit(solution)/shard_map/ppermute | solution.py:24
  103.6 20.0 %collective-permute-start.23 = (bf16[768,256]{1,0:T(8,128)(2,1)S(1)}, bf16[768,256]{1,0:T(8,128)(2,1)S(1)}, u32[]{:S(2)}, u32[]{:S(2)}) collective-permute-start(bf16[768,256]{1,0:T(8,128)(2,1)S(1)} %copy-done.5), channel_id=1, source_target_pairs={{1,0},{2,1},{3,2},{5,4},{6,5},{7,6},{9,8},{10,9},{11,10},{13,12},{... | collective-permute-start | bytes 1179656 | tf_op jit(solution)/shard_map/ppermute | solution.py:25
  112.3 14.4 %collective-permute-start.29 = (bf16[768,256]{1,0:T(8,128)(2,1)}, bf16[768,256]{1,0:T(8,128)(2,1)S(1)}, u32[]{:S(2)}, u32[]{:S(2)}) collective-permute-start(bf16[768,256]{1,0:T(8,128)(2,1)} %shard_map.60.refs_5_), channel_id=1, source_target_pairs={{0,1},{1,2},{2,3},{4,5},{5,6},{6,7},{8,9},{9,10},{10,11},{12,13},{... | collective-permute-start | bytes 1179656 | tf_op jit(solution)/shard_map/ppermute | solution.py:24
  116.9 14.9 %collective-permute-start.31 = (bf16[768,256]{1,0:T(8,128)(2,1)}, bf16[768,256]{1,0:T(8,128)(2,1)S(1)}, u32[]{:S(2)}, u32[]{:S(2)}) collective-permute-start(bf16[768,256]{1,0:T(8,128)(2,1)} %shard_map.60.refs_5_), channel_id=1, source_target_pairs={{1,0},{2,1},{3,2},{5,4},{6,5},{7,6},{9,8},{10,9},{11,10},{13,12},{... | collective-permute-start | bytes 1179656 | tf_op jit(solution)/shard_map/ppermute | solution.py:25
  118.2 31.8 %copy-start.6 = (bf16[768,256]{1,0:T(8,128)(2,1)}, bf16[768,256]{1,0:T(8,128)(2,1)S(1)}, u32[]{:S(2)}) copy-start(bf16[768,256]{1,0:T(8,128)(2,1)S(1)} %collective-permute-done.21.refs_1_) | copy-start | bytes 1179652
  118.2 16.8 %collective-permute-start.22 = (bf16[768,256]{1,0:T(8,128)(2,1)S(1)}, bf16[768,256]{1,0:T(8,128)(2,1)}, u32[]{:S(2)}, u32[]{:S(2)}) collective-permute-start(bf16[768,256]{1,0:T(8,128)(2,1)S(1)} %collective-permute-done.21.refs_1_), channel_id=1, source_target_pairs={{0,1},{1,2},{2,3},{4,5},{5,6},{6,7},{8,9},{9,10},{10,11},{12,13},{... | collective-permute-start | bytes 1179656 | tf_op jit(solution)/shard_map/ppermute | solution.py:24
  123.5 26.5 %copy-start.7 = (bf16[768,256]{1,0:T(8,128)(2,1)}, bf16[768,256]{1,0:T(8,128)(2,1)S(1)}, u32[]{:S(2)}) copy-start(bf16[768,256]{1,0:T(8,128)(2,1)S(1)} %collective-permute-done.23.refs_3_) | copy-start | bytes 1179652
  123.5 16.7 %collective-permute-start.24 = (bf16[768,256]{1,0:T(8,128)(2,1)S(1)}, bf16[768,256]{1,0:T(8,128)(2,1)S(1)}, u32[]{:S(2)}, u32[]{:S(2)}) collective-permute-start(bf16[768,256]{1,0:T(8,128)(2,1)S(1)} %collective-permute-done.23.refs_3_), channel_id=1, source_target_pairs={{1,0},{2,1},{3,2},{5,4},{6,5},{7,6},{9,8},{10,9},{11,10},{13,12},{... | collective-permute-start | bytes 1179656 | tf_op jit(solution)/shard_map/ppermute | solution.py:25
  126.7 23.3 %copy-start.8 = (bf16[768,256]{1,0:T(8,128)(2,1)}, bf16[768,256]{1,0:T(8,128)(2,1)S(1)}, u32[]{:S(2)}) copy-start(bf16[768,256]{1,0:T(8,128)(2,1)S(1)} %collective-permute-done.29.refs_6_) | copy-start | bytes 1179652
  126.7 16.7 %collective-permute-start.30 = (bf16[768,256]{1,0:T(8,128)(2,1)S(1)}, bf16[768,256]{1,0:T(8,128)(2,1)}, u32[]{:S(2)}, u32[]{:S(2)}) collective-permute-start(bf16[768,256]{1,0:T(8,128)(2,1)S(1)} %collective-permute-done.29.refs_6_), channel_id=1, source_target_pairs={{0,1},{1,2},{2,3},{4,5},{5,6},{6,7},{8,9},{9,10},{10,11},{12,13},{... | collective-permute-start | bytes 1179656 | tf_op jit(solution)/shard_map/ppermute | solution.py:24
  131.7 16.9 %copy-start.9 = (bf16[768,256]{1,0:T(8,128)(2,1)}, bf16[768,256]{1,0:T(8,128)(2,1)S(1)}, u32[]{:S(2)}) copy-start(bf16[768,256]{1,0:T(8,128)(2,1)S(1)} %collective-permute-done.31.refs_8_) | copy-start | bytes 1179652
  131.7 16.9 %collective-permute-start.32 = (bf16[768,256]{1,0:T(8,128)(2,1)S(1)}, bf16[768,256]{1,0:T(8,128)(2,1)}, u32[]{:S(2)}, u32[]{:S(2)}) collective-permute-start(bf16[768,256]{1,0:T(8,128)(2,1)S(1)} %collective-permute-done.31.refs_8_), channel_id=1, source_target_pairs={{1,0},{2,1},{3,2},{5,4},{6,5},{7,6},{9,8},{10,9},{11,10},{13,12},{... | collective-permute-start | bytes 1179656 | tf_op jit(solution)/shard_map/ppermute | solution.py:25
  135.0 22.2 %collective-permute-start.34 = (bf16[768,256]{1,0:T(8,128)(2,1)}, bf16[768,256]{1,0:T(8,128)(2,1)}, u32[]{:S(2)}, u32[]{:S(2)}) collective-permute-start(bf16[768,256]{1,0:T(8,128)(2,1)} %collective-permute-done.22.refs_2_), channel_id=1, source_target_pairs={{0,1},{1,2},{2,3},{4,5},{5,6},{6,7},{8,9},{9,10},{10,11},{12,13},{... | collective-permute-start | bytes 1179656 | tf_op jit(solution)/shard_map/ppermute | solution.py:24
  140.3 16.9 %collective-permute-start.35 = (bf16[768,256]{1,0:T(8,128)(2,1)S(1)}, bf16[768,256]{1,0:T(8,128)(2,1)}, u32[]{:S(2)}, u32[]{:S(2)}) collective-permute-start(bf16[768,256]{1,0:T(8,128)(2,1)S(1)} %collective-permute-done.24.refs_4_), channel_id=1, source_target_pairs={{1,0},{2,1},{3,2},{5,4},{6,5},{7,6},{9,8},{10,9},{11,10},{13,12},{... | collective-permute-start | bytes 1179656 | tf_op jit(solution)/shard_map/ppermute | solution.py:25
  143.4 15.7 %collective-permute-start.36 = (bf16[768,256]{1,0:T(8,128)(2,1)}, bf16[768,256]{1,0:T(8,128)(2,1)}, u32[]{:S(2)}, u32[]{:S(2)}) collective-permute-start(bf16[768,256]{1,0:T(8,128)(2,1)} %collective-permute-done.30.refs_7_), channel_id=1, source_target_pairs={{0,1},{1,2},{2,3},{4,5},{5,6},{6,7},{8,9},{9,10},{10,11},{12,13},{... | collective-permute-start | bytes 1179656 | tf_op jit(solution)/shard_map/ppermute | solution.py:24
  148.7 14.6 %collective-permute-start.37 = (bf16[768,256]{1,0:T(8,128)(2,1)}, bf16[768,256]{1,0:T(8,128)(2,1)}, u32[]{:S(2)}, u32[]{:S(2)}) collective-permute-start(bf16[768,256]{1,0:T(8,128)(2,1)} %collective-permute-done.32.refs_9_), channel_id=1, source_target_pairs={{1,0},{2,1},{3,2},{5,4},{6,5},{7,6},{9,8},{10,9},{11,10},{13,12},{... | collective-permute-start | bytes 1179656 | tf_op jit(solution)/shard_map/ppermute | solution.py:25
  (19 other events, 91.7 us)

commit v5 on v4

--- a/solution.py
+++ b/solution.py
@@ -13,6 +13,7 @@
 MIB = 1024 * 1024
 LOG2E = 1.4426950408889634
 HBM = pl.BlockSpec(memory_space=pltpu.HBM)
+ANY = pl.BlockSpec(memory_space=pl.ANY)
 SMEM = pl.BlockSpec(memory_space=pltpu.SMEM)
 VMEM_LIMIT = 60 * MIB
 
@@ -146,7 +147,7 @@
             jax.ShapeDtypeStruct((tok_rows, columns), jnp.float32),
             jax.ShapeDtypeStruct((deferred * cut, columns), jnp.bfloat16),
         ],
-        in_specs=[SMEM] + [HBM] * (len(flat) + len(stacks)),
+        in_specs=[SMEM] + [ANY] * (len(flat) + len(stacks)),
         out_specs=[HBM, HBM],
         scratch_shapes=[
             pltpu.VMEM((tok_rows, full), jnp.bfloat16),
@@ -335,7 +336,7 @@
     return pl.pallas_call(
         functools.partial(attend_kernel, tok_size=tok_size, heads=heads),
         out_shape=jax.ShapeDtypeStruct((tok_rows, wide), jnp.bfloat16),
-        in_specs=[SMEM] * 3 + [HBM] * (2 + tok_size // 2),
+        in_specs=[SMEM] * 3 + [ANY] * (2 + tok_size // 2),
         out_specs=HBM,
         scratch_shapes=[
             pltpu.VMEM((tok_rows + (tok_size - 1) * 2 * BLK, 2 * wide), jnp.bfloat16),
@@ -343,7 +344,7 @@
             pltpu.VMEM((tok_rows, wide), jnp.bfloat16),
             pltpu.SemaphoreType.DMA((tok_size + 1,)),
         ],
-        compiler_params=pltpu.CompilerParams(vmem_limit_bytes=VMEM_LIMIT),
+        compiler_params=pltpu.CompilerParams(vmem_limit_bytes=16 * MIB),
         cost_estimate=pl.CostEstimate(
             flops=8 * tok_rows * NEIGH * BLK * wide,
             bytes_accessed=2 * tok_rows * wide * 10,

time: 168 us -> 168 us (level)
    pallas_call x2, Pallas kernels: 14.9 us -> 13.3 us  [attend(): pl.pallas_call(functools.partial(attend_kernel, tok_size=tok_size, heads=...]
    unnamed x60 -> x62, local copies, waits for them, and re-layouts: 3.6 us -> 2.34 us
  transfers between devices with their start and end apart: 38 -> 38, of which waited for: 13 -> 13; matrix products, arithmetic and copies ran while one was open for 2% -> 2% of each run, Pallas kernels for 23% -> 22%
where the time goes in v5:
time: 168 us; the launch traced here: 167 us
  starting transfers between devices  70.2 us (42%)
  Pallas kernels  46.1 us (27%)
  waiting for transfers between devices  44 us (26%)
  local copies, waits for them, and re-layouts  5.25 us (3%)
    ppermute x9, starting transfers between devices, line_step(): left = lax.ppermute((from_left or [own])[-1], axis, to_right)  40.7 us
    ppermute x20, waiting for transfers between devices, swap(): return lax.ppermute(x, axis, [(i, i ^ s) for i in range(size)])  26.8 us
    ppermute x20, starting transfers between devices, swap(): return lax.ppermute(x, axis, [(i, i ^ s) for i in range(size)])  17.9 us
    pallas_call x2, Pallas kernels, accumulate(): pl.pallas_call(functools.partial(accumulate_kernel, reach=reach, hid_size...  16.9 us
    pallas_call x3, Pallas kernels, finish(): pl.pallas_call(functools.partial(finish_kernel, deferred=deferred, hid_si...  14.5 us
    pallas_call x2, Pallas kernels, attend(): pl.pallas_call(functools.partial(attend_kernel, tok_size=tok_size, heads=...  13.3 us
    ppermute x9, starting transfers between devices, line_step(): right = lax.ppermute((from_right or [own])[-1], axis, to_left)  11.6 us
    ppermute x9, waiting for transfers between devices, line_step(): left = lax.ppermute((from_left or [own])[-1], axis, to_right)  9.36 us
  transfers between devices with their start and end apart: 38, of which 13 were waited for; matrix products, arithmetic and copies ran while one was open for 2% of the time, Pallas kernels for 22%

profile of v5, /device:TPU:0, one launch (start us, length us, event | category | flops | bytes accessed | tf_op | source)
XLA Modules:
  0.0 166.9 jit_solution(13767449280992993075)
XLA Ops:
  0.0 3.0 %collective-permute-start.7 = (bf16[256,1536]{1,0:T(8,128)(2,1)}, bf16[256,1536]{1,0:T(8,128)(2,1)}, u32[]{:S(2)}, u32[]{:S(2)}) collective-permute-start(bf16[256,1536]{1,0:T(8,128)(2,1)} %refs_5_.1), channel_id=1, source_target_pairs={{0,16},{4,20},{8,24},{12,28},{16,0},{20,4},{24,8},{28,12},{1,17},{... | collective-permute-start | bytes 2359304 | tf_op jit(solution)/shard_map/ppermute | solution.py:31
  3.0 1.5 collective-permute-start.5
  4.5 3.5 %collective-permute-start = (bf16[768,512]{1,0:T(8,128)(2,1)}, bf16[768,512]{1,0:T(8,128)(2,1)S(1)}, u32[]{:S(2)}, u32[]{:S(2)}) collective-permute-start(bf16[768,512]{1,0:T(8,128)(2,1)} %refs_0_.1), channel_id=1, source_target_pairs={{0,1},{1,2},{2,3},{4,5},{5,6},{6,7},{8,9},{9,10},{10,11},{12,13},{... | collective-permute-start | bytes 2359304 | tf_op jit(solution)/shard_map/ppermute | solution.py:25
  8.1 1.3 collective-permute-start.2
  9.4 11.5 %collective-permute-done.7.refs_9_ = bf16[256,1536]{1,0:T(8,128)(2,1)} collective-permute-done((bf16[256,1536]{1,0:T(8,128)(2,1)}, bf16[256,1536]{1,0:T(8,128)(2,1)}, u32[]{:S(2)}, u32[]{:S(2)}) %collective-permute-start.7) | collective-permute-done | bytes 786464 | tf_op jit(solution)/shard_map/ppermute | solution.py:31
  20.9 1.7 %collective-permute-start.13 = (bf16[256,512]{1,0:T(8,128)(2,1)}, bf16[256,512]{1,0:T(8,128)(2,1)S(1)}, u32[]{:S(2)}, u32[]{:S(2)}) collective-permute-start(bf16[256,512]{1,0:T(8,128)(2,1)} %param.7), channel_id=1, source_target_pairs={{0,16},{4,20},{8,24},{12,28},{16,0},{20,4},{24,8},{28,12},{1,17},{... | collective-permute-start | bytes 786440 | tf_op jit(solution)/shard_map/ppermute | solution.py:31
  22.6 1.0 slice.32
  23.7 1.6 collective-permute-start.9
  25.2 4.5 %collective-permute-start.1 = (bf16[768,512]{1,0:T(8,128)(2,1)S(1)}, bf16[768,512]{1,0:T(8,128)(2,1)}, u32[]{:S(2)}, u32[]{:S(2)}) collective-permute-start(bf16[768,512]{1,0:T(8,128)(2,1)S(1)} %collective-permute-done.refs_1_), channel_id=1, source_target_pairs={{0,1},{1,2},{2,3},{4,5},{5,6},{6,7},{8,9},{9,10},{10,11},{12,13},{... | collective-permute-start | bytes 2359304 | tf_op jit(solution)/shard_map/ppermute | solution.py:25
  29.7 1.3 collective-permute-start.3
  31.0 1.0 slice.33
  34.0 7.2 %collective-permute-done.10.refs_12_ = bf16[128,1536]{1,0:T(8,128)(2,1)S(1)} collective-permute-done((bf16[128,1536]{1,0:T(8,128)(2,1)S(1)}, bf16[128,1536]{1,0:T(8,128)(2,1)S(1)}, u32[]{:S(2)}, u32[]{:S(2)}) %collective-permute-start.10) | collective-permute-done | bytes 393248 | tf_op jit(solution)/shard_map/ppermute | solution.py:31
  42.0 2.1 %collective-permute-done.1.refs_2_ = bf16[768,512]{1,0:T(8,128)(2,1)} collective-permute-done((bf16[768,512]{1,0:T(8,128)(2,1)S(1)}, bf16[768,512]{1,0:T(8,128)(2,1)}, u32[]{:S(2)}, u32[]{:S(2)}) %collective-permute-start.1) | collective-permute-done | bytes 786464 | tf_op jit(solution)/shard_map/ppermute | solution.py:25
  44.1 4.5 %collective-permute-start.15 = (bf16[768,512]{1,0:T(8,128)(2,1)}, bf16[768,512]{1,0:T(8,128)(2,1)S(1)}, u32[]{:S(2)}, u32[]{:S(2)}) collective-permute-start(bf16[768,512]{1,0:T(8,128)(2,1)} %collective-permute-done.1.refs_2_), channel_id=1, source_target_pairs={{0,1},{1,2},{2,3},{4,5},{5,6},{6,7},{8,9},{9,10},{10,11},{12,13},{... | collective-permute-start | bytes 2359304 | tf_op jit(solution)/shard_map/ppermute | solution.py:25
  49.2 1.3 collective-permute-start.16
  52.7 1.4 shard_map.56
  54.1 10.7 %shard_map.55 = (f32[768,1536]{1,0:T(8,128)}, bf16[512,1536]{1,0:T(8,128)(2,1)}) custom-call(s32[2]{0:T(128)} %pad_add_fusion.place, bf16[768,512]{1,0:T(8,128)(2,1)} %refs_0_.1, bf16[768,512]{1,0:T(8,128)(2,1)} %copy-done.22, bf16[768,512]{1,0:T(8,128)(2,1)} %collective-permute-done.1.refs_2_, bf16[768,512]{1,0:T(8,128)(2,1)} %copy-done.23, ...), custom_call_target="tpu_custom_call" | custom-call | flops 4831838208 | bytes 9437184 | tf_op jit(solution)/shard_map/pallas_call | solution.py:141
  64.9 3.2 %collective-permute-done.16.refs_2_ = bf16[768,512]{1,0:T(8,128)(2,1)S(1)} collective-permute-done((bf16[768,512]{1,0:T(8,128)(2,1)}, bf16[768,512]{1,0:T(8,128)(2,1)S(1)}, u32[]{:S(2)}, u32[]{:S(2)}) %collective-permute-start.16) | collective-permute-done | bytes 786464 | tf_op jit(solution)/shard_map/ppermute | solution.py:26
  68.1 0.9 copy-done.10
  69.0 5.2 %shard_map.57 = (bf16[768,256]{1,0:T(8,128)(2,1)}, bf16[768,512]{1,0:T(8,128)(2,1)}, bf16[128,512]{1,0:T(8,128)(2,1)}, bf16[256,512]{1,0:T(8,128)(2,1)}, bf16[25...) custom-call(s32[2]{0:T(128)} %pad_add_fusion.place, s32[8,128]{1,0:T(8,128)} %get-tuple-element.42.send_ids, ...), custom_call_target="tpu_custom_call" | custom-call | flops 603979776 | bytes 4718592 | tf_op jit(solution)/shard_map/pallas_call | solution.py:253
  75.3 2.5 %collective-permute-start.19 = (bf16[256,512]{1,0:T(8,128)(2,1)}, bf16[256,512]{1,0:T(8,128)(2,1)S(1)}, u32[]{:S(2)}, u32[]{:S(2)}) collective-permute-start(bf16[256,512]{1,0:T(8,128)(2,1)} %get-tuple-element.51), channel_id=1, source_target_pairs={{0,24},{4,28},{8,16},{12,20},{16,8},{20,12},{24,0},{28,4},{1,25},{... | collective-permute-start | bytes 786440 | tf_op jit(solution)/shard_map/ppermute | solution.py:31
  77.8 5.2 %shard_map.58 = (bf16[768,256]{1,0:T(8,128)(2,1)}, bf16[768,512]{1,0:T(8,128)(2,1)}, bf16[128,512]{1,0:T(8,128)(2,1)}, bf16[256,512]{1,0:T(8,128)(2,1)}, bf16[25...) custom-call(s32[2]{0:T(128)} %pad_add_fusion.place, s32[8,128]{1,0:T(8,128)} %get-tuple-element.42.send_ids, ...), custom_call_target="tpu_custom_call" | custom-call | flops 603979776 | bytes 4718592 | tf_op jit(solution)/shard_map/pallas_call | solution.py:253
  83.1 1.9 %collective-permute-done.18.refs_2_ = bf16[256,512]{1,0:T(8,128)(2,1)S(1)} collective-permute-done((bf16[256,512]{1,0:T(8,128)(2,1)}, bf16[256,512]{1,0:T(8,128)(2,1)S(1)}, u32[]{:S(2)}, u32[]{:S(2)}) %collective-permute-start.18) | collective-permute-done | bytes 262176 | tf_op jit(solution)/shard_map/ppermute | solution.py:31
  85.1 1.6 collective-permute-start.25
  87.2 1.5 collective-permute-start.27
  88.7 6.6 %shard_map.59.refs_0_ = bf16[768,256]{1,0:T(8,128)(2,1)S(1)} custom-call(s32[2]{0:T(128)S(1)} %copy-done.2, s32[1,108]{1,0:T(1,128)S(1)} %copy-done.8, s32[96]{0:T(128)S(1)} %copy-done.3, bf16[768,256]{1,0:T(8,128)(2,1)S(1)} %copy-done.7, bf16[768,512]{1,0:T(8,128)(2,1)S(1)} %copy-done.5, bf16[512,512]{1,0:T(8,128)(2,1)S(1)} %collective-permute-done.20.refs_0_, ...), custom_call_target="tpu_custom_call" | custom-call | flops 905969664 | bytes 3932160 | tf_op jit(solution)/shard_map/pallas_call | solution.py:336
  95.4 5.3 %collective-permute-done.26.refs_2_ = bf16[256,512]{1,0:T(8,128)(2,1)S(1)} collective-permute-done((bf16[256,512]{1,0:T(8,128)(2,1)S(1)}, bf16[256,512]{1,0:T(8,128)(2,1)S(1)}, u32[]{:S(2)}, u32[]{:S(2)}) %collective-permute-start.26) | collective-permute-done | bytes 262176 | tf_op jit(solution)/shard_map/ppermute | solution.py:31
  101.6 2.7 %collective-permute-start.21 = (bf16[768,256]{1,0:T(8,128)(2,1)S(1)}, bf16[768,256]{1,0:T(8,128)(2,1)S(1)}, u32[]{:S(2)}, u32[]{:S(2)}) collective-permute-start(bf16[768,256]{1,0:T(8,128)(2,1)S(1)} %shard_map.59.refs_0_), channel_id=1, source_target_pairs={{0,1},{1,2},{2,3},{4,5},{5,6},{6,7},{8,9},{9,10},{10,11},{12,13},{... | collective-permute-start | bytes 1179656 | tf_op jit(solution)/shard_map/ppermute | solution.py:25
  104.3 1.3 collective-permute-start.23
  105.6 6.6 %shard_map.60.refs_5_ = bf16[768,256]{1,0:T(8,128)(2,1)S(1)} custom-call(s32[2]{0:T(128)S(1)} %copy-done.2, s32[1,108]{1,0:T(1,128)S(1)} %copy-done.8, s32[96]{0:T(128)S(1)} %copy-done.3, bf16[768,256]{1,0:T(8,128)(2,1)S(1)} %copy-done.6, bf16[768,512]{1,0:T(8,128)(2,1)S(1)} %copy-done.4, bf16[512,512]{1,0:T(8,128)(2,1)S(1)} %collective-permute-done.28.refs_0_, ...), custom_call_target="tpu_custom_call" | custom-call | flops 905969664 | bytes 3932160 | tf_op jit(solution)/shard_map/pallas_call | solution.py:336
  112.3 4.6 %collective-permute-start.29 = (bf16[768,256]{1,0:T(8,128)(2,1)S(1)}, bf16[768,256]{1,0:T(8,128)(2,1)S(1)}, u32[]{:S(2)}, u32[]{:S(2)}) collective-permute-start(bf16[768,256]{1,0:T(8,128)(2,1)S(1)} %shard_map.60.refs_5_), channel_id=1, source_target_pairs={{0,1},{1,2},{2,3},{4,5},{5,6},{6,7},{8,9},{9,10},{10,11},{12,13},{... | collective-permute-start | bytes 1179656 | tf_op jit(solution)/shard_map/ppermute | solution.py:25
  116.8 1.3 collective-permute-start.31
  118.2 5.3 %collective-permute-start.22 = (bf16[768,256]{1,0:T(8,128)(2,1)S(1)}, bf16[768,256]{1,0:T(8,128)(2,1)}, u32[]{:S(2)}, u32[]{:S(2)}) collective-permute-start(bf16[768,256]{1,0:T(8,128)(2,1)S(1)} %collective-permute-done.21.refs_1_), channel_id=1, source_target_pairs={{0,1},{1,2},{2,3},{4,5},{5,6},{6,7},{8,9},{9,10},{10,11},{12,13},{... | collective-permute-start | bytes 1179656 | tf_op jit(solution)/shard_map/ppermute | solution.py:25
  123.5 1.3 collective-permute-start.24
  124.8 1.6 collective-permute-done.29.refs_6_
  126.4 5.1 %collective-permute-start.30 = (bf16[768,256]{1,0:T(8,128)(2,1)S(1)}, bf16[768,256]{1,0:T(8,128)(2,1)}, u32[]{:S(2)}, u32[]{:S(2)}) collective-permute-start(bf16[768,256]{1,0:T(8,128)(2,1)S(1)} %collective-permute-done.29.refs_6_), channel_id=1, source_target_pairs={{0,1},{1,2},{2,3},{4,5},{5,6},{6,7},{8,9},{9,10},{10,11},{12,13},{... | collective-permute-start | bytes 1179656 | tf_op jit(solution)/shard_map/ppermute | solution.py:25
  131.5 1.3 collective-permute-start.32
  132.8 2.0 %collective-permute-done.22.refs_2_ = bf16[768,256]{1,0:T(8,128)(2,1)} collective-permute-done((bf16[768,256]{1,0:T(8,128)(2,1)S(1)}, bf16[768,256]{1,0:T(8,128)(2,1)}, u32[]{:S(2)}, u32[]{:S(2)}) %collective-permute-start.22) | collective-permute-done | bytes 393248 | tf_op jit(solution)/shard_map/ppermute | solution.py:25
  134.8 5.2 %collective-permute-start.34 = (bf16[768,256]{1,0:T(8,128)(2,1)}, bf16[768,256]{1,0:T(8,128)(2,1)}, u32[]{:S(2)}, u32[]{:S(2)}) collective-permute-start(bf16[768,256]{1,0:T(8,128)(2,1)} %collective-permute-done.22.refs_2_), channel_id=1, source_target_pairs={{0,1},{1,2},{2,3},{4,5},{5,6},{6,7},{8,9},{9,10},{10,11},{12,13},{... | collective-permute-start | bytes 1179656 | tf_op jit(solution)/shard_map/ppermute | solution.py:25
  140.0 1.3 collective-permute-start.35
  141.3 1.9 %collective-permute-done.30.refs_7_ = bf16[768,256]{1,0:T(8,128)(2,1)} collective-permute-done((bf16[768,256]{1,0:T(8,128)(2,1)S(1)}, bf16[768,256]{1,0:T(8,128)(2,1)}, u32[]{:S(2)}, u32[]{:S(2)}) %collective-permute-start.30) | collective-permute-done | bytes 393248 | tf_op jit(solution)/shard_map/ppermute | solution.py:25
  143.2 5.2 %collective-permute-start.36 = (bf16[768,256]{1,0:T(8,128)(2,1)}, bf16[768,256]{1,0:T(8,128)(2,1)}, u32[]{:S(2)}, u32[]{:S(2)}) collective-permute-start(bf16[768,256]{1,0:T(8,128)(2,1)} %collective-permute-done.30.refs_7_), channel_id=1, source_target_pairs={{0,1},{1,2},{2,3},{4,5},{5,6},{6,7},{8,9},{9,10},{10,11},{12,13},{... | collective-permute-start | bytes 1179656 | tf_op jit(solution)/shard_map/ppermute | solution.py:25
  148.5 1.3 collective-permute-start.37
  149.8 1.0 copy-done.13
  150.8 6.1 %shard_map.61 = (f32[768,512]{1,0:T(8,128)}, bf16[512,512]{1,0:T(8,128)(2,1)}) custom-call(s32[2]{0:T(128)} %pad_add_fusion.place, bf16[768,256]{1,0:T(8,128)(2,1)} %copy-done, bf16[768,256]{1,0:T(8,128)(2,1)} %copy-done.14, bf16[768,256]{1,0:T(8,128)(2,1)} %collective-permute-done.22.refs_2_, bf16[768,256]{1,0:T(8,128)(2,1)} %copy-done.15, ...), custom_call_target="tpu_custom_call" | custom-call | flops 1610612736 | bytes 5242880 | tf_op jit(solution)/shard_map/pallas_call | solution.py:141
  157.0 1.8 %collective-permute-done.36.refs_3_ = bf16[768,256]{1,0:T(8,128)(2,1)} collective-permute-done((bf16[768,256]{1,0:T(8,128)(2,1)}, bf16[768,256]{1,0:T(8,128)(2,1)}, u32[]{:S(2)}, u32[]{:S(2)}) %collective-permute-start.36) | collective-permute-done | bytes 393248 | tf_op jit(solution)/shard_map/ppermute | solution.py:25
  158.7 4.1 %collective-permute-done.37.refs_4_ = bf16[768,256]{1,0:T(8,128)(2,1)} collective-permute-done((bf16[768,256]{1,0:T(8,128)(2,1)}, bf16[768,256]{1,0:T(8,128)(2,1)}, u32[]{:S(2)}, u32[]{:S(2)}) %collective-permute-start.37) | collective-permute-done | bytes 393248 | tf_op jit(solution)/shard_map/ppermute | solution.py:26
  162.9 4.1 %shard_map.62 = bf16[768,512]{1,0:T(8,128)(2,1)} custom-call(s32[2]{0:T(128)} %pad_add_fusion.place, s32[8,128]{1,0:T(8,128)} %get-tuple-element.42.send_ids, f32[768,512]{1,0:T(8,128)} %get-tuple-element.71.refs_0_, bf16[768,256]{1,0:T(8,128)(2,1)} %collective-permute-done.34.refs_1_, bf16[768,256]{1,0:T(8,128)(2,1)} %collective-permute-done.35.refs_2_, ...), custom_call_target="tpu_custom_call" | custom-call | flops 402653184 | bytes 3145728 | tf_op jit(solution)/shard_map/pallas_call | solution.py:253
  (114 shorter events, 8.1 us)
Async XLA Ops:
  0.0 51.4 %copy-start.12 = (bf16[256,512]{1,0:T(8,128)(2,1)S(1)}, bf16[256,512]{1,0:T(8,128)(2,1)}, u32[]{:S(2)}) copy-start(bf16[256,512]{1,0:T(8,128)(2,1)} %param.7) | copy-start | bytes 786436
  0.0 50.5 %copy-start.21 = (s32[96,9]{0,1:T(8,128)S(1)}, s32[96,9]{0,1:T(8,128)}, u32[]{:S(2)}) copy-start(s32[96,9]{0,1:T(8,128)} %param.8) | copy-start | bytes 10372
  0.0 50.5 %copy-start.3 = (s32[96]{0:T(128)S(1)}, s32[96]{0:T(128)}, u32[]{:S(2)}) copy-start(s32[96]{0:T(128)} %counts.3) | copy-start | bytes 1156
  0.0 20.9 %collective-permute-start.7 = (bf16[256,1536]{1,0:T(8,128)(2,1)}, bf16[256,1536]{1,0:T(8,128)(2,1)}, u32[]{:S(2)}, u32[]{:S(2)}) collective-permute-start(bf16[256,1536]{1,0:T(8,128)(2,1)} %refs_5_.1), channel_id=1, source_target_pairs={{0,16},{4,20},{8,24},{12,28},{16,0},{20,4},{24,8},{28,12},{1,17},{... | collective-permute-start | bytes 2359304 | tf_op jit(solution)/shard_map/ppermute | solution.py:31
  3.0 20.6 %collective-permute-start.5 = (bf16[256,1536]{1,0:T(8,128)(2,1)}, bf16[256,1536]{1,0:T(8,128)(2,1)}, u32[]{:S(2)}, u32[]{:S(2)}) collective-permute-start(bf16[256,1536]{1,0:T(8,128)(2,1)} %refs_5_.1), channel_id=1, source_target_pairs={{0,8},{4,12},{8,0},{12,4},{16,24},{20,28},{24,16},{28,20},{1,9},{5... | collective-permute-start | bytes 2359304 | tf_op jit(solution)/shard_map/ppermute | solution.py:31
  4.5 20.7 %collective-permute-start = (bf16[768,512]{1,0:T(8,128)(2,1)}, bf16[768,512]{1,0:T(8,128)(2,1)S(1)}, u32[]{:S(2)}, u32[]{:S(2)}) collective-permute-start(bf16[768,512]{1,0:T(8,128)(2,1)} %refs_0_.1), channel_id=1, source_target_pairs={{0,1},{1,2},{2,3},{4,5},{5,6},{6,7},{8,9},{9,10},{10,11},{12,13},{... | collective-permute-start | bytes 2359304 | tf_op jit(solution)/shard_map/ppermute | solution.py:25
  8.1 21.7 %collective-permute-start.2 = (bf16[768,512]{1,0:T(8,128)(2,1)}, bf16[768,512]{1,0:T(8,128)(2,1)S(1)}, u32[]{:S(2)}, u32[]{:S(2)}) collective-permute-start(bf16[768,512]{1,0:T(8,128)(2,1)} %refs_0_.1), channel_id=1, source_target_pairs={{1,0},{2,1},{3,2},{5,4},{6,5},{7,6},{9,8},{10,9},{11,10},{13,12},{... | collective-permute-start | bytes 2359304 | tf_op jit(solution)/shard_map/ppermute | solution.py:26
  9.4 24.1 %collective-permute-start.4 = (bf16[256,1536]{1,0:T(8,128)(2,1)}, bf16[256,1536]{1,0:T(8,128)(2,1)S(1)}, u32[]{:S(2)}, u32[]{:S(2)}) collective-permute-start(bf16[256,1536]{1,0:T(8,128)(2,1)} %refs_5_.1), channel_id=1, source_target_pairs={{0,4},{4,0},{8,12},{12,8},{16,20},{20,16},{24,28},{28,24},{1,5},{5... | collective-permute-start | bytes 2359304 | tf_op jit(solution)/shard_map/ppermute | solution.py:31
  20.9 11.1 %collective-permute-start.13 = (bf16[256,512]{1,0:T(8,128)(2,1)}, bf16[256,512]{1,0:T(8,128)(2,1)S(1)}, u32[]{:S(2)}, u32[]{:S(2)}) collective-permute-start(bf16[256,512]{1,0:T(8,128)(2,1)} %param.7), channel_id=1, source_target_pairs={{0,16},{4,20},{8,24},{12,28},{16,0},{20,4},{24,8},{28,12},{1,17},{... | collective-permute-start | bytes 786440 | tf_op jit(solution)/shard_map/ppermute | solution.py:31
  23.7 9.8 %collective-permute-start.9 = (bf16[128,1536]{1,0:T(8,128)(2,1)S(1)}, bf16[128,1536]{1,0:T(8,128)(2,1)S(1)}, u32[]{:S(2)}, u32[]{:S(2)}) collective-permute-start(bf16[128,1536]{1,0:T(8,128)(2,1)S(1)} %slice.32), channel_id=1, source_target_pairs={{0,8},{4,12},{8,0},{12,4},{16,24},{20,28},{24,16},{28,20},{1,9},{5... | collective-permute-start | bytes 1179656 | tf_op jit(solution)/shard_map/ppermute | solution.py:31
  25.2 23.4 %copy-start.22 = (bf16[768,512]{1,0:T(8,128)(2,1)}, bf16[768,512]{1,0:T(8,128)(2,1)S(1)}, u32[]{:S(2)}) copy-start(bf16[768,512]{1,0:T(8,128)(2,1)S(1)} %collective-permute-done.refs_1_) | copy-start | bytes 2359300
  25.2 18.9 %collective-permute-start.1 = (bf16[768,512]{1,0:T(8,128)(2,1)S(1)}, bf16[768,512]{1,0:T(8,128)(2,1)}, u32[]{:S(2)}, u32[]{:S(2)}) collective-permute-start(bf16[768,512]{1,0:T(8,128)(2,1)S(1)} %collective-permute-done.refs_1_), channel_id=1, source_target_pairs={{0,1},{1,2},{2,3},{4,5},{5,6},{6,7},{8,9},{9,10},{10,11},{12,13},{... | collective-permute-start | bytes 2359304 | tf_op jit(solution)/shard_map/ppermute | solution.py:25
  29.7 20.8 %copy-start.23 = (bf16[768,512]{1,0:T(8,128)(2,1)}, bf16[768,512]{1,0:T(8,128)(2,1)S(1)}, u32[]{:S(2)}) copy-start(bf16[768,512]{1,0:T(8,128)(2,1)S(1)} %collective-permute-done.2.refs_3_) | copy-start | bytes 2359300
  29.7 19.5 %collective-permute-start.3 = (bf16[768,512]{1,0:T(8,128)(2,1)S(1)}, bf16[768,512]{1,0:T(8,128)(2,1)}, u32[]{:S(2)}, u32[]{:S(2)}) collective-permute-start(bf16[768,512]{1,0:T(8,128)(2,1)S(1)} %collective-permute-done.2.refs_3_), channel_id=1, source_target_pairs={{1,0},{2,1},{3,2},{5,4},{6,5},{7,6},{9,8},{10,9},{11,10},{13,12},{... | collective-permute-start | bytes 2359304 | tf_op jit(solution)/shard_map/ppermute | solution.py:26
  32.0 9.2 %collective-permute-start.10 = (bf16[128,1536]{1,0:T(8,128)(2,1)S(1)}, bf16[128,1536]{1,0:T(8,128)(2,1)S(1)}, u32[]{:S(2)}, u32[]{:S(2)}) collective-permute-start(bf16[128,1536]{1,0:T(8,128)(2,1)S(1)} %slice.33), channel_id=1, source_target_pairs={{0,16},{4,20},{8,24},{12,28},{16,0},{20,4},{24,8},{28,12},{1,17},{... | collective-permute-start | bytes 1179656 | tf_op jit(solution)/shard_map/ppermute | solution.py:31
  33.4 17.2 %copy-start.25 = (bf16[128,1536]{1,0:T(8,128)(2,1)}, bf16[128,1536]{1,0:T(8,128)(2,1)S(1)}, u32[]{:S(2)}) copy-start(bf16[128,1536]{1,0:T(8,128)(2,1)S(1)} %collective-permute-done.9.refs_11_) | copy-start | bytes 1179652
  33.4 7.8 %collective-permute-start.11 = (bf16[128,1536]{1,0:T(8,128)(2,1)S(1)}, bf16[128,1536]{1,0:T(8,128)(2,1)S(1)}, u32[]{:S(2)}, u32[]{:S(2)}) collective-permute-start(bf16[128,1536]{1,0:T(8,128)(2,1)S(1)} %collective-permute-done.9.refs_11_), channel_id=1, source_target_pairs={{0,4},{4,0},{8,12},{12,8},{16,20},{20,16},{24,28},{28,24},{1,5},{5... | collective-permute-start | bytes 1179656 | tf_op jit(solution)/shard_map/ppermute | solution.py:31
  33.5 20.6 %collective-permute-start.6 = (bf16[256,1536]{1,0:T(8,128)(2,1)}, bf16[256,1536]{1,0:T(8,128)(2,1)}, u32[]{:S(2)}, u32[]{:S(2)}) collective-permute-start(bf16[256,1536]{1,0:T(8,128)(2,1)} %collective-permute-done.5.refs_7_), channel_id=1, source_target_pairs={{0,4},{4,0},{8,12},{12,8},{16,20},{20,16},{24,28},{28,24},{1,5},{5... | collective-permute-start | bytes 2359304 | tf_op jit(solution)/shard_map/ppermute | solution.py:31
  41.2 12.9 %collective-permute-start.8 = (bf16[256,1536]{1,0:T(8,128)(2,1)}, bf16[256,1536]{1,0:T(8,128)(2,1)}, u32[]{:S(2)}, u32[]{:S(2)}) collective-permute-start(bf16[256,1536]{1,0:T(8,128)(2,1)} %collective-permute-done.7.refs_9_), channel_id=1, source_target_pairs={{0,4},{4,0},{8,12},{12,8},{16,20},{20,16},{24,28},{28,24},{1,5},{5... | collective-permute-start | bytes 2359304 | tf_op jit(solution)/shard_map/ppermute | solution.py:31
  41.2 10.2 %collective-permute-start.12 = (bf16[128,1536]{1,0:T(8,128)(2,1)S(1)}, bf16[128,1536]{1,0:T(8,128)(2,1)}, u32[]{:S(2)}, u32[]{:S(2)}) collective-permute-start(bf16[128,1536]{1,0:T(8,128)(2,1)S(1)} %collective-permute-done.10.refs_12_), channel_id=1, source_target_pairs={{0,4},{4,0},{8,12},{12,8},{16,20},{20,16},{24,28},{28,24},{1,5},{5... | collective-permute-start | bytes 1179656 | tf_op jit(solution)/shard_map/ppermute | solution.py:31
  44.1 20.7 %collective-permute-start.15 = (bf16[768,512]{1,0:T(8,128)(2,1)}, bf16[768,512]{1,0:T(8,128)(2,1)S(1)}, u32[]{:S(2)}, u32[]{:S(2)}) collective-permute-start(bf16[768,512]{1,0:T(8,128)(2,1)} %collective-permute-done.1.refs_2_), channel_id=1, source_target_pairs={{0,1},{1,2},{2,3},{4,5},{5,6},{6,7},{8,9},{9,10},{10,11},{12,13},{... | collective-permute-start | bytes 2359304 | tf_op jit(solution)/shard_map/ppermute | solution.py:25
  49.2 18.8 %collective-permute-start.16 = (bf16[768,512]{1,0:T(8,128)(2,1)}, bf16[768,512]{1,0:T(8,128)(2,1)S(1)}, u32[]{:S(2)}, u32[]{:S(2)}) collective-permute-start(bf16[768,512]{1,0:T(8,128)(2,1)} %collective-permute-done.3.refs_4_), channel_id=1, source_target_pairs={{1,0},{2,1},{3,2},{5,4},{6,5},{7,6},{9,8},{10,9},{11,10},{13,12},{... | collective-permute-start | bytes 2359304 | tf_op jit(solution)/shard_map/ppermute | solution.py:26
  51.4 13.4 %collective-permute-start.14 = (bf16[512,512]{1,0:T(8,128)(2,1)S(1)}, bf16[512,512]{1,0:T(8,128)(2,1)S(1)}, u32[]{:S(2)}, u32[]{:S(2)}) collective-permute-start(bf16[512,512]{1,0:T(8,128)(2,1)S(1)} %pad_maximum_fusion), channel_id=1, source_target_pairs={{0,8},{4,12},{8,0},{12,4},{16,24},{20,28},{24,16},{28,20},{1,9},{5... | collective-permute-start | bytes 1572872 | tf_op jit(solution)/shard_map/ppermute | solution.py:31
  74.2 8.8 %collective-permute-start.17 = (bf16[256,512]{1,0:T(8,128)(2,1)}, bf16[256,512]{1,0:T(8,128)(2,1)S(1)}, u32[]{:S(2)}, u32[]{:S(2)}) collective-permute-start(bf16[256,512]{1,0:T(8,128)(2,1)} %get-tuple-element.49), channel_id=1, source_target_pairs={{0,8},{4,12},{8,0},{12,4},{16,24},{20,28},{24,16},{28,20},{1,9},{5... | collective-permute-start | bytes 786440 | tf_op jit(solution)/shard_map/ppermute | solution.py:31
  74.8 10.1 %collective-permute-start.18 = (bf16[256,512]{1,0:T(8,128)(2,1)}, bf16[256,512]{1,0:T(8,128)(2,1)S(1)}, u32[]{:S(2)}, u32[]{:S(2)}) collective-permute-start(bf16[256,512]{1,0:T(8,128)(2,1)} %get-tuple-element.50), channel_id=1, source_target_pairs={{0,16},{4,20},{8,24},{12,28},{16,0},{20,4},{24,8},{28,12},{1,17},{... | collective-permute-start | bytes 786440 | tf_op jit(solution)/shard_map/ppermute | solution.py:31
  75.3 9.6 %collective-permute-start.19 = (bf16[256,512]{1,0:T(8,128)(2,1)}, bf16[256,512]{1,0:T(8,128)(2,1)S(1)}, u32[]{:S(2)}, u32[]{:S(2)}) collective-permute-start(bf16[256,512]{1,0:T(8,128)(2,1)} %get-tuple-element.51), channel_id=1, source_target_pairs={{0,24},{4,28},{8,16},{12,20},{16,8},{20,12},{24,0},{28,4},{1,25},{... | collective-permute-start | bytes 786440 | tf_op jit(solution)/shard_map/ppermute | solution.py:31
  85.1 3.6 %collective-permute-start.20 = (bf16[512,512]{1,0:T(8,128)(2,1)S(1)}, bf16[512,512]{1,0:T(8,128)(2,1)S(1)}, u32[]{:S(2)}, u32[]{:S(2)}) collective-permute-start(bf16[512,512]{1,0:T(8,128)(2,1)S(1)} %pad_maximum_fusion.1), channel_id=1, source_target_pairs={{0,4},{4,0},{8,12},{12,8},{16,20},{20,16},{24,28},{28,24},{1,5},{5... | collective-permute-start | bytes 1572872 | tf_op jit(solution)/shard_map/ppermute | solution.py:31
  85.1 10.3 %collective-permute-start.25 = (bf16[256,512]{1,0:T(8,128)(2,1)}, bf16[256,512]{1,0:T(8,128)(2,1)S(1)}, u32[]{:S(2)}, u32[]{:S(2)}) collective-permute-start(bf16[256,512]{1,0:T(8,128)(2,1)} %get-tuple-element.64), channel_id=1, source_target_pairs={{0,8},{4,12},{8,0},{12,4},{16,24},{20,28},{24,16},{28,20},{1,9},{5... | collective-permute-start | bytes 786440 | tf_op jit(solution)/shard_map/ppermute | solution.py:31
  86.7 14.0 %collective-permute-start.26 = (bf16[256,512]{1,0:T(8,128)(2,1)S(1)}, bf16[256,512]{1,0:T(8,128)(2,1)S(1)}, u32[]{:S(2)}, u32[]{:S(2)}) collective-permute-start(bf16[256,512]{1,0:T(8,128)(2,1)S(1)} %copy-done.29), channel_id=1, source_target_pairs={{0,16},{4,20},{8,24},{12,28},{16,0},{20,4},{24,8},{28,12},{1,17},{... | collective-permute-start | bytes 786440 | tf_op jit(solution)/shard_map/ppermute | solution.py:31
  87.2 13.5 %collective-permute-start.27 = (bf16[256,512]{1,0:T(8,128)(2,1)S(1)}, bf16[256,512]{1,0:T(8,128)(2,1)S(1)}, u32[]{:S(2)}, u32[]{:S(2)}) collective-permute-start(bf16[256,512]{1,0:T(8,128)(2,1)S(1)} %copy-done.28), channel_id=1, source_target_pairs={{0,24},{4,28},{8,16},{12,20},{16,8},{20,12},{24,0},{28,4},{1,25},{... | collective-permute-start | bytes 786440 | tf_op jit(solution)/shard_map/ppermute | solution.py:31
  100.8 4.7 %collective-permute-start.28 = (bf16[512,512]{1,0:T(8,128)(2,1)S(1)}, bf16[512,512]{1,0:T(8,128)(2,1)S(1)}, u32[]{:S(2)}, u32[]{:S(2)}) collective-permute-start(bf16[512,512]{1,0:T(8,128)(2,1)S(1)} %pad_maximum_fusion.2), channel_id=1, source_target_pairs={{0,4},{4,0},{8,12},{12,8},{16,20},{20,16},{24,28},{28,24},{1,5},{5... | collective-permute-start | bytes 1572872 | tf_op jit(solution)/shard_map/ppermute | solution.py:31
  101.0 48.7 %collective-permute-start.33 = (bf16[1024,512]{1,0:T(8,128)(2,1)S(1)}, bf16[1024,512]{1,0:T(8,128)(2,1)S(1)}, u32[]{:S(2)}, u32[]{:S(2)}) collective-permute-start(bf16[1024,512]{1,0:T(8,128)(2,1)S(1)} %constant_dynamic-update-slice_fusion.refs_10_), channel_id=1, source_target_pairs={{0,4},{4,0},{8,12},{12,8},{16,20},{20,16},{24,28},{28,24},{1,5},{5... | collective-permute-start | bytes 3145736 | tf_op jit(solution)/shard_map/ppermute | solution.py:31
  101.6 16.6 %collective-permute-start.21 = (bf16[768,256]{1,0:T(8,128)(2,1)S(1)}, bf16[768,256]{1,0:T(8,128)(2,1)S(1)}, u32[]{:S(2)}, u32[]{:S(2)}) collective-permute-start(bf16[768,256]{1,0:T(8,128)(2,1)S(1)} %shard_map.59.refs_0_), channel_id=1, source_target_pairs={{0,1},{1,2},{2,3},{4,5},{5,6},{6,7},{8,9},{9,10},{10,11},{12,13},{... | collective-permute-start | bytes 1179656 | tf_op jit(solution)/shard_map/ppermute | solution.py:25
  104.3 19.2 %collective-permute-start.23 = (bf16[768,256]{1,0:T(8,128)(2,1)S(1)}, bf16[768,256]{1,0:T(8,128)(2,1)S(1)}, u32[]{:S(2)}, u32[]{:S(2)}) collective-permute-start(bf16[768,256]{1,0:T(8,128)(2,1)S(1)} %shard_map.59.refs_0_), channel_id=1, source_target_pairs={{1,0},{2,1},{3,2},{5,4},{6,5},{7,6},{9,8},{10,9},{11,10},{13,12},{... | collective-permute-start | bytes 1179656 | tf_op jit(solution)/shard_map/ppermute | solution.py:26
  112.3 37.5 %copy-start.1 = (bf16[768,256]{1,0:T(8,128)(2,1)}, bf16[768,256]{1,0:T(8,128)(2,1)S(1)}, u32[]{:S(2)}) copy-start(bf16[768,256]{1,0:T(8,128)(2,1)S(1)} %shard_map.60.refs_5_) | copy-start | bytes 1179652
  112.3 14.1 %collective-permute-start.29 = (bf16[768,256]{1,0:T(8,128)(2,1)S(1)}, bf16[768,256]{1,0:T(8,128)(2,1)S(1)}, u32[]{:S(2)}, u32[]{:S(2)}) collective-permute-start(bf16[768,256]{1,0:T(8,128)(2,1)S(1)} %shard_map.60.refs_5_), channel_id=1, source_target_pairs={{0,1},{1,2},{2,3},{4,5},{5,6},{6,7},{8,9},{9,10},{10,11},{12,13},{... | collective-permute-start | bytes 1179656 | tf_op jit(solution)/shard_map/ppermute | solution.py:25
  116.8 14.7 %collective-permute-start.31 = (bf16[768,256]{1,0:T(8,128)(2,1)S(1)}, bf16[768,256]{1,0:T(8,128)(2,1)S(1)}, u32[]{:S(2)}, u32[]{:S(2)}) collective-permute-start(bf16[768,256]{1,0:T(8,128)(2,1)S(1)} %shard_map.60.refs_5_), channel_id=1, source_target_pairs={{1,0},{2,1},{3,2},{5,4},{6,5},{7,6},{9,8},{10,9},{11,10},{13,12},{... | collective-permute-start | bytes 1179656 | tf_op jit(solution)/shard_map/ppermute | solution.py:26
  118.1 31.6 %copy-start.14 = (bf16[768,256]{1,0:T(8,128)(2,1)}, bf16[768,256]{1,0:T(8,128)(2,1)S(1)}, u32[]{:S(2)}) copy-start(bf16[768,256]{1,0:T(8,128)(2,1)S(1)} %collective-permute-done.21.refs_1_) | copy-start | bytes 1179652
  118.2 16.6 %collective-permute-start.22 = (bf16[768,256]{1,0:T(8,128)(2,1)S(1)}, bf16[768,256]{1,0:T(8,128)(2,1)}, u32[]{:S(2)}, u32[]{:S(2)}) collective-permute-start(bf16[768,256]{1,0:T(8,128)(2,1)S(1)} %collective-permute-done.21.refs_1_), channel_id=1, source_target_pairs={{0,1},{1,2},{2,3},{4,5},{5,6},{6,7},{8,9},{9,10},{10,11},{12,13},{... | collective-permute-start | bytes 1179656 | tf_op jit(solution)/shard_map/ppermute | solution.py:25
  123.5 26.3 %copy-start.15 = (bf16[768,256]{1,0:T(8,128)(2,1)}, bf16[768,256]{1,0:T(8,128)(2,1)S(1)}, u32[]{:S(2)}) copy-start(bf16[768,256]{1,0:T(8,128)(2,1)S(1)} %collective-permute-done.23.refs_3_) | copy-start | bytes 1179652
  123.5 16.5 %collective-permute-start.24 = (bf16[768,256]{1,0:T(8,128)(2,1)S(1)}, bf16[768,256]{1,0:T(8,128)(2,1)S(1)}, u32[]{:S(2)}, u32[]{:S(2)}) collective-permute-start(bf16[768,256]{1,0:T(8,128)(2,1)S(1)} %collective-permute-done.23.refs_3_), channel_id=1, source_target_pairs={{1,0},{2,1},{3,2},{5,4},{6,5},{7,6},{9,8},{10,9},{11,10},{13,12},{... | collective-permute-start | bytes 1179656 | tf_op jit(solution)/shard_map/ppermute | solution.py:26
  126.4 23.4 %copy-start.16 = (bf16[768,256]{1,0:T(8,128)(2,1)}, bf16[768,256]{1,0:T(8,128)(2,1)S(1)}, u32[]{:S(2)}) copy-start(bf16[768,256]{1,0:T(8,128)(2,1)S(1)} %collective-permute-done.29.refs_6_) | copy-start | bytes 1179652
  126.4 16.9 %collective-permute-start.30 = (bf16[768,256]{1,0:T(8,128)(2,1)S(1)}, bf16[768,256]{1,0:T(8,128)(2,1)}, u32[]{:S(2)}, u32[]{:S(2)}) collective-permute-start(bf16[768,256]{1,0:T(8,128)(2,1)S(1)} %collective-permute-done.29.refs_6_), channel_id=1, source_target_pairs={{0,1},{1,2},{2,3},{4,5},{5,6},{6,7},{8,9},{9,10},{10,11},{12,13},{... | collective-permute-start | bytes 1179656 | tf_op jit(solution)/shard_map/ppermute | solution.py:25
  131.5 17.0 %collective-permute-start.32 = (bf16[768,256]{1,0:T(8,128)(2,1)S(1)}, bf16[768,256]{1,0:T(8,128)(2,1)}, u32[]{:S(2)}, u32[]{:S(2)}) collective-permute-start(bf16[768,256]{1,0:T(8,128)(2,1)S(1)} %collective-permute-done.31.refs_8_), channel_id=1, source_target_pairs={{1,0},{2,1},{3,2},{5,4},{6,5},{7,6},{9,8},{10,9},{11,10},{13,12},{... | collective-permute-start | bytes 1179656 | tf_op jit(solution)/shard_map/ppermute | solution.py:26
  134.8 22.2 %collective-permute-start.34 = (bf16[768,256]{1,0:T(8,128)(2,1)}, bf16[768,256]{1,0:T(8,128)(2,1)}, u32[]{:S(2)}, u32[]{:S(2)}) collective-permute-start(bf16[768,256]{1,0:T(8,128)(2,1)} %collective-permute-done.22.refs_2_), channel_id=1, source_target_pairs={{0,1},{1,2},{2,3},{4,5},{5,6},{6,7},{8,9},{9,10},{10,11},{12,13},{... | collective-permute-start | bytes 1179656 | tf_op jit(solution)/shard_map/ppermute | solution.py:25
  140.0 17.0 %collective-permute-start.35 = (bf16[768,256]{1,0:T(8,128)(2,1)S(1)}, bf16[768,256]{1,0:T(8,128)(2,1)}, u32[]{:S(2)}, u32[]{:S(2)}) collective-permute-start(bf16[768,256]{1,0:T(8,128)(2,1)S(1)} %collective-permute-done.24.refs_4_), channel_id=1, source_target_pairs={{1,0},{2,1},{3,2},{5,4},{6,5},{7,6},{9,8},{10,9},{11,10},{13,12},{... | collective-permute-start | bytes 1179656 | tf_op jit(solution)/shard_map/ppermute | solution.py:26
  143.2 15.5 %collective-permute-start.36 = (bf16[768,256]{1,0:T(8,128)(2,1)}, bf16[768,256]{1,0:T(8,128)(2,1)}, u32[]{:S(2)}, u32[]{:S(2)}) collective-permute-start(bf16[768,256]{1,0:T(8,128)(2,1)} %collective-permute-done.30.refs_7_), channel_id=1, source_target_pairs={{0,1},{1,2},{2,3},{4,5},{5,6},{6,7},{8,9},{9,10},{10,11},{12,13},{... | collective-permute-start | bytes 1179656 | tf_op jit(solution)/shard_map/ppermute | solution.py:25
  148.5 14.4 %collective-permute-start.37 = (bf16[768,256]{1,0:T(8,128)(2,1)}, bf16[768,256]{1,0:T(8,128)(2,1)}, u32[]{:S(2)}, u32[]{:S(2)}) collective-permute-start(bf16[768,256]{1,0:T(8,128)(2,1)} %collective-permute-done.32.refs_9_), channel_id=1, source_target_pairs={{1,0},{2,1},{3,2},{5,4},{6,5},{7,6},{9,8},{10,9},{11,10},{13,12},{... | collective-permute-start | bytes 1179656 | tf_op jit(solution)/shard_map/ppermute | solution.py:26
  (20 other events, 142.1 us)
